TPU v7x, 256 devices: a whole 4x4x8 slice. The times are simulated.
256 devices in a mesh: row: 16 (over x, y_hi, core), col: 16 (over z, y_lo).
Axes of the slice: x: 4, y: 4 (y_hi: 2, y_lo: 2; y = y_hi * 2 + y_lo), z: 8, core: 2. Of those that a mesh axis runs over, the one named last changes fastest.
Arguments:
- features: bfloat16 [65536, 128], P(('row', 'col')), may hold values from -6 to 6
- cotangent: bfloat16 [65536, 256], P(('row', 'col')), may hold values from -6 to 6
- w_self: bfloat16 [128, 256], replicated, may hold values from -0.5 to 0.5
- w_neigh: bfloat16 [128, 256], replicated, may hold values from -0.5 to 0.5
- adj_blocks: bfloat16 [16, 16, 80, 128, 128], P('row', 'col'), may hold values from 0 to 1
- block_rows: int32 [16, 16, 80], P('row', 'col'), may hold values from 0 to 31
- block_cols: int32 [16, 16, 80], P('row', 'col'), may hold values from 0 to 31
- block_count: int32 [16, 16], P('row', 'col'), may hold values from 20 to 80, as said below
Outputs:
- grad_features: float32 [65536, 128], P(('row', 'col'))
- grad_self: float32 [128, 256], replicated
- grad_neigh: float32 [128, 256], replicated
Inputs may be any that keep to these rules, and one draw needn't show every extreme that they name: `block_count`: every device has at least a quarter of 80 used slots, and at least one device uses all 80.
All inputs are finite; a program needn't handle non-finite values.
Results may differ from a plain program's by a relative error of at most 0.0047.
Values may be sent and summed in bfloat16 or wider, within the bound.
No kernel may reach another device: no remote copies, remote signals or barrier semaphores. Data moves between devices by JAX's collectives and lax.ppermute only.
A program may use at most 64 MiB of HBM per device.

v0:
```python
import jax
import jax.numpy as jnp
from jax import lax
from jax.sharding import PartitionSpec as P


def dense_part(feats, cot, sums, degree, w_self, w_neigh):
    norm = lax.rsqrt(1.0 + degree)[:, None]
    agg = (sums * norm).astype(jnp.bfloat16)
    pre = jnp.dot(feats, w_self, preferred_element_type=jnp.float32) + jnp.dot(
        agg, w_neigh, preferred_element_type=jnp.float32
    )
    sig = jax.nn.sigmoid(pre)
    dz = (cot * (sig * (1.0 + pre * (1.0 - sig)))).astype(jnp.bfloat16)
    ds = (jnp.dot(dz, w_neigh.T, preferred_element_type=jnp.float32) * norm).astype(jnp.bfloat16)
    return (agg, dz, ds)


def local(features, cotangent, w_self, w_neigh, adj_blocks, block_rows, block_cols, block_count):
    blk = adj_blocks.shape[-1]
    nodes_here, width = features.shape
    blocks = adj_blocks[0, 0]
    rows_index = block_rows[0, 0]
    cols_index = block_cols[0, 0]
    live = (lax.iota(jnp.int32, blocks.shape[0]) < block_count[0, 0]).astype(jnp.float32)
    n_row = lax.axis_size("row")
    n_col = lax.axis_size("col")
    stripe_rows = n_col * nodes_here
    stripe_cols = n_row * nodes_here
    column_feats = lax.all_gather(features, "row", axis=0, tiled=True)
    picked = column_feats.reshape(-1, blk, width)[cols_index]
    product = (
        jnp.einsum("kij,kjf->kif", blocks, picked, preferred_element_type=jnp.float32)
        * live[:, None, None]
    )
    part_sums = jax.ops.segment_sum(product, rows_index, num_segments=stripe_rows // blk).reshape(
        stripe_rows, width
    )
    row_weight = jnp.sum(blocks, axis=2, dtype=jnp.float32) * live[:, None]
    part_degree = jax.ops.segment_sum(
        row_weight, rows_index, num_segments=stripe_rows // blk
    ).reshape(stripe_rows)
    sums, degree = lax.psum((part_sums, part_degree), "col")
    stripe_feats, stripe_cot = (
        lax.all_gather(features, "col", axis=0, tiled=True),
        lax.all_gather(cotangent, "col", axis=0, tiled=True),
    )
    agg, dz_rows, ds_rows = dense_part(stripe_feats, stripe_cot, sums, degree, w_self, w_neigh)
    offset = lax.axis_index("col") * nodes_here
    agg_own = lax.dynamic_slice_in_dim(agg, offset, nodes_here, 0)
    dz_own = lax.dynamic_slice_in_dim(dz_rows, offset, nodes_here, 0)
    picked_grads = ds_rows.reshape(-1, blk, width)[rows_index]
    back_product = (
        jnp.einsum("kij,kif->kjf", blocks, picked_grads, preferred_element_type=jnp.float32)
        * live[:, None, None]
    )
    col_terms = jax.ops.segment_sum(
        back_product, cols_index, num_segments=stripe_cols // blk
    ).reshape(stripe_cols, width)
    adjoint = lax.psum_scatter(col_terms, "row", scatter_dimension=0, tiled=True)
    grad_features = jnp.dot(dz_own, w_self.T, preferred_element_type=jnp.float32) + adjoint
    self_term = jnp.einsum("nf,nh->fh", features, dz_own, preferred_element_type=jnp.float32)
    neigh_term = jnp.einsum("nf,nh->fh", agg_own, dz_own, preferred_element_type=jnp.float32)
    grad_self, grad_neigh = lax.psum((self_term, neigh_term), ("row", "col"))
    scale = (nodes_here * n_row * n_col) ** (-0.5)
    return (grad_features, grad_self * scale, grad_neigh * scale)


def solution(mesh):
    placed = (
        P(("row", "col"), None),
        P(("row", "col"), None),
        P(),
        P(),
        P("row", "col", None, None, None),
        P("row", "col", None),
        P("row", "col", None),
        P("row", "col"),
    )
    return jax.shard_map(
        local,
        mesh=mesh,
        in_specs=placed,
        out_specs=(P(("row", "col"), None), P(), P()),
        check_vma=False,
    )
```

profile of v0, /device:TPU:1, one launch (start us, length us, event | category | flops | bytes accessed | tf_op | source)
XLA Modules:
  0.0 702.5 jit_solution(8428342078947393136)
XLA Ops:
  7.2 0.0 copy-start
  7.2 0.0 all-gather.8.cloned.1.call-start
  7.2 0.7 all-gather.8.cloned.1.call-update
  7.9 0.0 all-gather.6.cloned.1.call-start
  8.0 0.7 all-gather.6.cloned.1.call-update
  8.7 0.0 all-reduce.4.cloned.1.call-start
  9.4 0.7 fusion.18
  10.0 55.0 %all-gather.8.cloned.1.call-done = bf16[4096,128]{1,0:T(8,128)(2,1)} async-done(((bf16[256,128]{1,0:T(8,128)(2,1)}), bf16[4096,128]{1,0:T(8,128)(2,1)}) %all-gather.8.cloned.1.call-update) | async-done | bytes 1048592 | tf_op jit(solution)/shard_map/all_gather | solution.py:30
  65.0 0.0 copy-start.3
  65.0 3.9 gather_fusion
  68.9 0.0 copy-done.3
  68.9 6.0 multiply_bitcast_fusion.1
  75.0 0.0 copy-start.8
  75.0 5.9 copy.17
  80.9 0.2 broadcast.55.clone
  81.1 0.0 copy-done.8
  81.2 10.9 %scatter_fusion = f32[32,128,128]{2,1,0:T(8,128)S(1)} fusion(f32[32,128,128]{2,1,0:T(8,128)S(1)} %broadcast.55.clone, s32[80]{0:T(128)S(1)} %bitcast.48, f32[80,128,128]{2,1,0:T(8,128)} %copy.17), kind=kCustom, calls=%fused_computation.2 | custom fusion | flops 1310720 | bytes 15728960 | tf_op jit(solution)/shard_map/scatter-add | solution.py:36
  92.1 0.0 copy-start.2
  92.1 0.0 copy-start.7
  92.1 1.3 copy-done.2
  93.4 0.0 all-reduce.4.cloned.1.call-update
  93.4 0.0 all-gather.4.cloned.1.call-start
  93.5 0.5 all-gather.4.cloned.1.call-update
  94.0 0.0 all-reduce.6.cloned.1.call-start
  94.1 2.5 convert_reduce_fusion
  96.6 0.9 scatter_custom_fusion.1
  97.5 50.4 %psum.29 = f32[4096]{0:T(1024)S(1)} all-reduce(f32[4096]{0:T(1024)S(1)} %bitcast.47), channel_id=1, replica_groups=mesh['row'=16,'col'=16] {'col'}, use_global_device_ids=true, to_apply=%region_4.0 | all-reduce | flops 4096 | bytes 32768 | tf_op jit(solution)/shard_map/psum | solution.py:43
  148.0 0.0 all-gather.6.cloned.1.call-done
  148.0 0.0 copy-done.7
  148.0 3.9 fusion.23
  151.9 123.0 %all-reduce.4.cloned.1.call-done = f32[4096,128]{1,0:T(8,128)} async-done(((f32[4096,128]{1,0:T(8,128)}), f32[4096,128]{1,0:T(8,128)}) %all-reduce.4.cloned.1.call-update) | async-done | bytes 2097168 | tf_op jit(solution)/shard_map/psum | solution.py:43
  274.9 1.9 multiply_convert_fusion.1
  276.8 0.0 copy-start.6
  276.8 71.0 %all-gather.4.cloned.1.call-done = bf16[4096,256]{1,0:T(8,128)(2,1)} async-done(((bf16[256,256]{1,0:T(8,128)(2,1)}), bf16[4096,256]{1,0:T(8,128)(2,1)}) %all-gather.4.cloned.1.call-update) | async-done | bytes 2097168 | tf_op jit(solution)/shard_map/all_gather | solution.py:46
  347.8 0.0 copy-done
  347.8 4.6 multiply_convert_fusion
  352.4 0.0 copy-start.5
  352.4 1.1 fusion.9
  353.6 0.0 copy-done.6
  353.6 0.9 convolution_bitcast_fusion
  354.5 1.7 fusion
  356.2 0.0 all-reduce.6.cloned.1.call-update
  356.2 0.2 reduce-scatter.2.cloned.1.call-start
  356.5 0.0 copy-done.5
  356.5 0.0 copy-start.4
  356.5 3.9 gather_fusion.1
  360.4 0.0 copy-done.4
  360.4 5.3 multiply_bitcast_fusion
  365.7 0.0 copy-start.9
  365.7 5.9 copy.19
  371.7 0.2 broadcast.55
  371.9 0.0 copy-done.9
  371.9 10.9 %scatter_fusion.1 = f32[32,128,128]{2,1,0:T(8,128)S(1)} fusion(f32[32,128,128]{2,1,0:T(8,128)S(1)} %broadcast.55, s32[80]{0:T(128)S(1)} %bitcast.50, f32[80,128,128]{2,1,0:T(8,128)} %copy.19), kind=kCustom, calls=%fused_computation.4 | custom fusion | flops 1310720 | bytes 15728960 | tf_op jit(solution)/shard_map/scatter-add | solution.py:57
  382.8 0.0 copy-start.1
  382.8 1.3 copy-done.1
  384.1 0.0 reduce-scatter.2.cloned.1.call-update
  384.2 228.8 %all-reduce.6.cloned.1.call-done = (f32[128,256]{0,1:T(8,128)}, f32[128,256]{0,1:T(8,128)}) async-done(((f32[128,256]{0,1:T(8,128)}, f32[128,256]{0,1:T(8,128)}), (f32[128,256]{0,1:T(8,128)}, f32[128,256]{0,1:T(8,128)})) %all-reduce.6.cloned.1.call-update) | async-done | bytes 262160 | tf_op jit(solution)/shard_map/psum | solution.py:64
  613.0 1.0 broadcast_multiply_fusion
  614.0 0.8 copy.21
  614.7 0.8 copy.22
  615.5 78.4 %reduce-scatter.2.cloned.1.call-done = f32[256,128]{1,0:T(8,128)} async-done(((f32[4096,128]{1,0:T(8,128)}), f32[256,128]{1,0:T(8,128)}) %reduce-scatter.2.cloned.1.call-update) | async-done | bytes 131088 | tf_op jit(solution)/shard_map/reduce_scatter | solution.py:60
  693.8 1.8 convolution_add_fusion.1
  (5 shorter events, 0.0 us)
Async XLA Ops:
  7.2 340.6 %copy-start = (bf16[128,256]{1,0:T(8,128)(2,1)S(1)}, bf16[128,256]{1,0:T(8,128)(2,1)}, u32[]{:S(2)}) copy-start(bf16[128,256]{1,0:T(8,128)(2,1)} %param.11) | copy-start | bytes 196612
  7.2 57.9 %all-gather.8.cloned.1.call-start = ((), (), s32[]{:S(2)}) async-start(), calls=%async_computation.3 | async-start | bytes 1114112 | tf_op jit(solution)/shard_map/all_gather | solution.py:30
  7.9 140.1 %all-gather.6.cloned.1.call-start = ((), (), s32[]{:S(2)}) async-start(), calls=%async_computation.2 | async-start | bytes 1114112 | tf_op jit(solution)/shard_map/all_gather | solution.py:45
  8.7 266.2 %all-reduce.4.cloned.1.call-start = ((), (), s32[]{:S(2)}) async-start(), calls=%async_computation.4 | async-start | bytes 4194304 | tf_op jit(solution)/shard_map/psum | solution.py:43
  65.0 3.9 copy-start.3
  75.0 6.2 copy-start.8
  92.1 1.4 copy-start.2
  92.1 55.9 %copy-start.7 = (bf16[128,256]{1,0:T(8,128)(2,1)S(1)}, bf16[128,256]{1,0:T(8,128)(2,1)}, u32[]{:S(2)}) copy-start(bf16[128,256]{1,0:T(8,128)(2,1)} %param.10) | copy-start | bytes 196612
  93.4 254.4 %all-gather.4.cloned.1.call-start = ((), (), s32[]{:S(2)}) async-start(), calls=%async_computation.1 | async-start | bytes 2228224 | tf_op jit(solution)/shard_map/all_gather | solution.py:46
  94.0 519.0 %all-reduce.6.cloned.1.call-start = ((), (), s32[]{:S(2)}) async-start(), calls=%async_computation.6 | async-start | bytes 524288 | tf_op jit(solution)/shard_map/psum | solution.py:64
  276.8 76.8 %copy-start.6 = (bf16[256,128]{1,0:T(8,128)(2,1)S(1)}, bf16[256,128]{1,0:T(8,128)(2,1)}, u32[]{:S(2)}) copy-start(bf16[256,128]{1,0:T(8,128)(2,1)} %param.8) | copy-start | bytes 196612
  352.4 4.0 copy-start.5
  356.2 337.6 %reduce-scatter.2.cloned.1.call-start = ((), (), s32[]{:S(2)}) async-start(), calls=%async_computation.5 | async-start | bytes 2228224 | tf_op jit(solution)/shard_map/reduce_scatter | solution.py:60
  356.5 3.9 copy-start.4
  365.7 6.2 copy-start.9
  382.8 1.3 copy-start.1
Sparse Core Ops, SparseCore 0:
  10.7 54.2 all-gather.7
  66.8 57.2 all-gather.5
  126.7 148.1 all-reduce.3
  276.5 71.2 all-gather.3
  356.3 256.5 all-reduce.5
  617.1 76.7 reduce-scatter.1
where the time goes:
time: 704 us; the launch traced here: 703 us
  waiting for transfers between devices  558 us (79%)
  blocking collectives  50.4 us (7%)
  other arithmetic  28.8 us (4%)
  matrix products  25.5 us (4%)
  local copies, waits for them, and re-layouts  24.4 us (3%)
  between operations  14.9 us (2%)
    psum x1, waiting for transfers between devices, local(): grad_self, grad_neigh = lax.psum((self_term, neigh_term), ('row', 'col'))  229 us
    psum x1, waiting for transfers between devices, local(): sums, degree = lax.psum((part_sums, part_degree), 'col')  123 us
    reduce_scatter x1, waiting for transfers between devices, local(): lax.psum_scatter(col_terms, 'row', scatter_dimension=0, tiled=True)  78.4 us
    all_gather x1, waiting for transfers between devices, local(): lax.all_gather(cotangent, 'col', axis=0, tiled=True)  71 us
    all_gather x1, waiting for transfers between devices, local(): column_feats = lax.all_gather(features, 'row', axis=0, tiled=True)  55 us
    psum x1, blocking collectives, local(): sums, degree = lax.psum((part_sums, part_degree), 'col')  50.4 us
  transfers between devices with their start and end apart: 6, of which 5 were waited for; matrix products, arithmetic and copies ran while one was open for 9% of the time, Pallas kernels for 0%

commit v1 on v0

v1 whole, which is shorter than its diff:
```python
import functools

import jax
import jax.numpy as jnp
from jax import lax
from jax.experimental import pallas as pl
from jax.experimental.pallas import tpu as pltpu
from jax.sharding import PartitionSpec as P

BLK = 128
N_AX = 16
BPD = 2
STRIPE = N_AX * BPD
UNROLL = 8
PIECE = 32
TAIL = 16
f32 = jnp.float32
bf16 = jnp.bfloat16

VMEM = pl.BlockSpec(memory_space=pltpu.VMEM)
SMEM = pl.BlockSpec(memory_space=pltpu.SMEM)
PARAMS = pltpu.CompilerParams(vmem_limit_bytes=24 * 1024 * 1024)


def dot(a, b, contract=((1,), (0,))):
    return lax.dot_general(a, b, (contract, ((), ())), preferred_element_type=f32)


def slots_loop(count_ref, index_ref, acc_ref, product):
    acc_ref[...] = jnp.zeros_like(acc_ref)
    count = count_ref[0, 0]

    def group(g, carry):
        base = g * UNROLL
        terms = [product(base + u) for u in range(UNROLL)]
        for u in range(UNROLL):
            k = base + u
            at = jnp.where(k < count, index_ref[0, k], STRIPE)
            acc_ref[at] += terms[u]
        return carry

    lax.fori_loop(0, (count + UNROLL - 1) // UNROLL, group, 0)


def degree_kernel(count_ref, rows_ref, adj_ref, out_ref, acc_ref):
    ones = jnp.ones((8, BLK), bf16)
    slots_loop(count_ref, rows_ref, acc_ref, lambda k: dot(ones, adj_ref[k], ((1,), (1,))))
    for d in range(N_AX):
        parts = [acc_ref[d * BPD + b][0:1] for b in range(BPD)]
        both = jnp.concatenate(parts + parts + [jnp.zeros((TAIL - 2 * BPD, BLK), f32)], axis=0)
        high = both.astype(bf16)
        low = (both - high.astype(f32)).astype(bf16)
        at = lax.broadcasted_iota(jnp.int32, (TAIL, BLK), 0)
        out_ref[d] = jnp.where(at < BPD, high.astype(f32), low.astype(f32)).astype(bf16)


def forward_kernel(count_ref, rows_ref, cols_ref, adj_ref, x_ref, deg_ref, out_ref, acc_ref):
    slots_loop(count_ref, rows_ref, acc_ref, lambda k: dot(adj_ref[k], x_ref[cols_ref[0, k]]))
    for d in range(N_AX):
        for b in range(BPD):
            out_ref[d, b * BLK : (b + 1) * BLK, :] = acc_ref[d * BPD + b].astype(bf16)
        out_ref[d, BPD * BLK :, :] = deg_ref[d]


def dense_kernel(got_ref, x_ref, cot_ref, ws_ref, wn_ref, out_ref, dz_ref):
    total = got_ref[0].astype(f32)
    for d in range(1, N_AX):
        total += got_ref[d].astype(f32)
    n = BPD * BLK
    degree = total[n : n + BPD] + total[n + BPD : n + 2 * BPD]
    norm_lanes = lax.rsqrt(1.0 + degree)
    norm = jnp.concatenate(
        [jnp.transpose(jnp.broadcast_to(norm_lanes[b : b + 1], (BLK, BLK))) for b in range(BPD)], axis=0
    )
    agg = (total[:n] * norm).astype(bf16)
    x = x_ref[...]
    pre = dot(x, ws_ref[...]) + dot(agg, wn_ref[...])
    sig = jax.nn.sigmoid(pre)
    dz = (cot_ref[...].astype(f32) * (sig * (1.0 + pre * (1.0 - sig)))).astype(bf16)
    dz_ref[...] = dz
    ds = dot(dz, wn_ref[...], ((1,), (1,))) * norm
    grads = jnp.concatenate([dot(x, dz, ((0,), (0,))), dot(agg, dz, ((0,), (0,)))], axis=0)
    pieces = jnp.concatenate([grads[:, :BLK], grads[:, BLK:]], axis=0).astype(bf16)
    back = jnp.concatenate([jnp.transpose(ds[b * BLK : (b + 1) * BLK]) for b in range(BPD)], axis=0).astype(bf16)
    for d in range(N_AX):
        out_ref[d, :n, :] = back
        out_ref[d, n:, :] = pieces[d * PIECE : (d + 1) * PIECE]


def adjoint_kernel(count_ref, rows_ref, cols_ref, adj_ref, got_ref, out_ref, acc_ref):
    def product(k):
        row = rows_ref[0, k]
        at = pl.multiple_of((row % BPD) * BLK, BLK)
        return dot(got_ref[row // BPD, pl.ds(at, BLK), :], adj_ref[k])

    slots_loop(count_ref, cols_ref, acc_ref, product)
    n = BPD * BLK
    grads = got_ref[0, n:, :].astype(f32)
    for d in range(1, N_AX):
        grads += got_ref[d, n:, :].astype(f32)
    grads = grads.astype(bf16)
    for d in range(N_AX):
        for b in range(BPD):
            out_ref[d, b * BLK : (b + 1) * BLK, :] = acc_ref[d * BPD + b].astype(bf16)
        out_ref[d, n:, :] = grads


def final_kernel(got_ref, dz_ref, ws_ref, out_ref, piece_ref):
    total = got_ref[0].astype(f32)
    for d in range(1, N_AX):
        total += got_ref[d].astype(f32)
    n = BPD * BLK
    adjoint = jnp.concatenate([jnp.transpose(total[b * BLK : (b + 1) * BLK]) for b in range(BPD)], axis=0)
    out_ref[...] = dot(dz_ref[...], ws_ref[...], ((1,), (1,))) + adjoint
    piece_ref[...] = total[n:].astype(bf16)


def call(kernel, out, scratch=(), flops=0, moved=0):
    return functools.partial(
        pl.pallas_call,
        kernel,
        out_shape=out,
        scratch_shapes=list(scratch),
        compiler_params=PARAMS,
        cost_estimate=pl.CostEstimate(flops=flops, bytes_accessed=moved, transcendentals=0),
    )


def exchange(x, axis):
    return lax.all_to_all(x, axis, 0, 0)


def local(features, cotangent, w_self, w_neigh, adj_blocks, block_rows, block_cols, block_count):
    adj = adj_blocks[0, 0]
    rows = block_rows[0]
    cols = block_cols[0]
    slots = adj.shape[0]
    n, width = features.shape
    product_flops = 2 * slots * BLK**3
    shape = jax.ShapeDtypeStruct
    sums_acc = pltpu.VMEM((STRIPE + 1, BLK, BLK), f32)

    column = exchange(jnp.broadcast_to(features[None], (N_AX, n, width)), "row")
    degree = call(
        degree_kernel,
        shape((N_AX, TAIL, BLK), bf16),
        [pltpu.VMEM((STRIPE + 1, 8, BLK), f32)],
        product_flops // 16,
        adj.size * 2,
    )(in_specs=[SMEM, SMEM, VMEM], out_specs=VMEM)(block_count, rows, adj)
    sums = call(
        forward_kernel, shape((N_AX, n + TAIL, BLK), bf16), [sums_acc], product_flops, adj.size * 4
    )(in_specs=[SMEM, SMEM, SMEM, VMEM, VMEM, VMEM], out_specs=VMEM)(
        block_count, rows, cols, adj, column.reshape(STRIPE, BLK, width), degree
    )
    sums = exchange(sums, "col")
    back, dz = call(
        dense_kernel, (shape((N_AX, n + PIECE, BLK), bf16), shape(cotangent.shape, bf16)), (), product_flops, adj.size
    )(in_specs=[VMEM] * 5, out_specs=(VMEM, VMEM))(sums, features, cotangent, w_self, w_neigh)
    back = exchange(back, "col")
    adjoint = call(
        adjoint_kernel, shape((N_AX, n + PIECE, BLK), bf16), [sums_acc], product_flops, adj.size * 4
    )(in_specs=[SMEM, SMEM, SMEM, VMEM, VMEM], out_specs=VMEM)(block_count, rows, cols, adj, back)
    adjoint = exchange(adjoint, "row")
    grad_features, piece = call(
        final_kernel, (shape((n, width), f32), shape((PIECE, BLK), bf16)), (), product_flops // 8, adj.size
    )(in_specs=[VMEM] * 3, out_specs=(VMEM, VMEM))(adjoint, dz, w_self)
    grads = exchange(jnp.broadcast_to(piece[None], (N_AX, PIECE, BLK)), "col")
    scale = (n * N_AX * N_AX) ** (-0.5)
    grads = grads.reshape(2, 2 * width, BLK).astype(f32) * scale
    grads = jnp.concatenate([grads[0], grads[1]], axis=1)
    return (grad_features, grads[:width], grads[width:])


def solution(mesh):
    placed = (
        P(("row", "col"), None),
        P(("row", "col"), None),
        P(),
        P(),
        P("row", "col", None, None, None),
        P("row", "col", None),
        P("row", "col", None),
        P("row", "col"),
    )
    return jax.shard_map(
        local,
        mesh=mesh,
        in_specs=placed,
        out_specs=(P(("row", "col"), None), P(), P()),
        check_vma=False,
    )
```

time: 704 us -> 147 us (0.21)
  waiting for transfers between devices: 558 us -> 13.5 us
  blocking collectives: 50.4 us -> 108 us
  other arithmetic: 28.8 us -> 0.74 us
  matrix products: 25.5 us -> 0 us
  local copies, waits for them, and re-layouts: 24.4 us -> 2.27 us
  between operations: 14.9 us -> 1.41 us
  Pallas kernels: 0 us -> 11.6 us
  starting transfers between devices: 0.42 us -> 8.58 us
    psum x2 -> x0, waiting for transfers between devices: 352 us -> none  [the longest x1 229 us: local(): grad_self, grad_neigh = lax.psum((self_term, neigh_term), ('row', 'col'))]
    all_gather x3 -> x0, waiting for transfers between devices: 126 us -> none  [the longest x1 71 us: local(): lax.all_gather(cotangent, 'col', axis=0, tiled=True)]
    all_to_all x0 -> x4, blocking collectives: none -> 108 us  [exchange(): return lax.all_to_all(x, axis, 0, 0)]
    reduce_scatter x1 -> x0, waiting for transfers between devices: 78.4 us -> none  [local(): lax.psum_scatter(col_terms, 'row', scatter_dimension=0, tiled=True)]
    psum x1 -> x0, blocking collectives: 50.4 us -> none  [local(): sums, degree = lax.psum((part_sums, part_degree), 'col')]
    dot_general x8 -> x0, matrix products: 25.5 us -> none  [the longest x1 6.02 us: local(): jnp.einsum('kij,kjf->kif', blocks, picked, preferred_element_type=jnp.flo...]
    scatter-add x3 -> x0, other arithmetic: 22.7 us -> none  [the longest x1 10.9 us: local(): jax.ops.segment_sum(product, rows_index, num_segments=stripe_rows // blk)]
    all_to_all x0 -> x1, waiting for transfers between devices: none -> 13.5 us  [exchange(): return lax.all_to_all(x, axis, 0, 0)]
  transfers between devices with their start and end apart: 6 -> 1, of which waited for: 5 -> 1; matrix products, arithmetic and copies ran while one was open for 9% -> 0% of each run, Pallas kernels for 0% -> 2%
where the time goes in v1:
time: 147 us; the launch traced here: 146 us
  blocking collectives  108 us (73%)
  waiting for transfers between devices  13.5 us (9%)
  Pallas kernels  11.6 us (8%)
  starting transfers between devices  8.58 us (6%)
  local copies, waits for them, and re-layouts  2.27 us (2%)
    all_to_all x4, blocking collectives, exchange(): return lax.all_to_all(x, axis, 0, 0)  108 us
    all_to_all x1, waiting for transfers between devices, exchange(): return lax.all_to_all(x, axis, 0, 0)  13.5 us
    all_to_all x1, starting transfers between devices, exchange(): return lax.all_to_all(x, axis, 0, 0)  8.58 us
    pallas_call x1, Pallas kernels, local(): call(forward_kernel, shape((N_AX, n + TAIL, BLK), bf16), [sums_acc], prod...  3.84 us
    pallas_call x1, Pallas kernels, local(): call(degree_kernel, shape((N_AX, TAIL, BLK), bf16), [pltpu.VMEM((STRIPE +...  3.12 us
    pallas_call x1, Pallas kernels, local(): call(adjoint_kernel, shape((N_AX, n + PIECE, BLK), bf16), [sums_acc], pro...  3.1 us
  transfers between devices with their start and end apart: 1, of which 1 were waited for; matrix products, arithmetic and copies ran while one was open for 0% of the time, Pallas kernels for 2%

profile of v1, /device:TPU:1, one launch (start us, length us, event | category | flops | bytes accessed | tf_op | source)
XLA Modules:
  0.0 146.3 jit_solution(16609277719485396641)
XLA Ops:
  0.6 0.0 copy-start
  0.6 2.2 %broadcast_in_dim.4 = bf16[16,256,128]{2,1,0:T(8,128)(2,1)} broadcast(bf16[256,128]{1,0:T(8,128)(2,1)} %x_ref.1), dimensions={1,2} | broadcast | bytes 1114112 | tf_op jit(solution)/shard_map/broadcast_in_dim | solution.py:143
  2.8 0.0 copy-start.5
  2.8 8.6 %all-to-all-start = ((bf16[16,256,128]{2,1,0:T(8,128)(2,1)}), bf16[16,256,128]{2,1,0:T(8,128)(2,1)}, u32[]{:S(2)}, u32[]{:S(2)}) async-start(bf16[16,256,128]{2,1,0:T(8,128)(2,1)} %broadcast_in_dim.4), calls=%async_computation | async-start | bytes 2097152 | tf_op jit(solution)/shard_map/all_to_all | solution.py:130
  12.1 0.0 copy-done
  12.1 0.0 copy-done.5
  12.1 0.0 copy-start.6
  12.1 3.1 %shard_map.103.deg_ref = bf16[16,16,128]{2,1,0:T(8,128)(2,1)S(1)} custom-call(s32[1,1]{1,0:T(1,128)S(6)} %copy.11.count_ref, s32[1,80]{1,0:T(1,128)S(1)} %bitcast.9, bf16[80,128,128]{2,1,0:T(8,128)(2,1)S(1)} %bitcast.6), custom_call_target="tpu_custom_call" | custom-call | flops 20971520 | bytes 2621440 | tf_op jit(solution)/shard_map/pallas_call | solution.py:144
  15.2 13.5 %all-to-all-done = bf16[16,256,128]{2,1,0:T(8,128)(2,1)} async-done(((bf16[16,256,128]{2,1,0:T(8,128)(2,1)}), bf16[16,256,128]{2,1,0:T(8,128)(2,1)}, u32[]{:S(2)}, u32[]{:S(2)}) %all-to-all-start) | async-done | bytes 1048608 | tf_op jit(solution)/shard_map/all_to_all | solution.py:130
  28.7 0.0 copy-done.6
  28.7 3.8 %shard_map.104 = bf16[16,272,128]{2,1,0:T(8,128)(2,1)S(1)} custom-call(s32[1,1]{1,0:T(1,128)S(6)} %copy.11.count_ref, s32[1,80]{1,0:T(1,128)S(1)} %bitcast.10, s32[1,80]{1,0:T(1,128)S(1)} %bitcast.12, bf16[80,128,128]{2,1,0:T(8,128)(2,1)S(1)} %bitcast.7, bf16[32,128,128]{2,1,0:T(8,128)(2,1)} %bitcast.3.x_ref, bf16[16,16,128]{2,1,0:T(8,128)(2,1)S(1)} %shard_map.103.deg_ref), custom_call_target="tpu_custom_call" | custom-call | flops 335544320 | bytes 5242880 | tf_op jit(solution)/shard_map/pallas_call | solution.py:151
  32.6 0.0 copy-start.1
  32.6 0.0 copy-start.2
  32.6 0.0 copy-start.3
  32.6 0.0 copy-start.4
  32.6 36.7 %all_to_all.25.got_ref = bf16[16,272,128]{2,1,0:T(8,128)(2,1)S(1)} all-to-all(bf16[16,272,128]{2,1,0:T(8,128)(2,1)S(1)} %shard_map.104), channel_id=1, replica_groups=mesh['row'=16,'col'=16] {'col'}, dimensions={0} | all-to-all | bytes 2228224 | tf_op jit(solution)/shard_map/all_to_all | solution.py:130
  69.3 0.0 copy-done.1
  69.3 0.0 copy-done.2
  69.3 0.0 copy-done.3
  69.3 0.0 copy-done.4
  69.3 0.6 shard_map.105
  69.9 32.1 %all_to_all.26.got_ref = bf16[16,288,128]{2,1,0:T(8,128)(2,1)S(1)} all-to-all(bf16[16,288,128]{2,1,0:T(8,128)(2,1)S(1)} %get-tuple-element.7), channel_id=1, replica_groups=mesh['row'=16,'col'=16] {'col'}, dimensions={0} | all-to-all | bytes 2359296 | tf_op jit(solution)/shard_map/all_to_all | solution.py:130
  102.0 3.1 %shard_map.106 = bf16[16,288,128]{2,1,0:T(8,128)(2,1)S(1)} custom-call(s32[1,1]{1,0:T(1,128)S(6)} %copy.11.count_ref, s32[1,80]{1,0:T(1,128)S(1)} %bitcast.11, s32[1,80]{1,0:T(1,128)S(1)} %bitcast.13, bf16[80,128,128]{2,1,0:T(8,128)(2,1)S(1)} %bitcast.8, bf16[16,288,128]{2,1,0:T(8,128)(2,1)S(1)} %all_to_all.26.got_ref), custom_call_target="tpu_custom_call" | custom-call | flops 335544320 | bytes 5242880 | tf_op jit(solution)/shard_map/pallas_call | solution.py:161
  105.1 27.9 %all_to_all.27.got_ref = bf16[16,288,128]{2,1,0:T(8,128)(2,1)S(1)} all-to-all(bf16[16,288,128]{2,1,0:T(8,128)(2,1)S(1)} %shard_map.106), channel_id=1, replica_groups=mesh['row'=16,'col'=16] {'row'}, dimensions={0} | all-to-all | bytes 2359296 | tf_op jit(solution)/shard_map/all_to_all | solution.py:130
  133.0 0.9 shard_map.107
  133.9 11.6 %all_to_all.28 = bf16[16,32,128]{2,1,0:T(8,128)(2,1)S(1)} all-to-all(bf16[16,32,128]{2,1,0:T(8,128)(2,1)S(1)} %broadcast_in_dim.5), channel_id=1, replica_groups=mesh['row'=16,'col'=16] {'col'}, dimensions={0} | all-to-all | bytes 262144 | tf_op jit(solution)/shard_map/all_to_all | solution.py:130
  145.5 0.7 pad_maximum_fusion
  (3 shorter events, 0.1 us)
Async XLA Ops:
  0.6 11.4 %copy-start = (bf16[1,1,80,128,128]{4,3,2,1,0:T(8,128)(2,1)S(1)}, bf16[1,1,80,128,128]{4,3,2,1,0:T(8,128)(2,1)}, u32[]{:S(2)}) copy-start(bf16[1,1,80,128,128]{4,3,2,1,0:T(8,128)(2,1)} %param.12) | copy-start | bytes 7864324
  2.8 9.2 %copy-start.5 = (s32[1,1,80]{2,1,0:T(1,128)S(1)}, s32[1,1,80]{2,1,0:T(1,128)}, u32[]{:S(2)}) copy-start(s32[1,1,80]{2,1,0:T(1,128)} %param.13) | copy-start | bytes 964
  2.8 25.9 %all-to-all-start = ((bf16[16,256,128]{2,1,0:T(8,128)(2,1)}), bf16[16,256,128]{2,1,0:T(8,128)(2,1)}, u32[]{:S(2)}, u32[]{:S(2)}) async-start(bf16[16,256,128]{2,1,0:T(8,128)(2,1)} %broadcast_in_dim.4), calls=%async_computation | async-start | bytes 2097152 | tf_op jit(solution)/shard_map/all_to_all | solution.py:130
  12.1 16.6 %copy-start.6 = (s32[1,1,80]{2,1,0:T(1,128)S(1)}, s32[1,1,80]{2,1,0:T(1,128)}, u32[]{:S(2)}) copy-start(s32[1,1,80]{2,1,0:T(1,128)} %param.14) | copy-start | bytes 964
  32.6 36.7 %copy-start.1 = (bf16[256,128]{1,0:T(8,128)(2,1)S(1)}, bf16[256,128]{1,0:T(8,128)(2,1)}, u32[]{:S(2)}) copy-start(bf16[256,128]{1,0:T(8,128)(2,1)} %x_ref.1) | copy-start | bytes 196612
  32.6 36.7 %copy-start.2 = (bf16[128,256]{1,0:T(8,128)(2,1)S(1)}, bf16[128,256]{1,0:T(8,128)(2,1)}, u32[]{:S(2)}) copy-start(bf16[128,256]{1,0:T(8,128)(2,1)} %ws_ref.3) | copy-start | bytes 196612
  32.6 36.7 %copy-start.3 = (bf16[256,256]{1,0:T(8,128)(2,1)S(1)}, bf16[256,256]{1,0:T(8,128)(2,1)}, u32[]{:S(2)}) copy-start(bf16[256,256]{1,0:T(8,128)(2,1)} %cot_ref.1) | copy-start | bytes 393220
  32.6 36.7 %copy-start.4 = (bf16[128,256]{1,0:T(8,128)(2,1)S(1)}, bf16[128,256]{1,0:T(8,128)(2,1)}, u32[]{:S(2)}) copy-start(bf16[128,256]{1,0:T(8,128)(2,1)} %wn_ref.1) | copy-start | bytes 196612

commit v2 on v1

--- a/solution.py
+++ b/solution.py
@@ -14,6 +14,7 @@
 UNROLL = 8
 PIECE = 32
 TAIL = 16
+HALF = N_AX // 2
 f32 = jnp.float32
 bf16 = jnp.bfloat16
 
@@ -40,6 +41,11 @@
         return carry
 
     lax.fori_loop(0, (count + UNROLL - 1) // UNROLL, group, 0)
+
+
+def wide(x):
+    high = x.astype(bf16)
+    return jnp.concatenate([high.astype(f32), x - high.astype(f32)], axis=0).astype(bf16)
 
 
 def degree_kernel(count_ref, rows_ref, adj_ref, out_ref, acc_ref):
@@ -54,8 +60,18 @@
         out_ref[d] = jnp.where(at < BPD, high.astype(f32), low.astype(f32)).astype(bf16)
 
 
-def forward_kernel(count_ref, rows_ref, cols_ref, adj_ref, x_ref, deg_ref, out_ref, acc_ref):
-    slots_loop(count_ref, rows_ref, acc_ref, lambda k: dot(adj_ref[k], x_ref[cols_ref[0, k]]))
+def forward_kernel(core_ref, count_ref, rows_ref, cols_ref, adj_ref, mine_ref, other_ref, deg_ref, out_ref, x_ref, acc_ref):
+    core = core_ref[0]
+    for p in range(HALF):
+        x_ref[2 * p + core] = mine_ref[p]
+        x_ref[2 * p + 1 - core] = other_ref[p]
+
+    def product(k):
+        col = cols_ref[0, k]
+        at = pl.multiple_of((col % BPD) * BLK, BLK)
+        return dot(adj_ref[k], x_ref[col // BPD, pl.ds(at, BLK), :])
+
+    slots_loop(count_ref, rows_ref, acc_ref, product)
     for d in range(N_AX):
         for b in range(BPD):
             out_ref[d, b * BLK : (b + 1) * BLK, :] = acc_ref[d * BPD + b].astype(bf16)
@@ -87,32 +103,44 @@
         out_ref[d, n:, :] = pieces[d * PIECE : (d + 1) * PIECE]
 
 
-def adjoint_kernel(count_ref, rows_ref, cols_ref, adj_ref, got_ref, out_ref, acc_ref):
+def adjoint_kernel(core_ref, count_ref, rows_ref, cols_ref, adj_ref, got_ref, keep_ref, grads_ref, send_ref, acc_ref):
     def product(k):
         row = rows_ref[0, k]
         at = pl.multiple_of((row % BPD) * BLK, BLK)
         return dot(got_ref[row // BPD, pl.ds(at, BLK), :], adj_ref[k])
 
     slots_loop(count_ref, cols_ref, acc_ref, product)
+    core = core_ref[0]
     n = BPD * BLK
     grads = got_ref[0, n:, :].astype(f32)
     for d in range(1, N_AX):
         grads += got_ref[d, n:, :].astype(f32)
-    grads = grads.astype(bf16)
-    for d in range(N_AX):
+    grads_ref[...] = grads
+    for p in range(HALF):
         for b in range(BPD):
-            out_ref[d, b * BLK : (b + 1) * BLK, :] = acc_ref[d * BPD + b].astype(bf16)
-        out_ref[d, n:, :] = grads
+            keep_ref[p, b * BLK : (b + 1) * BLK, :] = acc_ref[(2 * p + core) * BPD + b]
+            at = p * n + b * BLK
+            send_ref[at : at + BLK, :] = acc_ref[(2 * p + 1 - core) * BPD + b].astype(bf16)
+    send_ref[HALF * n :, :] = wide(grads)
+
+
+def merge_kernel(keep_ref, grads_ref, got_ref, out_ref):
+    n = BPD * BLK
+    tail = got_ref[HALF * n :, :].astype(f32)
+    grads = wide(grads_ref[...] + tail[:PIECE] + tail[PIECE:])
+    for p in range(HALF):
+        out_ref[p, :n, :] = (keep_ref[p] + got_ref[p * n : (p + 1) * n, :].astype(f32)).astype(bf16)
+        out_ref[p, n:, :] = grads
 
 
 def final_kernel(got_ref, dz_ref, ws_ref, out_ref, piece_ref):
     total = got_ref[0].astype(f32)
-    for d in range(1, N_AX):
+    for d in range(1, HALF):
         total += got_ref[d].astype(f32)
     n = BPD * BLK
     adjoint = jnp.concatenate([jnp.transpose(total[b * BLK : (b + 1) * BLK]) for b in range(BPD)], axis=0)
     out_ref[...] = dot(dz_ref[...], ws_ref[...], ((1,), (1,))) + adjoint
-    piece_ref[...] = total[n:].astype(bf16)
+    piece_ref[...] = total[n : n + PIECE] + total[n + PIECE :]
 
 
 def call(kernel, out, scratch=(), flops=0, moved=0):
@@ -126,8 +154,12 @@
     )
 
 
-def exchange(x, axis):
-    return lax.all_to_all(x, axis, 0, 0)
+def exchange(x, axis, groups=None):
+    return lax.all_to_all(x, axis, 0, 0, axis_index_groups=groups)
+
+
+SAME_CORE = [list(range(core, N_AX, 2)) for core in range(2)]
+SWAP_CORE = [(i, i ^ 1) for i in range(N_AX)]
 
 
 def local(features, cotangent, w_self, w_neigh, adj_blocks, block_rows, block_cols, block_count):
@@ -139,8 +171,10 @@
     product_flops = 2 * slots * BLK**3
     shape = jax.ShapeDtypeStruct
     sums_acc = pltpu.VMEM((STRIPE + 1, BLK, BLK), f32)
-
-    column = exchange(jnp.broadcast_to(features[None], (N_AX, n, width)), "row")
+    core = (lax.axis_index("row") % 2).astype(jnp.int32).reshape(1)
+
+    mine = exchange(jnp.broadcast_to(features[None], (HALF, n, width)), "row", SAME_CORE)
+    other = lax.ppermute(mine, "row", SWAP_CORE)
     degree = call(
         degree_kernel,
         shape((N_AX, TAIL, BLK), bf16),
@@ -149,25 +183,41 @@
         adj.size * 2,
     )(in_specs=[SMEM, SMEM, VMEM], out_specs=VMEM)(block_count, rows, adj)
     sums = call(
-        forward_kernel, shape((N_AX, n + TAIL, BLK), bf16), [sums_acc], product_flops, adj.size * 4
-    )(in_specs=[SMEM, SMEM, SMEM, VMEM, VMEM, VMEM], out_specs=VMEM)(
-        block_count, rows, cols, adj, column.reshape(STRIPE, BLK, width), degree
+        forward_kernel,
+        shape((N_AX, n + TAIL, BLK), bf16),
+        [pltpu.VMEM((N_AX, n, width), bf16), sums_acc],
+        product_flops,
+        adj.size * 4,
+    )(in_specs=[SMEM] * 4 + [VMEM] * 4, out_specs=VMEM)(
+        core, block_count, rows, cols, adj, mine, other, degree
     )
     sums = exchange(sums, "col")
     back, dz = call(
         dense_kernel, (shape((N_AX, n + PIECE, BLK), bf16), shape(cotangent.shape, bf16)), (), product_flops, adj.size
     )(in_specs=[VMEM] * 5, out_specs=(VMEM, VMEM))(sums, features, cotangent, w_self, w_neigh)
     back = exchange(back, "col")
-    adjoint = call(
-        adjoint_kernel, shape((N_AX, n + PIECE, BLK), bf16), [sums_acc], product_flops, adj.size * 4
-    )(in_specs=[SMEM, SMEM, SMEM, VMEM, VMEM], out_specs=VMEM)(block_count, rows, cols, adj, back)
-    adjoint = exchange(adjoint, "row")
+    keep, grads, send = call(
+        adjoint_kernel,
+        (
+            shape((HALF, n, width), f32),
+            shape((PIECE, BLK), f32),
+            shape((HALF * n + 2 * PIECE, BLK), bf16),
+        ),
+        [sums_acc],
+        product_flops,
+        adj.size * 4,
+    )(in_specs=[SMEM] * 4 + [VMEM] * 2, out_specs=(VMEM,) * 3)(core, block_count, rows, cols, adj, back)
+    send = lax.ppermute(send, "row", SWAP_CORE)
+    merged = call(merge_kernel, shape((HALF, n + 2 * PIECE, BLK), bf16), (), adj.size, adj.size)(
+        in_specs=[VMEM] * 3, out_specs=VMEM
+    )(keep, grads, send)
+    merged = exchange(merged, "row", SAME_CORE)
     grad_features, piece = call(
-        final_kernel, (shape((n, width), f32), shape((PIECE, BLK), bf16)), (), product_flops // 8, adj.size
-    )(in_specs=[VMEM] * 3, out_specs=(VMEM, VMEM))(adjoint, dz, w_self)
+        final_kernel, (shape((n, width), f32), shape((PIECE, BLK), f32)), (), product_flops // 8, adj.size
+    )(in_specs=[VMEM] * 3, out_specs=(VMEM, VMEM))(merged, dz, w_self)
     grads = exchange(jnp.broadcast_to(piece[None], (N_AX, PIECE, BLK)), "col")
     scale = (n * N_AX * N_AX) ** (-0.5)
-    grads = grads.reshape(2, 2 * width, BLK).astype(f32) * scale
+    grads = grads.reshape(2, 2 * width, BLK) * scale
     grads = jnp.concatenate([grads[0], grads[1]], axis=1)
     return (grad_features, grads[:width], grads[width:])
 

time: 147 us -> 139 us (0.946)
  waiting for transfers between devices: 13.5 us -> 1.56 us
  blocking collectives: 108 us -> 117 us
  Pallas kernels: 11.6 us -> 7.45 us
  starting transfers between devices: 8.58 us -> 6.23 us
    all_to_all x1 -> x0, waiting for transfers between devices: 13.5 us -> none  [exchange(): return lax.all_to_all(x, axis, 0, 0)]
    all_to_all x4 -> x5, blocking collectives: 108 us -> 117 us  [exchange(): return lax.all_to_all(x, axis, 0, 0, axis_index_groups=groups)]
    all_to_all x1 -> x0, starting transfers between devices: 8.58 us -> none  [exchange(): return lax.all_to_all(x, axis, 0, 0)]
    ppermute x0 -> x2, starting transfers between devices: none -> 6.23 us  [the longest x1 3.62 us: local(): send = lax.ppermute(send, 'row', SWAP_CORE)]
    pallas_call x3 -> x4, Pallas kernels: 7.84 us -> 4.99 us  [the longest x1 2.05 us: local(): call(forward_kernel, shape((N_AX, n + TAIL, BLK), bf16), [pltpu.VMEM((N_A...]
    unnamed x14 -> x16, local copies, waits for them, and re-layouts: 0.04 us -> 1.77 us
    ppermute x0 -> x2, waiting for transfers between devices: none -> 1.56 us  [the longest x1 1.56 us: local(): send = lax.ppermute(send, 'row', SWAP_CORE)]
  transfers between devices with their start and end apart: 1 -> 2, of which waited for: 1 -> 1; matrix products, arithmetic and copies ran while one was open for 0% -> 0% of each run, Pallas kernels for 2% -> 1%
where the time goes in v2:
time: 139 us; the launch traced here: 137 us
  blocking collectives  117 us (84%)
  Pallas kernels  7.45 us (5%)
  starting transfers between devices  6.23 us (4%)
  local copies, waits for them, and re-layouts  2.73 us (2%)
  waiting for transfers between devices  1.56 us (1%)
  between operations  1.44 us (1%)
    all_to_all x5, blocking collectives, exchange(): return lax.all_to_all(x, axis, 0, 0, axis_index_groups=groups)  117 us
    ppermute x1, starting transfers between devices, local(): send = lax.ppermute(send, 'row', SWAP_CORE)  3.62 us
  transfers between devices with their start and end apart: 2, of which 1 were waited for; matrix products, arithmetic and copies ran while one was open for 0% of the time, Pallas kernels for 1%

profile of v2, /device:TPU:1, one launch (start us, length us, event | category | flops | bytes accessed | tf_op | source)
XLA Modules:
  0.0 137.2 jit_solution(15345745937164813751)
XLA Ops:
  0.6 0.0 copy-start.6
  0.6 0.9 broadcast_in_dim.4
  1.6 16.9 %all_to_all.25.mine_ref = bf16[8,256,128]{2,1,0:T(8,128)(2,1)S(1)} all-to-all(bf16[8,256,128]{2,1,0:T(8,128)(2,1)S(1)} %broadcast_in_dim.4), channel_id=1, replica_groups={{0,32,64,96,128,160,192,224},{16,48,80,112,144,176,208,240},{1,33,65,97..., dimensions={0} | all-to-all | bytes 1048576 | tf_op jit(solution)/shard_map/all_to_all | solution.py:158
  18.4 2.6 %collective-permute-start = (bf16[8,256,128]{2,1,0:T(8,128)(2,1)S(1)}, bf16[8,256,128]{2,1,0:T(8,128)(2,1)S(1)}, u32[]{:S(2)}, u32[]{:S(2)}) collective-permute-start(bf16[8,256,128]{2,1,0:T(8,128)(2,1)S(1)} %all_to_all.25.mine_ref), channel_id=1, source_target_pairs={{0,16},{16,0},{32,48},{48,32},{64,80},{80,64},{96,112},{112,96},{1... | collective-permute-start | bytes 1572872 | tf_op jit(solution)/shard_map/ppermute | solution.py:177
  21.7 0.0 copy-done.6
  21.7 0.0 copy-start
  21.7 1.7 %copy-done = bf16[1,1,80,128,128]{4,3,2,1,0:T(8,128)(2,1)S(1)} copy-done((bf16[1,1,80,128,128]{4,3,2,1,0:T(8,128)(2,1)S(1)}, bf16[1,1,80,128,128]{4,3,2,1,0:T(8,128)(2,1)}, u32[]{:S(2)}) %copy-start) | copy-done | bytes 2621464
  23.4 0.0 copy-start.7
  23.4 1.8 %shard_map.103.deg_ref = bf16[16,16,128]{2,1,0:T(8,128)(2,1)S(1)} custom-call(s32[1,1]{1,0:T(1,128)S(6)} %copy.11.count_ref, s32[1,80]{1,0:T(1,128)S(1)} %bitcast.9, bf16[80,128,128]{2,1,0:T(8,128)(2,1)S(1)} %bitcast.6), custom_call_target="tpu_custom_call" | custom-call | flops 20971520 | bytes 2621440 | tf_op jit(solution)/shard_map/pallas_call | solution.py:178
  25.3 0.0 collective-permute-done.other_ref
  25.3 0.0 copy-done.7
  25.3 2.1 %shard_map.104 = bf16[16,272,128]{2,1,0:T(8,128)(2,1)S(1)} custom-call(s32[1]{0:T(128)} %bitcast.core_ref, s32[1,1]{1,0:T(1,128)S(6)} %copy.11.count_ref, s32[1,80]{1,0:T(1,128)S(1)} %bitcast.10, s32[1,80]{1,0:T(1,128)S(1)} %bitcast.12, bf16[80,128,128]{2,1,0:T(8,128)(2,1)S(1)} %bitcast.7, bf16[8,256,128]{2,1,0:T(8,128)(2,1)S(1)} %all_to_all.25.mine_ref, ...), custom_call_target="tpu_custom_call" | custom-call | flops 335544320 | bytes 5242880 | tf_op jit(solution)/shard_map/pallas_call | solution.py:185
  27.4 0.0 copy-start.2
  27.4 0.0 copy-start.3
  27.4 0.0 copy-start.4
  27.4 0.0 copy-start.5
  27.4 37.9 %all_to_all.26.got_ref = bf16[16,272,128]{2,1,0:T(8,128)(2,1)S(1)} all-to-all(bf16[16,272,128]{2,1,0:T(8,128)(2,1)S(1)} %shard_map.104), channel_id=1, replica_groups=mesh['row'=16,'col'=16] {'col'}, dimensions={0} | all-to-all | bytes 2228224 | tf_op jit(solution)/shard_map/all_to_all | solution.py:158
  65.3 0.0 copy-done.2
  65.3 0.0 copy-done.3
  65.3 0.0 copy-done.4
  65.3 0.0 copy-done.5
  65.3 0.0 copy-start.1
  65.4 0.6 shard_map.105
  66.0 32.7 %all_to_all.27.got_ref = bf16[16,288,128]{2,1,0:T(8,128)(2,1)S(1)} all-to-all(bf16[16,288,128]{2,1,0:T(8,128)(2,1)S(1)} %get-tuple-element.10), channel_id=1, replica_groups=mesh['row'=16,'col'=16] {'col'}, dimensions={0} | all-to-all | bytes 2359296 | tf_op jit(solution)/shard_map/all_to_all | solution.py:158
  98.7 0.0 copy-done.1
  98.7 1.9 %shard_map.106 = (f32[8,256,128]{2,1,0:T(8,128)S(1)}, f32[32,128]{1,0:T(8,128)S(1)}, bf16[2112,128]{1,0:T(8,128)(2,1)S(1)}) custom-call(s32[1]{0:T(128)} %bitcast.core_ref, s32[1,1]{1,0:T(1,128)S(6)} %copy.11.count_ref, s32[1,80]{1,0:T(1,128)S(1)} %bitcast.11, s32[1,80]{1,0:T(1,128)S(1)} %bitcast.13, bf16[80,128,128]{2,1,0:T(8,128)(2,1)S(1)} %bitcast.8, ...), custom_call_target="tpu_custom_call" | custom-call | flops 335544320 | bytes 5242880 | tf_op jit(solution)/shard_map/pallas_call | solution.py:199
  100.7 3.6 %collective-permute-start.1 = (bf16[2112,128]{1,0:T(8,128)(2,1)S(1)}, bf16[2112,128]{1,0:T(8,128)(2,1)S(1)}, u32[]{:S(2)}, u32[]{:S(2)}) collective-permute-start(bf16[2112,128]{1,0:T(8,128)(2,1)S(1)} %get-tuple-element.13), channel_id=1, source_target_pairs={{0,16},{16,0},{32,48},{48,32},{64,80},{80,64},{96,112},{112,96},{1... | collective-permute-start | bytes 1622024 | tf_op jit(solution)/shard_map/ppermute | solution.py:210
  104.3 1.6 %collective-permute-done.1.got_ref = bf16[2112,128]{1,0:T(8,128)(2,1)S(1)} collective-permute-done((bf16[2112,128]{1,0:T(8,128)(2,1)S(1)}, bf16[2112,128]{1,0:T(8,128)(2,1)S(1)}, u32[]{:S(2)}, u32[]{:S(2)}) %collective-permute-start.1) | collective-permute-done | bytes 540704 | tf_op jit(solution)/shard_map/ppermute | solution.py:210
  105.8 0.1 shard_map.107
  106.0 17.3 %all_to_all.28.got_ref = bf16[8,320,128]{2,1,0:T(8,128)(2,1)S(1)} all-to-all(bf16[8,320,128]{2,1,0:T(8,128)(2,1)S(1)} %shard_map.107), channel_id=1, replica_groups={{0,32,64,96,128,160,192,224},{16,48,80,112,144,176,208,240},{1,33,65,97..., dimensions={0} | all-to-all | bytes 1310720 | tf_op jit(solution)/shard_map/all_to_all | solution.py:158
  123.3 0.9 shard_map.108
  124.2 12.2 %all_to_all.29 = f32[16,32,128]{2,1,0:T(8,128)S(1)} all-to-all(f32[16,32,128]{2,1,0:T(8,128)S(1)} %broadcast_in_dim.5), channel_id=1, replica_groups=mesh['row'=16,'col'=16] {'col'}, dimensions={0} | all-to-all | bytes 524288 | tf_op jit(solution)/shard_map/all_to_all | solution.py:158
  136.4 0.7 pad_maximum_fusion
  (3 shorter events, 0.1 us)
Async XLA Ops:
  0.6 21.1 %copy-start.6 = (s32[1,1,80]{2,1,0:T(1,128)S(1)}, s32[1,1,80]{2,1,0:T(1,128)}, u32[]{:S(2)}) copy-start(s32[1,1,80]{2,1,0:T(1,128)} %param.13) | copy-start | bytes 964
  18.4 6.9 %collective-permute-start = (bf16[8,256,128]{2,1,0:T(8,128)(2,1)S(1)}, bf16[8,256,128]{2,1,0:T(8,128)(2,1)S(1)}, u32[]{:S(2)}, u32[]{:S(2)}) collective-permute-start(bf16[8,256,128]{2,1,0:T(8,128)(2,1)S(1)} %all_to_all.25.mine_ref), channel_id=1, source_target_pairs={{0,16},{16,0},{32,48},{48,32},{64,80},{80,64},{96,112},{112,96},{1... | collective-permute-start | bytes 1572872 | tf_op jit(solution)/shard_map/ppermute | solution.py:177
  21.7 1.7 %copy-start = (bf16[1,1,80,128,128]{4,3,2,1,0:T(8,128)(2,1)S(1)}, bf16[1,1,80,128,128]{4,3,2,1,0:T(8,128)(2,1)}, u32[]{:S(2)}) copy-start(bf16[1,1,80,128,128]{4,3,2,1,0:T(8,128)(2,1)} %param.12) | copy-start | bytes 7864324
  23.4 1.9 %copy-start.7 = (s32[1,1,80]{2,1,0:T(1,128)S(1)}, s32[1,1,80]{2,1,0:T(1,128)}, u32[]{:S(2)}) copy-start(s32[1,1,80]{2,1,0:T(1,128)} %param.14) | copy-start | bytes 964
  27.4 38.0 %copy-start.2 = (bf16[256,128]{1,0:T(8,128)(2,1)S(1)}, bf16[256,128]{1,0:T(8,128)(2,1)}, u32[]{:S(2)}) copy-start(bf16[256,128]{1,0:T(8,128)(2,1)} %x_ref.1) | copy-start | bytes 196612
  27.4 37.9 %copy-start.3 = (bf16[128,256]{1,0:T(8,128)(2,1)S(1)}, bf16[128,256]{1,0:T(8,128)(2,1)}, u32[]{:S(2)}) copy-start(bf16[128,256]{1,0:T(8,128)(2,1)} %ws_ref.3) | copy-start | bytes 196612
  27.4 37.9 %copy-start.4 = (bf16[256,256]{1,0:T(8,128)(2,1)S(1)}, bf16[256,256]{1,0:T(8,128)(2,1)}, u32[]{:S(2)}) copy-start(bf16[256,256]{1,0:T(8,128)(2,1)} %cot_ref.1) | copy-start | bytes 393220
  27.4 37.9 %copy-start.5 = (bf16[128,256]{1,0:T(8,128)(2,1)S(1)}, bf16[128,256]{1,0:T(8,128)(2,1)}, u32[]{:S(2)}) copy-start(bf16[128,256]{1,0:T(8,128)(2,1)} %wn_ref.1) | copy-start | bytes 196612
  65.3 33.4 %copy-start.1 = (bf16[1,1,80,128,128]{4,3,2,1,0:T(8,128)(2,1)S(1)}, bf16[1,1,80,128,128]{4,3,2,1,0:T(8,128)(2,1)}, u32[]{:S(2)}) copy-start(bf16[1,1,80,128,128]{4,3,2,1,0:T(8,128)(2,1)} %param.12) | copy-start | bytes 7864324
  100.7 5.2 %collective-permute-start.1 = (bf16[2112,128]{1,0:T(8,128)(2,1)S(1)}, bf16[2112,128]{1,0:T(8,128)(2,1)S(1)}, u32[]{:S(2)}, u32[]{:S(2)}) collective-permute-start(bf16[2112,128]{1,0:T(8,128)(2,1)S(1)} %get-tuple-element.13), channel_id=1, source_target_pairs={{0,16},{16,0},{32,48},{48,32},{64,80},{80,64},{96,112},{112,96},{1... | collective-permute-start | bytes 1622024 | tf_op jit(solution)/shard_map/ppermute | solution.py:210

commit v3 on v2

v3 whole, which is shorter than its diff:
```python
import functools

import jax
import jax.numpy as jnp
from jax import lax
from jax.experimental import pallas as pl
from jax.experimental.pallas import tpu as pltpu
from jax.sharding import PartitionSpec as P

BLK = 128
N_AX = 16
BPD = 2
STRIPE = N_AX * BPD
UNROLL = 8
PIECE = 32
TAIL = 16
HALF = N_AX // 2
Z = 8
NEAR = (0, 2, 6, 1, 7)
FAR = (4, 3, 5)
f32 = jnp.float32
bf16 = jnp.bfloat16

VMEM = pl.BlockSpec(memory_space=pltpu.VMEM)
SMEM = pl.BlockSpec(memory_space=pltpu.SMEM)
PARAMS = pltpu.CompilerParams(vmem_limit_bytes=24 * 1024 * 1024)


def dot(a, b, contract=((1,), (0,))):
    return lax.dot_general(a, b, (contract, ((), ())), preferred_element_type=f32)


def slots_loop(count_ref, index_ref, acc_ref, product):
    acc_ref[...] = jnp.zeros_like(acc_ref)
    count = count_ref[0, 0]

    def group(g, carry):
        base = g * UNROLL
        terms = [product(base + u) for u in range(UNROLL)]
        for u in range(UNROLL):
            k = base + u
            at = jnp.where(k < count, index_ref[0, k], STRIPE)
            acc_ref[at] += terms[u]
        return carry

    lax.fori_loop(0, (count + UNROLL - 1) // UNROLL, group, 0)


def wide(x):
    high = x.astype(bf16)
    return jnp.concatenate([high.astype(f32), x - high.astype(f32)], axis=0).astype(bf16)


def degree_kernel(count_ref, rows_ref, adj_ref, out_ref, acc_ref):
    ones = jnp.ones((8, BLK), bf16)
    slots_loop(count_ref, rows_ref, acc_ref, lambda k: dot(ones, adj_ref[k], ((1,), (1,))))
    for d in range(N_AX):
        parts = [acc_ref[d * BPD + b][0:1] for b in range(BPD)]
        both = jnp.concatenate(parts + parts + [jnp.zeros((TAIL - 2 * BPD, BLK), f32)], axis=0)
        high = both.astype(bf16)
        low = (both - high.astype(f32)).astype(bf16)
        at = lax.broadcasted_iota(jnp.int32, (TAIL, BLK), 0)
        out_ref[d] = jnp.where(at < BPD, high.astype(f32), low.astype(f32)).astype(bf16)


def forward_kernel(place_ref, count_ref, rows_ref, cols_ref, adj_ref, mine_ref, other_ref, deg_ref, out_ref, x_ref, acc_ref):
    core = place_ref[0]
    for p in range(HALF):
        x_ref[2 * p + core] = mine_ref[p]
        x_ref[2 * p + 1 - core] = other_ref[p]

    def product(k):
        col = cols_ref[0, k]
        at = pl.multiple_of((col % BPD) * BLK, BLK)
        return dot(adj_ref[k], x_ref[col // BPD, pl.ds(at, BLK), :])

    slots_loop(count_ref, rows_ref, acc_ref, product)
    for d in range(N_AX):
        for b in range(BPD):
            out_ref[d, b * BLK : (b + 1) * BLK, :] = acc_ref[d * BPD + b].astype(bf16)
        out_ref[d, BPD * BLK :, :] = deg_ref[d]


def narrow(parts):
    total = parts[0].astype(f32)
    for d in range(1, N_AX):
        total += parts[d].astype(f32)
    return total[:PIECE] + total[PIECE:]


def dense_kernel(got_ref, x_ref, cot_ref, ws_ref, wn_ref, back_ref, grads_ref, dz_ref):
    total = got_ref[0].astype(f32)
    for d in range(1, N_AX):
        total += got_ref[d].astype(f32)
    n = BPD * BLK
    degree = total[n : n + BPD] + total[n + BPD : n + 2 * BPD]
    norm_lanes = lax.rsqrt(1.0 + degree)
    norm = jnp.concatenate(
        [jnp.transpose(jnp.broadcast_to(norm_lanes[b : b + 1], (BLK, BLK))) for b in range(BPD)], axis=0
    )
    agg = (total[:n] * norm).astype(bf16)
    x = x_ref[...]
    pre = dot(x, ws_ref[...]) + dot(agg, wn_ref[...])
    sig = jax.nn.sigmoid(pre)
    dz = (cot_ref[...].astype(f32) * (sig * (1.0 + pre * (1.0 - sig)))).astype(bf16)
    dz_ref[...] = dz
    ds = dot(dz, wn_ref[...], ((1,), (1,))) * norm
    for b in range(BPD):
        back_ref[b * BLK : (b + 1) * BLK, :] = jnp.transpose(ds[b * BLK : (b + 1) * BLK]).astype(bf16)
    grads = jnp.concatenate([dot(x, dz, ((0,), (0,))), dot(agg, dz, ((0,), (0,)))], axis=0)
    pieces = jnp.concatenate([grads[:, :BLK], grads[:, BLK:]], axis=0)
    for d in range(N_AX):
        grads_ref[d] = wide(pieces[d * PIECE : (d + 1) * PIECE])


def stack_kernel(*refs):
    *parts, out_ref, again_ref = refs
    for j in range(out_ref.shape[0]):
        out_ref[j] = parts[j][...]
    again_ref[...] = parts[0][...]


def spread_kernel(got_ref, after_ref, out_ref):
    total = wide(narrow(got_ref))
    for d in range(N_AX):
        out_ref[d] = total


def piece_kernel(got_ref, out_ref):
    out_ref[...] = narrow(got_ref).astype(bf16)


def adjoint_kernel(
    place_ref, count_ref, rows_ref, cols_ref, adj_ref, near_ref, far_ref, near2_ref, far2_ref, after_ref, keep_ref, send_ref, x_ref, acc_ref
):
    z, yl = place_ref[1], place_ref[2]
    for mine, other, shifts in ((near_ref, near2_ref, NEAR), (far_ref, far2_ref, FAR)):
        for j, s in enumerate(shifts):
            at = 2 * ((z + Z - s) % Z)
            x_ref[at + yl] = mine[j]
            x_ref[at + 1 - yl] = other[j]

    def product(k):
        row = rows_ref[0, k]
        at = pl.multiple_of((row % BPD) * BLK, BLK)
        return dot(x_ref[row // BPD, pl.ds(at, BLK), :], adj_ref[k])

    slots_loop(count_ref, cols_ref, acc_ref, product)
    core = place_ref[0]
    n = BPD * BLK
    for p in range(HALF):
        for b in range(BPD):
            keep_ref[p, b * BLK : (b + 1) * BLK, :] = acc_ref[(2 * p + core) * BPD + b]
            send_ref[p, b * BLK : (b + 1) * BLK, :] = acc_ref[(2 * p + 1 - core) * BPD + b].astype(bf16)


def merge_kernel(place_ref, keep_ref, got_ref, piece_ref, piece2_ref, out_ref, both_ref):
    n = BPD * BLK
    core = place_ref[0]
    both_ref[core] = piece_ref[...]
    both_ref[1 - core] = piece2_ref[...]
    for p in range(HALF):
        out_ref[p, :n, :] = (keep_ref[p] + got_ref[p].astype(f32)).astype(bf16)
        for c in range(2):
            out_ref[p, n + c * PIECE : n + (c + 1) * PIECE, :] = both_ref[c]


def final_kernel(scale, got_ref, dz_ref, ws_ref, out_ref, self_ref, neigh_ref):
    n = BPD * BLK
    total = got_ref[0, :n, :].astype(f32)
    for d in range(1, HALF):
        total += got_ref[d, :n, :].astype(f32)
    adjoint = jnp.concatenate([jnp.transpose(total[b * BLK : (b + 1) * BLK]) for b in range(BPD)], axis=0)
    out_ref[...] = dot(dz_ref[...], ws_ref[...], ((1,), (1,))) + adjoint
    per = BLK // (2 * PIECE)
    for d in range(HALF):
        quarter, at = d // per, (d % per) * 2 * PIECE
        lanes = (quarter // 2) * BLK
        into = neigh_ref if quarter % 2 else self_ref
        into[at : at + 2 * PIECE, lanes : lanes + BLK] = got_ref[d, n:, :].astype(f32) * scale


def call(kernel, out, scratch=(), flops=0, moved=0):
    return functools.partial(
        pl.pallas_call,
        kernel,
        out_shape=out,
        scratch_shapes=list(scratch),
        compiler_params=PARAMS,
        cost_estimate=pl.CostEstimate(flops=flops, bytes_accessed=moved, transcendentals=0),
    )


def exchange(x, axis, groups=None):
    return lax.all_to_all(x, axis, 0, 0, axis_index_groups=groups)


SAME_CORE = [list(range(core, N_AX, 2)) for core in range(2)]
SWAP = [(i, i ^ 1) for i in range(N_AX)]


def z_shift(x, s):
    return lax.ppermute(x, "col", [(i, (i + 2 * s) % N_AX) for i in range(N_AX)])


def local(features, cotangent, w_self, w_neigh, adj_blocks, block_rows, block_cols, block_count):
    adj = adj_blocks[0, 0]
    rows = block_rows[0]
    cols = block_cols[0]
    slots = adj.shape[0]
    n, width = features.shape
    product_flops = 2 * slots * BLK**3
    shape = jax.ShapeDtypeStruct
    sums_acc = pltpu.VMEM((STRIPE + 1, BLK, BLK), f32)
    stripe = pltpu.VMEM((N_AX, n, width), bf16)
    row_at, col_at = lax.axis_index("row"), lax.axis_index("col")
    place = jnp.stack([row_at % 2, col_at // 2, col_at % 2]).astype(jnp.int32)

    mine = exchange(jnp.broadcast_to(features[None], (HALF, n, width)), "row", SAME_CORE)
    degree = call(
        degree_kernel,
        shape((N_AX, TAIL, BLK), bf16),
        [pltpu.VMEM((STRIPE + 1, 8, BLK), f32)],
        product_flops // 16,
        adj.size * 2,
    )(in_specs=[SMEM, SMEM, VMEM], out_specs=VMEM)(block_count, rows, adj)
    mine, degree = lax.optimization_barrier((mine, degree))
    other = lax.ppermute(mine, "row", SWAP)
    sums = call(
        forward_kernel, shape((N_AX, n + TAIL, BLK), bf16), [stripe, sums_acc], product_flops, adj.size * 4
    )(in_specs=[SMEM] * 4 + [VMEM] * 4, out_specs=VMEM)(
        place, block_count, rows, cols, adj, mine, other, degree
    )
    sums = exchange(sums, "col")
    back, grads, dz = call(
        dense_kernel,
        (shape((n, BLK), bf16), shape((N_AX, 2 * PIECE, BLK), bf16), shape(cotangent.shape, bf16)),
        (),
        product_flops,
        adj.size,
    )(in_specs=[VMEM] * 5, out_specs=(VMEM,) * 3)(sums, features, cotangent, w_self, w_neigh)

    grads = exchange(grads, "row")
    near = [back] + [z_shift(back, s) for s in NEAR[1:]]
    near, back = call(
        stack_kernel, (shape((len(NEAR), n, BLK), bf16), shape((n, BLK), bf16)), (), adj.size, adj.size
    )(in_specs=[VMEM] * len(NEAR), out_specs=(VMEM, VMEM))(*near)
    far = jnp.stack([z_shift(back, s) for s in FAR])
    near2 = lax.ppermute(near, "col", SWAP)
    far2 = lax.ppermute(far, "col", SWAP)
    grads = call(spread_kernel, shape(grads.shape, bf16), (), adj.size, adj.size)(
        in_specs=[VMEM, pl.BlockSpec(memory_space=pl.ANY)], out_specs=VMEM
    )(grads, near)
    grads = exchange(grads, "col")
    piece = call(piece_kernel, shape((PIECE, BLK), bf16), (), adj.size, adj.size)(in_specs=[VMEM], out_specs=VMEM)(grads)
    piece2 = lax.ppermute(piece, "row", SWAP)

    keep, send = call(
        adjoint_kernel,
        (shape((HALF, n, width), f32), shape((HALF, n, width), bf16)),
        [stripe, sums_acc],
        product_flops,
        adj.size * 4,
    )(in_specs=[SMEM] * 4 + [VMEM] * 5 + [pl.BlockSpec(memory_space=pl.ANY)], out_specs=(VMEM,) * 2)(
        place, block_count, rows, cols, adj, near, far, near2, far2, piece
    )
    send = lax.ppermute(send, "row", SWAP)
    merged = call(
        merge_kernel,
        shape((HALF, n + 2 * PIECE, BLK), bf16),
        [pltpu.VMEM((2, PIECE, BLK), bf16)],
        adj.size,
        adj.size,
    )(in_specs=[SMEM] + [VMEM] * 4, out_specs=VMEM)(place, keep, send, piece, piece2)
    merged = exchange(merged, "row", SAME_CORE)
    scale = (n * N_AX * N_AX) ** (-0.5)
    return call(
        functools.partial(final_kernel, scale),
        (shape((n, width), f32), shape(w_self.shape, f32), shape(w_neigh.shape, f32)),
        (),
        product_flops // 8,
        adj.size,
    )(in_specs=[VMEM] * 3, out_specs=(VMEM,) * 3)(merged, dz, w_self)


def solution(mesh):
    placed = (
        P(("row", "col"), None),
        P(("row", "col"), None),
        P(),
        P(),
        P("row", "col", None, None, None),
        P("row", "col", None),
        P("row", "col", None),
        P("row", "col"),
    )
    return jax.shard_map(
        local,
        mesh=mesh,
        in_specs=placed,
        out_specs=(P(("row", "col"), None), P(), P()),
        check_vma=False,
    )
```

time: 139 us -> 136 us (0.978)
  blocking collectives: 117 us -> 55.2 us
  starting transfers between devices: 6.23 us -> 39.8 us
  waiting for transfers between devices: 1.56 us -> 23.4 us
  Pallas kernels: 7.45 us -> 10.5 us
  local copies, waits for them, and re-layouts: 2.73 us -> 4.17 us
    all_to_all x5 -> x2, blocking collectives: 117 us -> 55.2 us  [exchange(): return lax.all_to_all(x, axis, 0, 0, axis_index_groups=groups)]
    all_to_all x0 -> x3, starting transfers between devices: none -> 18.6 us  [exchange(): return lax.all_to_all(x, axis, 0, 0, axis_index_groups=groups)]
    ppermute x2 -> x12, waiting for transfers between devices: 1.56 us -> 17 us  [the longest x7 8.98 us: z_shift(): lax.ppermute(x, 'col', [(i, (i + 2 * s) % N_AX) for i in range(N_AX)])]
    ppermute x2 -> x12, starting transfers between devices: 6.23 us -> 21.2 us  [the longest x7 16 us: z_shift(): lax.ppermute(x, 'col', [(i, (i + 2 * s) % N_AX) for i in range(N_AX)])]
    all_to_all x0 -> x3, waiting for transfers between devices: none -> 6.37 us  [exchange(): return lax.all_to_all(x, axis, 0, 0, axis_index_groups=groups)]
    pallas_call x5 -> x8, Pallas kernels: 5.6 us -> 8.67 us  [the longest x1 2.54 us: local(): call(forward_kernel, shape((N_AX, n + TAIL, BLK), bf16), [stripe, sums_ac...]
  transfers between devices with their start and end apart: 2 -> 15, of which waited for: 1 -> 10; matrix products, arithmetic and copies ran while one was open for 0% -> 0% of each run, Pallas kernels for 1% -> 1%
where the time goes in v3:
time: 136 us; the launch traced here: 135 us
  blocking collectives  55.2 us (41%)
  starting transfers between devices  39.8 us (29%)
  waiting for transfers between devices  23.4 us (17%)
  Pallas kernels  10.5 us (8%)
  local copies, waits for them, and re-layouts  4.17 us (3%)
  between operations  1.44 us (1%)
    all_to_all x2, blocking collectives, exchange(): return lax.all_to_all(x, axis, 0, 0, axis_index_groups=groups)  55.2 us
    all_to_all x3, starting transfers between devices, exchange(): return lax.all_to_all(x, axis, 0, 0, axis_index_groups=groups)  18.6 us
    ppermute x7, starting transfers between devices, z_shift(): lax.ppermute(x, 'col', [(i, (i + 2 * s) % N_AX) for i in range(N_AX)])  16 us
    ppermute x7, waiting for transfers between devices, z_shift(): lax.ppermute(x, 'col', [(i, (i + 2 * s) % N_AX) for i in range(N_AX)])  8.98 us
    all_to_all x3, waiting for transfers between devices, exchange(): return lax.all_to_all(x, axis, 0, 0, axis_index_groups=groups)  6.37 us
    ppermute x1, waiting for transfers between devices, local(): far2 = lax.ppermute(far, 'col', SWAP)  5.01 us
  transfers between devices with their start and end apart: 15, of which 10 were waited for; matrix products, arithmetic and copies ran while one was open for 0% of the time, Pallas kernels for 1%

profile of v3, /device:TPU:1, one launch (start us, length us, event | category | flops | bytes accessed | tf_op | source)
XLA Modules:
  0.0 134.6 jit_solution(3541182351208737631)
XLA Ops:
  0.6 0.0 copy-start.8
  0.6 1.7 %broadcast_in_dim.2 = bf16[8,256,128]{2,1,0:T(8,128)(2,1)} broadcast(bf16[256,128]{1,0:T(8,128)(2,1)} %x_ref.1), dimensions={1,2} | broadcast | bytes 589824 | tf_op jit(solution)/shard_map/broadcast_in_dim | solution.py:219
  2.4 7.5 %all-to-all-start = ((bf16[8,256,128]{2,1,0:T(8,128)(2,1)}), bf16[8,256,128]{2,1,0:T(8,128)(2,1)S(1)}, u32[]{:S(2)}, u32[]{:S(2)}) async-start(bf16[8,256,128]{2,1,0:T(8,128)(2,1)} %broadcast_in_dim.2), calls=%async_computation | async-start | bytes 1048576 | tf_op jit(solution)/shard_map/all_to_all | solution.py:195
  10.5 0.0 copy-done.8
  10.5 0.0 copy-start
  10.5 1.7 %copy-done = bf16[1,1,80,128,128]{4,3,2,1,0:T(8,128)(2,1)S(1)} copy-done((bf16[1,1,80,128,128]{4,3,2,1,0:T(8,128)(2,1)S(1)}, bf16[1,1,80,128,128]{4,3,2,1,0:T(8,128)(2,1)}, u32[]{:S(2)}) %copy-start) | copy-done | bytes 2621464
  12.3 0.0 copy-start.1
  12.3 0.0 copy-start.9
  12.3 1.9 %shard_map.103.deg_ref = bf16[16,16,128]{2,1,0:T(8,128)(2,1)S(1)} custom-call(s32[1,1]{1,0:T(1,128)S(6)} %copy.11.count_ref, s32[1,80]{1,0:T(1,128)S(1)} %bitcast.12, bf16[80,128,128]{2,1,0:T(8,128)(2,1)S(1)} %bitcast.9), custom_call_target="tpu_custom_call" | custom-call | flops 20971520 | bytes 2621440 | tf_op jit(solution)/shard_map/pallas_call | solution.py:220
  14.1 5.9 %all-to-all-done.mine_ref = bf16[8,256,128]{2,1,0:T(8,128)(2,1)S(1)} async-done(((bf16[8,256,128]{2,1,0:T(8,128)(2,1)}), bf16[8,256,128]{2,1,0:T(8,128)(2,1)S(1)}, u32[]{:S(2)}, u32[]{:S(2)}) %all-to-all-start) | async-done | bytes 524320 | tf_op jit(solution)/shard_map/all_to_all | solution.py:195
  20.1 1.6 %collective-permute-start = (bf16[8,256,128]{2,1,0:T(8,128)(2,1)S(1)}, bf16[8,256,128]{2,1,0:T(8,128)(2,1)}, u32[]{:S(2)}, u32[]{:S(2)}) collective-permute-start(bf16[8,256,128]{2,1,0:T(8,128)(2,1)S(1)} %all-to-all-done.mine_ref), channel_id=1, source_target_pairs={{0,16},{16,0},{32,48},{48,32},{64,80},{80,64},{96,112},{112,96},{1... | collective-permute-start | bytes 1572872 | tf_op jit(solution)/shard_map/ppermute | solution.py:228
  21.7 0.1 pad_add_fusion.place_ref
  21.8 1.6 %collective-permute-done.other_ref = bf16[8,256,128]{2,1,0:T(8,128)(2,1)} collective-permute-done((bf16[8,256,128]{2,1,0:T(8,128)(2,1)S(1)}, bf16[8,256,128]{2,1,0:T(8,128)(2,1)}, u32[]{:S(2)}, u32[]{:S(2)}) %collective-permute-start) | collective-permute-done | bytes 524320 | tf_op jit(solution)/shard_map/ppermute | solution.py:228
  23.4 0.0 copy-done.1
  23.4 0.0 copy-done.9
  23.4 2.5 %shard_map.104 = bf16[16,272,128]{2,1,0:T(8,128)(2,1)S(1)} custom-call(s32[3]{0:T(128)S(1)} %pad_add_fusion.place_ref, s32[1,1]{1,0:T(1,128)S(6)} %copy.11.count_ref, s32[1,80]{1,0:T(1,128)S(1)} %bitcast.13, s32[1,80]{1,0:T(1,128)S(1)} %bitcast.15, bf16[80,128,128]{2,1,0:T(8,128)(2,1)S(1)} %bitcast.10, bf16[8,256,128]{2,1,0:T(8,128)(2,1)S(1)} %all-to-all-done.mine_ref, ...), custom_call_target="tpu_custom_call" | custom-call | flops 335544320 | bytes 5242880 | tf_op jit(solution)/shard_map/pallas_call | solution.py:229
  25.9 0.0 copy-start.2
  25.9 0.0 copy-start.3
  25.9 0.0 copy-start.6
  26.0 0.0 copy-start.7
  26.0 37.9 %all_to_all.25.got_ref = bf16[16,272,128]{2,1,0:T(8,128)(2,1)S(1)} all-to-all(bf16[16,272,128]{2,1,0:T(8,128)(2,1)S(1)} %shard_map.104), channel_id=1, replica_groups=mesh['row'=16,'col'=16] {'col'}, dimensions={0} | all-to-all | bytes 2228224 | tf_op jit(solution)/shard_map/all_to_all | solution.py:195
  63.9 0.0 copy-done.2
  63.9 0.0 copy-done.3
  63.9 0.0 copy-done.6
  63.9 0.0 copy-done.7
  63.9 1.3 shard_map.105
  65.2 0.0 copy-start.4
  65.2 0.7 copy-done.4
  65.8 7.5 %all-to-all-start.2 = ((bf16[16,64,128]{2,1,0:T(8,128)(2,1)}), bf16[16,64,128]{2,1,0:T(8,128)(2,1)S(1)}, u32[]{:S(2)}, u32[]{:S(2)}) async-start(bf16[16,64,128]{2,1,0:T(8,128)(2,1)} %get-tuple-element.17), calls=%async_computation.2 | async-start | bytes 524288 | tf_op jit(solution)/shard_map/all_to_all | solution.py:195
  73.3 0.3 collective-permute-start.1
  73.6 3.2 %collective-permute-start.2 = (bf16[256,128]{1,0:T(8,128)(2,1)S(1)}, bf16[256,128]{1,0:T(8,128)(2,1)S(1)}, u32[]{:S(2)}, u32[]{:S(2)}) collective-permute-start(bf16[256,128]{1,0:T(8,128)(2,1)S(1)} %get-tuple-element.14.refs_0_), channel_id=1, source_target_pairs={{0,12},{1,13},{2,14},{3,15},{4,0},{5,1},{6,2},{7,3},{8,4},{9,5},{1... | collective-permute-start | bytes 196616 | tf_op jit(solution)/shard_map/ppermute | solution.py:203
  76.8 0.2 collective-permute-start.3
  77.0 2.5 %collective-permute-start.4 = (bf16[256,128]{1,0:T(8,128)(2,1)S(1)}, bf16[256,128]{1,0:T(8,128)(2,1)S(1)}, u32[]{:S(2)}, u32[]{:S(2)}) collective-permute-start(bf16[256,128]{1,0:T(8,128)(2,1)S(1)} %get-tuple-element.14.refs_0_), channel_id=1, source_target_pairs={{0,14},{1,15},{2,0},{3,1},{4,2},{5,3},{6,4},{7,5},{8,6},{9,7},{10,... | collective-permute-start | bytes 196616 | tf_op jit(solution)/shard_map/ppermute | solution.py:203
  79.5 0.7 collective-permute-done.1.refs_1_
  80.2 0.0 collective-permute-done.2.refs_2_
  80.2 1.3 collective-permute-done.3.refs_3_
  81.5 0.2 collective-permute-done.4.refs_4_
  81.7 0.4 all-to-all-done.2.got_ref
  82.2 0.8 shard_map.107
  82.9 3.7 %all-to-all-start.3 = ((bf16[16,64,128]{2,1,0:T(8,128)(2,1)}), bf16[16,64,128]{2,1,0:T(8,128)(2,1)S(1)}, u32[]{:S(2)}, u32[]{:S(2)}) async-start(bf16[16,64,128]{2,1,0:T(8,128)(2,1)} %shard_map.107), calls=%async_computation.3 | async-start | bytes 524288 | tf_op jit(solution)/shard_map/all_to_all | solution.py:195
  86.6 5.3 %collective-permute-start.5 = (bf16[256,128]{1,0:T(8,128)(2,1)S(1)}, bf16[256,128]{1,0:T(8,128)(2,1)S(1)}, u32[]{:S(2)}, u32[]{:S(2)}) collective-permute-start(bf16[256,128]{1,0:T(8,128)(2,1)S(1)} %get-tuple-element.16), channel_id=1, source_target_pairs={{0,8},{1,9},{2,10},{3,11},{4,12},{5,13},{6,14},{7,15},{8,0},{9,1},... | collective-permute-start | bytes 196616 | tf_op jit(solution)/shard_map/ppermute | solution.py:203
  91.9 0.3 collective-permute-start.6
  92.2 4.2 %collective-permute-start.7 = (bf16[256,128]{1,0:T(8,128)(2,1)S(1)}, bf16[256,128]{1,0:T(8,128)(2,1)S(1)}, u32[]{:S(2)}, u32[]{:S(2)}) collective-permute-start(bf16[256,128]{1,0:T(8,128)(2,1)S(1)} %get-tuple-element.16), channel_id=1, source_target_pairs={{0,10},{1,11},{2,12},{3,13},{4,14},{5,15},{6,0},{7,1},{8,2},{9,3},... | collective-permute-start | bytes 196616 | tf_op jit(solution)/shard_map/ppermute | solution.py:203
  96.4 1.2 collective-permute-start.8
  97.6 0.9 collective-permute-done.5
  98.4 5.9 %collective-permute-done.6 = bf16[256,128]{1,0:T(8,128)(2,1)S(1)} collective-permute-done((bf16[256,128]{1,0:T(8,128)(2,1)S(1)}, bf16[256,128]{1,0:T(8,128)(2,1)S(1)}, u32[]{:S(2)}, u32[]{:S(2)}) %collective-permute-start.6) | collective-permute-done | bytes 65568 | tf_op jit(solution)/shard_map/ppermute | solution.py:203
  104.4 0.0 collective-permute-done.7
  104.4 0.1 collective-permute-start.9
  104.5 0.0 all-to-all-done.3.got_ref
  104.6 5.0 %collective-permute-done.9.far2_ref = bf16[3,256,128]{2,1,0:T(8,128)(2,1)} collective-permute-done((bf16[3,256,128]{2,1,0:T(8,128)(2,1)S(1)}, bf16[3,256,128]{2,1,0:T(8,128)(2,1)}, u32[]{:S(2)}, u32[]{:S(2)}) %collective-permute-start.9) | collective-permute-done | bytes 196640 | tf_op jit(solution)/shard_map/ppermute | solution.py:250
  109.6 0.0 collective-permute-done.8.near2_ref
  109.6 2.5 %shard_map.109 = (f32[8,256,128]{2,1,0:T(8,128)S(1)}, bf16[8,256,128]{2,1,0:T(8,128)(2,1)S(1)}) custom-call(s32[3]{0:T(128)S(1)} %pad_add_fusion.place_ref, s32[1,1]{1,0:T(1,128)S(6)} %copy.11.count_ref, s32[1,80]{1,0:T(1,128)S(1)} %bitcast.14, s32[1,80]{1,0:T(1,128)S(1)} %bitcast.16, bf16[80,128,128]{2,1,0:T(8,128)(2,1)S(1)} %bitcast.11, ...), custom_call_target="tpu_custom_call" | custom-call | flops 335544320 | bytes 5242880 | tf_op jit(solution)/shard_map/pallas_call | solution.py:258
  112.1 2.2 %collective-permute-start.10 = (bf16[8,256,128]{2,1,0:T(8,128)(2,1)S(1)}, bf16[8,256,128]{2,1,0:T(8,128)(2,1)S(1)}, u32[]{:S(2)}, u32[]{:S(2)}) collective-permute-start(bf16[8,256,128]{2,1,0:T(8,128)(2,1)S(1)} %get-tuple-element.19), channel_id=1, source_target_pairs={{0,16},{16,0},{32,48},{48,32},{64,80},{80,64},{96,112},{112,96},{1... | collective-permute-start | bytes 1572872 | tf_op jit(solution)/shard_map/ppermute | solution.py:267
  114.3 0.1 collective-permute-start.11
  114.4 1.4 %collective-permute-done.11.piece2_ref = bf16[32,128]{1,0:T(8,128)(2,1)S(1)} collective-permute-done((bf16[32,128]{1,0:T(8,128)(2,1)S(1)}, bf16[32,128]{1,0:T(8,128)(2,1)S(1)}, u32[]{:S(2)}, u32[]{:S(2)}) %collective-permute-start.11) | collective-permute-done | bytes 8224 | tf_op jit(solution)/shard_map/ppermute | solution.py:256
  115.9 0.0 collective-permute-done.10.got_ref
  115.9 0.6 shard_map.110
  116.5 0.0 copy-start.5
  116.5 17.3 %all_to_all.26.got_ref = bf16[8,320,128]{2,1,0:T(8,128)(2,1)S(1)} all-to-all(bf16[8,320,128]{2,1,0:T(8,128)(2,1)S(1)} %shard_map.110), channel_id=1, replica_groups={{0,32,64,96,128,160,192,224},{16,48,80,112,144,176,208,240},{1,33,65,97..., dimensions={0} | all-to-all | bytes 1310720 | tf_op jit(solution)/shard_map/all_to_all | solution.py:195
  133.8 0.0 copy-done.5
  133.8 0.9 shard_map.111
  (3 shorter events, 0.1 us)
Async XLA Ops:
  0.6 9.9 %copy-start.8 = (s32[1,1,80]{2,1,0:T(1,128)S(1)}, s32[1,1,80]{2,1,0:T(1,128)}, u32[]{:S(2)}) copy-start(s32[1,1,80]{2,1,0:T(1,128)} %param.13) | copy-start | bytes 964
  2.4 17.7 %all-to-all-start = ((bf16[8,256,128]{2,1,0:T(8,128)(2,1)}), bf16[8,256,128]{2,1,0:T(8,128)(2,1)S(1)}, u32[]{:S(2)}, u32[]{:S(2)}) async-start(bf16[8,256,128]{2,1,0:T(8,128)(2,1)} %broadcast_in_dim.2), calls=%async_computation | async-start | bytes 1048576 | tf_op jit(solution)/shard_map/all_to_all | solution.py:195
  10.5 1.7 %copy-start = (bf16[1,1,80,128,128]{4,3,2,1,0:T(8,128)(2,1)S(1)}, bf16[1,1,80,128,128]{4,3,2,1,0:T(8,128)(2,1)}, u32[]{:S(2)}) copy-start(bf16[1,1,80,128,128]{4,3,2,1,0:T(8,128)(2,1)} %param.12) | copy-start | bytes 7864324
  12.3 11.1 %copy-start.1 = (bf16[1,1,80,128,128]{4,3,2,1,0:T(8,128)(2,1)S(1)}, bf16[1,1,80,128,128]{4,3,2,1,0:T(8,128)(2,1)}, u32[]{:S(2)}) copy-start(bf16[1,1,80,128,128]{4,3,2,1,0:T(8,128)(2,1)} %param.12) | copy-start | bytes 7864324
  12.3 11.1 %copy-start.9 = (s32[1,1,80]{2,1,0:T(1,128)S(1)}, s32[1,1,80]{2,1,0:T(1,128)}, u32[]{:S(2)}) copy-start(s32[1,1,80]{2,1,0:T(1,128)} %param.14) | copy-start | bytes 964
  20.1 3.3 %collective-permute-start = (bf16[8,256,128]{2,1,0:T(8,128)(2,1)S(1)}, bf16[8,256,128]{2,1,0:T(8,128)(2,1)}, u32[]{:S(2)}, u32[]{:S(2)}) collective-permute-start(bf16[8,256,128]{2,1,0:T(8,128)(2,1)S(1)} %all-to-all-done.mine_ref), channel_id=1, source_target_pairs={{0,16},{16,0},{32,48},{48,32},{64,80},{80,64},{96,112},{112,96},{1... | collective-permute-start | bytes 1572872 | tf_op jit(solution)/shard_map/ppermute | solution.py:228
  25.9 37.9 %copy-start.2 = (bf16[256,128]{1,0:T(8,128)(2,1)S(1)}, bf16[256,128]{1,0:T(8,128)(2,1)}, u32[]{:S(2)}) copy-start(bf16[256,128]{1,0:T(8,128)(2,1)} %x_ref.1) | copy-start | bytes 196612
  25.9 37.9 %copy-start.3 = (bf16[128,256]{1,0:T(8,128)(2,1)S(1)}, bf16[128,256]{1,0:T(8,128)(2,1)}, u32[]{:S(2)}) copy-start(bf16[128,256]{1,0:T(8,128)(2,1)} %ws_ref.3) | copy-start | bytes 196612
  25.9 37.9 %copy-start.6 = (bf16[256,256]{1,0:T(8,128)(2,1)S(1)}, bf16[256,256]{1,0:T(8,128)(2,1)}, u32[]{:S(2)}) copy-start(bf16[256,256]{1,0:T(8,128)(2,1)} %cot_ref.1) | copy-start | bytes 393220
  26.0 37.9 %copy-start.7 = (bf16[128,256]{1,0:T(8,128)(2,1)S(1)}, bf16[128,256]{1,0:T(8,128)(2,1)}, u32[]{:S(2)}) copy-start(bf16[128,256]{1,0:T(8,128)(2,1)} %wn_ref.1) | copy-start | bytes 196612
  65.2 0.7 copy-start.4
  65.8 16.4 %all-to-all-start.2 = ((bf16[16,64,128]{2,1,0:T(8,128)(2,1)}), bf16[16,64,128]{2,1,0:T(8,128)(2,1)S(1)}, u32[]{:S(2)}, u32[]{:S(2)}) async-start(bf16[16,64,128]{2,1,0:T(8,128)(2,1)} %get-tuple-element.17), calls=%async_computation.2 | async-start | bytes 524288 | tf_op jit(solution)/shard_map/all_to_all | solution.py:195
  73.3 6.9 %collective-permute-start.1 = (bf16[256,128]{1,0:T(8,128)(2,1)S(1)}, bf16[256,128]{1,0:T(8,128)(2,1)S(1)}, u32[]{:S(2)}, u32[]{:S(2)}) collective-permute-start(bf16[256,128]{1,0:T(8,128)(2,1)S(1)} %get-tuple-element.14.refs_0_), channel_id=1, source_target_pairs={{0,4},{1,5},{2,6},{3,7},{4,8},{5,9},{6,10},{7,11},{8,12},{9,13},{1... | collective-permute-start | bytes 196616 | tf_op jit(solution)/shard_map/ppermute | solution.py:203
  73.6 6.6 %collective-permute-start.2 = (bf16[256,128]{1,0:T(8,128)(2,1)S(1)}, bf16[256,128]{1,0:T(8,128)(2,1)S(1)}, u32[]{:S(2)}, u32[]{:S(2)}) collective-permute-start(bf16[256,128]{1,0:T(8,128)(2,1)S(1)} %get-tuple-element.14.refs_0_), channel_id=1, source_target_pairs={{0,12},{1,13},{2,14},{3,15},{4,0},{5,1},{6,2},{7,3},{8,4},{9,5},{1... | collective-permute-start | bytes 196616 | tf_op jit(solution)/shard_map/ppermute | solution.py:203
  76.8 4.7 %collective-permute-start.3 = (bf16[256,128]{1,0:T(8,128)(2,1)S(1)}, bf16[256,128]{1,0:T(8,128)(2,1)S(1)}, u32[]{:S(2)}, u32[]{:S(2)}) collective-permute-start(bf16[256,128]{1,0:T(8,128)(2,1)S(1)} %get-tuple-element.14.refs_0_), channel_id=1, source_target_pairs={{0,2},{1,3},{2,4},{3,5},{4,6},{5,7},{6,8},{7,9},{8,10},{9,11},{10,... | collective-permute-start | bytes 196616 | tf_op jit(solution)/shard_map/ppermute | solution.py:203
  77.0 4.6 %collective-permute-start.4 = (bf16[256,128]{1,0:T(8,128)(2,1)S(1)}, bf16[256,128]{1,0:T(8,128)(2,1)S(1)}, u32[]{:S(2)}, u32[]{:S(2)}) collective-permute-start(bf16[256,128]{1,0:T(8,128)(2,1)S(1)} %get-tuple-element.14.refs_0_), channel_id=1, source_target_pairs={{0,14},{1,15},{2,0},{3,1},{4,2},{5,3},{6,4},{7,5},{8,6},{9,7},{10,... | collective-permute-start | bytes 196616 | tf_op jit(solution)/shard_map/ppermute | solution.py:203
  82.9 21.6 %all-to-all-start.3 = ((bf16[16,64,128]{2,1,0:T(8,128)(2,1)}), bf16[16,64,128]{2,1,0:T(8,128)(2,1)S(1)}, u32[]{:S(2)}, u32[]{:S(2)}) async-start(bf16[16,64,128]{2,1,0:T(8,128)(2,1)} %shard_map.107), calls=%async_computation.3 | async-start | bytes 524288 | tf_op jit(solution)/shard_map/all_to_all | solution.py:195
  86.6 11.8 %collective-permute-start.5 = (bf16[256,128]{1,0:T(8,128)(2,1)S(1)}, bf16[256,128]{1,0:T(8,128)(2,1)S(1)}, u32[]{:S(2)}, u32[]{:S(2)}) collective-permute-start(bf16[256,128]{1,0:T(8,128)(2,1)S(1)} %get-tuple-element.16), channel_id=1, source_target_pairs={{0,8},{1,9},{2,10},{3,11},{4,12},{5,13},{6,14},{7,15},{8,0},{9,1},... | collective-permute-start | bytes 196616 | tf_op jit(solution)/shard_map/ppermute | solution.py:203
  91.9 12.5 %collective-permute-start.6 = (bf16[256,128]{1,0:T(8,128)(2,1)S(1)}, bf16[256,128]{1,0:T(8,128)(2,1)S(1)}, u32[]{:S(2)}, u32[]{:S(2)}) collective-permute-start(bf16[256,128]{1,0:T(8,128)(2,1)S(1)} %get-tuple-element.16), channel_id=1, source_target_pairs={{0,6},{1,7},{2,8},{3,9},{4,10},{5,11},{6,12},{7,13},{8,14},{9,15},... | collective-permute-start | bytes 196616 | tf_op jit(solution)/shard_map/ppermute | solution.py:203
  92.2 12.2 %collective-permute-start.7 = (bf16[256,128]{1,0:T(8,128)(2,1)S(1)}, bf16[256,128]{1,0:T(8,128)(2,1)S(1)}, u32[]{:S(2)}, u32[]{:S(2)}) collective-permute-start(bf16[256,128]{1,0:T(8,128)(2,1)S(1)} %get-tuple-element.16), channel_id=1, source_target_pairs={{0,10},{1,11},{2,12},{3,13},{4,14},{5,15},{6,0},{7,1},{8,2},{9,3},... | collective-permute-start | bytes 196616 | tf_op jit(solution)/shard_map/ppermute | solution.py:203
  96.4 13.2 %collective-permute-start.8 = (bf16[5,256,128]{2,1,0:T(8,128)(2,1)S(1)}, bf16[5,256,128]{2,1,0:T(8,128)(2,1)}, u32[]{:S(2)}, u32[]{:S(2)}) collective-permute-start(bf16[5,256,128]{2,1,0:T(8,128)(2,1)S(1)} %get-tuple-element.15.after_ref.near_ref), channel_id=1, source_target_pairs={{0,1},{1,0},{2,3},{3,2},{4,5},{5,4},{6,7},{7,6},{8,9},{9,8},{10,11... | collective-permute-start | bytes 983048 | tf_op jit(solution)/shard_map/ppermute | solution.py:249
  104.4 5.2 %collective-permute-start.9 = (bf16[3,256,128]{2,1,0:T(8,128)(2,1)S(1)}, bf16[3,256,128]{2,1,0:T(8,128)(2,1)}, u32[]{:S(2)}, u32[]{:S(2)}) collective-permute-start(bf16[3,256,128]{2,1,0:T(8,128)(2,1)S(1)} %pad_maximum_fusion.far_ref), channel_id=1, source_target_pairs={{0,1},{1,0},{2,3},{3,2},{4,5},{5,4},{6,7},{7,6},{8,9},{9,8},{10,11... | collective-permute-start | bytes 589832 | tf_op jit(solution)/shard_map/ppermute | solution.py:250
  112.1 3.7 %collective-permute-start.10 = (bf16[8,256,128]{2,1,0:T(8,128)(2,1)S(1)}, bf16[8,256,128]{2,1,0:T(8,128)(2,1)S(1)}, u32[]{:S(2)}, u32[]{:S(2)}) collective-permute-start(bf16[8,256,128]{2,1,0:T(8,128)(2,1)S(1)} %get-tuple-element.19), channel_id=1, source_target_pairs={{0,16},{16,0},{32,48},{48,32},{64,80},{80,64},{96,112},{112,96},{1... | collective-permute-start | bytes 1572872 | tf_op jit(solution)/shard_map/ppermute | solution.py:267
  114.3 1.5 %collective-permute-start.11 = (bf16[32,128]{1,0:T(8,128)(2,1)S(1)}, bf16[32,128]{1,0:T(8,128)(2,1)S(1)}, u32[]{:S(2)}, u32[]{:S(2)}) collective-permute-start(bf16[32,128]{1,0:T(8,128)(2,1)S(1)} %shard_map.108.after_ref.piece_ref), channel_id=1, source_target_pairs={{0,16},{16,0},{32,48},{48,32},{64,80},{80,64},{96,112},{112,96},{1... | collective-permute-start | bytes 24584 | tf_op jit(solution)/shard_map/ppermute | solution.py:256
  116.5 17.3 %copy-start.5 = (bf16[256,256]{1,0:T(8,128)(2,1)S(1)}, bf16[256,256]{1,0:T(8,128)(2,1)}, u32[]{:S(2)}) copy-start(bf16[256,256]{1,0:T(8,128)(2,1)} %copy-done.4) | copy-start | bytes 393220

commit v4 on v3

--- a/solution.py
+++ b/solution.py
@@ -18,10 +18,13 @@
 Z = 8
 NEAR = (0, 2, 6, 1, 7)
 FAR = (4, 3, 5)
+EVEN = (0, 4, 2, 6)
+ODD = (1, 5, 7, 3)
 f32 = jnp.float32
 bf16 = jnp.bfloat16
 
 VMEM = pl.BlockSpec(memory_space=pltpu.VMEM)
+ANY = pl.BlockSpec(memory_space=pl.ANY)
 SMEM = pl.BlockSpec(memory_space=pltpu.SMEM)
 PARAMS = pltpu.CompilerParams(vmem_limit_bytes=24 * 1024 * 1024)
 
@@ -56,15 +59,25 @@
     slots_loop(count_ref, rows_ref, acc_ref, lambda k: dot(ones, adj_ref[k], ((1,), (1,))))
     for d in range(N_AX):
         parts = [acc_ref[d * BPD + b][0:1] for b in range(BPD)]
-        both = jnp.concatenate(parts + parts + [jnp.zeros((TAIL - 2 * BPD, BLK), f32)], axis=0)
-        high = both.astype(bf16)
-        low = (both - high.astype(f32)).astype(bf16)
-        at = lax.broadcasted_iota(jnp.int32, (TAIL, BLK), 0)
-        out_ref[d] = jnp.where(at < BPD, high.astype(f32), low.astype(f32)).astype(bf16)
-
-
-def forward_kernel(place_ref, count_ref, rows_ref, cols_ref, adj_ref, mine_ref, other_ref, deg_ref, out_ref, x_ref, acc_ref):
-    core = place_ref[0]
+        out_ref[d] = jnp.concatenate(parts + [jnp.zeros((8 - BPD, BLK), f32)], axis=0)
+
+
+def tail_of(degree):
+    low = degree - degree.astype(bf16).astype(f32)
+    parts = [degree[:BPD], low[:BPD], jnp.zeros((TAIL - 2 * BPD, BLK), f32)]
+    return jnp.concatenate(parts, axis=0).astype(bf16)
+
+
+def degree_of(tail):
+    tail = tail.astype(f32)
+    return jnp.concatenate([tail[:BPD] + tail[BPD : 2 * BPD], jnp.zeros((8 - BPD, BLK), f32)], axis=0)
+
+
+def forward_kernel(
+    place_ref, count_ref, rows_ref, cols_ref, adj_ref, mine_ref, other_ref, deg_ref,
+    near_ref, far_ref, near_deg_ref, far_deg_ref, near_send_ref, far_send_ref, x_ref, acc_ref,
+):
+    core, z, yl = place_ref[0], place_ref[1], place_ref[2]
     for p in range(HALF):
         x_ref[2 * p + core] = mine_ref[p]
         x_ref[2 * p + 1 - core] = other_ref[p]
@@ -75,10 +88,35 @@
         return dot(adj_ref[k], x_ref[col // BPD, pl.ds(at, BLK), :])
 
     slots_loop(count_ref, rows_ref, acc_ref, product)
-    for d in range(N_AX):
-        for b in range(BPD):
-            out_ref[d, b * BLK : (b + 1) * BLK, :] = acc_ref[d * BPD + b].astype(bf16)
-        out_ref[d, BPD * BLK :, :] = deg_ref[d]
+    n = BPD * BLK
+    for keep, degree, send, shifts in (
+        (far_ref, far_deg_ref, far_send_ref, FAR),
+        (near_ref, near_deg_ref, near_send_ref, NEAR),
+    ):
+        for j, s in enumerate(shifts):
+            at = 2 * ((z + s) % Z)
+            here, there = at + yl, at + 1 - yl
+            for b in range(BPD):
+                keep[j, b * BLK : (b + 1) * BLK, :] = acc_ref[here * BPD + b]
+                send[j, b * BLK : (b + 1) * BLK, :] = acc_ref[there * BPD + b].astype(bf16)
+            degree[j] = deg_ref[here]
+            send[j, n:, :] = tail_of(deg_ref[there])
+
+
+def gate_kernel(x_ref, after_ref, out_ref):
+    pass
+
+
+def pair_kernel(keep_ref, deg_ref, got_ref, *out_refs):
+    n = BPD * BLK
+    first = len(out_refs) - keep_ref.shape[0]
+    if first:
+        own_ref, own_deg_ref, *out_refs = out_refs
+        own_ref[...] = keep_ref[0] + got_ref[0, :n, :].astype(f32)
+        own_deg_ref[...] = deg_ref[0] + degree_of(got_ref[0, n:, :])
+    for j, out_ref in enumerate(out_refs, first):
+        out_ref[:n, :] = (keep_ref[j] + got_ref[j, :n, :].astype(f32)).astype(bf16)
+        out_ref[n:, :] = tail_of(deg_ref[j] + degree_of(got_ref[j, n:, :]))
 
 
 def narrow(parts):
@@ -88,17 +126,19 @@
     return total[:PIECE] + total[PIECE:]
 
 
-def dense_kernel(got_ref, x_ref, cot_ref, ws_ref, wn_ref, back_ref, grads_ref, dz_ref):
-    total = got_ref[0].astype(f32)
-    for d in range(1, N_AX):
-        total += got_ref[d].astype(f32)
-    n = BPD * BLK
-    degree = total[n : n + BPD] + total[n + BPD : n + 2 * BPD]
+def dense_kernel(own_ref, own_deg_ref, *refs):
+    *got_refs, x_ref, cot_ref, ws_ref, wn_ref, back_ref, grads_ref, dz_ref = refs
+    n = BPD * BLK
+    total = own_ref[...]
+    degree = own_deg_ref[...]
+    for got_ref in got_refs:
+        total += got_ref[:n, :].astype(f32)
+        degree += degree_of(got_ref[n:, :])
     norm_lanes = lax.rsqrt(1.0 + degree)
     norm = jnp.concatenate(
         [jnp.transpose(jnp.broadcast_to(norm_lanes[b : b + 1], (BLK, BLK))) for b in range(BPD)], axis=0
     )
-    agg = (total[:n] * norm).astype(bf16)
+    agg = (total * norm).astype(bf16)
     x = x_ref[...]
     pre = dot(x, ws_ref[...]) + dot(agg, wn_ref[...])
     sig = jax.nn.sigmoid(pre)
@@ -114,13 +154,12 @@
 
 
 def stack_kernel(*refs):
-    *parts, out_ref, again_ref = refs
-    for j in range(out_ref.shape[0]):
-        out_ref[j] = parts[j][...]
-    again_ref[...] = parts[0][...]
-
-
-def spread_kernel(got_ref, after_ref, out_ref):
+    *parts, out_ref = refs
+    for j, part in enumerate(parts):
+        out_ref[j] = part[...]
+
+
+def spread_kernel(got_ref, after_ref, after2_ref, out_ref):
     total = wide(narrow(got_ref))
     for d in range(N_AX):
         out_ref[d] = total
@@ -131,10 +170,10 @@
 
 
 def adjoint_kernel(
-    place_ref, count_ref, rows_ref, cols_ref, adj_ref, near_ref, far_ref, near2_ref, far2_ref, after_ref, keep_ref, send_ref, x_ref, acc_ref
+    place_ref, count_ref, rows_ref, cols_ref, adj_ref, even_ref, odd_ref, even2_ref, odd2_ref, after_ref, keep_ref, send_ref, x_ref, acc_ref
 ):
     z, yl = place_ref[1], place_ref[2]
-    for mine, other, shifts in ((near_ref, near2_ref, NEAR), (far_ref, far2_ref, FAR)):
+    for mine, other, shifts in ((even_ref, even2_ref, EVEN), (odd_ref, odd2_ref, ODD)):
         for j, s in enumerate(shifts):
             at = 2 * ((z + Z - s) % Z)
             x_ref[at + yl] = mine[j]
@@ -219,38 +258,71 @@
     mine = exchange(jnp.broadcast_to(features[None], (HALF, n, width)), "row", SAME_CORE)
     degree = call(
         degree_kernel,
-        shape((N_AX, TAIL, BLK), bf16),
+        shape((N_AX, 8, BLK), f32),
         [pltpu.VMEM((STRIPE + 1, 8, BLK), f32)],
         product_flops // 16,
         adj.size * 2,
     )(in_specs=[SMEM, SMEM, VMEM], out_specs=VMEM)(block_count, rows, adj)
     mine, degree = lax.optimization_barrier((mine, degree))
     other = lax.ppermute(mine, "row", SWAP)
-    sums = call(
-        forward_kernel, shape((N_AX, n + TAIL, BLK), bf16), [stripe, sums_acc], product_flops, adj.size * 4
-    )(in_specs=[SMEM] * 4 + [VMEM] * 4, out_specs=VMEM)(
+    near, far = len(NEAR), len(FAR)
+    near_keep, far_keep, near_deg, far_deg, near_send, far_send = call(
+        forward_kernel,
+        (
+            shape((near, n, BLK), f32),
+            shape((far, n, BLK), f32),
+            shape((near, 8, BLK), f32),
+            shape((far, 8, BLK), f32),
+            shape((near, n + TAIL, BLK), bf16),
+            shape((far, n + TAIL, BLK), bf16),
+        ),
+        [stripe, sums_acc],
+        product_flops,
+        adj.size * 4,
+    )(in_specs=[SMEM] * 4 + [VMEM] * 4, out_specs=(VMEM,) * 6)(
         place, block_count, rows, cols, adj, mine, other, degree
     )
-    sums = exchange(sums, "col")
+    far_got = lax.ppermute(far_send, "col", SWAP)
+    near_send = call(gate_kernel, shape(near_send.shape, bf16))(
+        in_specs=[ANY, ANY], out_specs=ANY, input_output_aliases={0: 0}
+    )(near_send, far_got)
+    near_got = lax.ppermute(near_send, "col", SWAP)
+    block = shape((n + TAIL, BLK), bf16)
+    far_out = call(pair_kernel, (block,) * far, (), adj.size, adj.size)(
+        in_specs=[VMEM] * 3, out_specs=(VMEM,) * far
+    )(far_keep, far_deg, far_got)
+    own, own_deg, *near_out = call(
+        pair_kernel, (shape((n, BLK), f32), shape((8, BLK), f32)) + (block,) * (near - 1), (), adj.size, adj.size
+    )(in_specs=[VMEM] * 3, out_specs=(VMEM,) * (near + 1))(near_keep, near_deg, near_got)
+    sums = [z_shift(x, s) for x, s in zip(far_out, FAR)] + [z_shift(x, s) for x, s in zip(near_out, NEAR[1:])]
     back, grads, dz = call(
         dense_kernel,
         (shape((n, BLK), bf16), shape((N_AX, 2 * PIECE, BLK), bf16), shape(cotangent.shape, bf16)),
         (),
         product_flops,
         adj.size,
-    )(in_specs=[VMEM] * 5, out_specs=(VMEM,) * 3)(sums, features, cotangent, w_self, w_neigh)
+    )(in_specs=[VMEM] * (6 + len(sums)), out_specs=(VMEM,) * 3)(own, own_deg, *sums, features, cotangent, w_self, w_neigh)
 
     grads = exchange(grads, "row")
-    near = [back] + [z_shift(back, s) for s in NEAR[1:]]
-    near, back = call(
-        stack_kernel, (shape((len(NEAR), n, BLK), bf16), shape((n, BLK), bf16)), (), adj.size, adj.size
-    )(in_specs=[VMEM] * len(NEAR), out_specs=(VMEM, VMEM))(*near)
-    far = jnp.stack([z_shift(back, s) for s in FAR])
-    near2 = lax.ppermute(near, "col", SWAP)
-    far2 = lax.ppermute(far, "col", SWAP)
+    opposite = z_shift(back, 4)
+    even = [back, opposite, z_shift(back, 2), z_shift(back, 6)]
+    two = jnp.stack([back, opposite])
+    even = call(stack_kernel, shape((4, n, BLK), bf16), (), adj.size, adj.size)(
+        in_specs=[VMEM] * 4, out_specs=VMEM
+    )(*even)
+    even2 = lax.ppermute(even, "col", SWAP)
+    odd = [z_shift(two, 1), z_shift(two, 7)]
+    odd = call(stack_kernel, shape((2, 2, n, BLK), bf16), (), adj.size, adj.size)(
+        in_specs=[VMEM] * 2, out_specs=VMEM
+    )(*odd).reshape(4, n, BLK)
+    odd_at = odd
+    odd = call(gate_kernel, shape(odd.shape, bf16))(
+        in_specs=[ANY, ANY], out_specs=ANY, input_output_aliases={0: 0}
+    )(odd, even2)
+    odd2 = lax.ppermute(odd, "col", SWAP)
     grads = call(spread_kernel, shape(grads.shape, bf16), (), adj.size, adj.size)(
-        in_specs=[VMEM, pl.BlockSpec(memory_space=pl.ANY)], out_specs=VMEM
-    )(grads, near)
+        in_specs=[VMEM, ANY, ANY], out_specs=VMEM
+    )(grads, even, odd_at)
     grads = exchange(grads, "col")
     piece = call(piece_kernel, shape((PIECE, BLK), bf16), (), adj.size, adj.size)(in_specs=[VMEM], out_specs=VMEM)(grads)
     piece2 = lax.ppermute(piece, "row", SWAP)
@@ -261,8 +333,8 @@
         [stripe, sums_acc],
         product_flops,
         adj.size * 4,
-    )(in_specs=[SMEM] * 4 + [VMEM] * 5 + [pl.BlockSpec(memory_space=pl.ANY)], out_specs=(VMEM,) * 2)(
-        place, block_count, rows, cols, adj, near, far, near2, far2, piece
+    )(in_specs=[SMEM] * 4 + [VMEM] * 5 + [ANY], out_specs=(VMEM,) * 2)(
+        place, block_count, rows, cols, adj, even, odd, even2, odd2, piece
     )
     send = lax.ppermute(send, "row", SWAP)
     merged = call(

time: 136 us -> 122 us (0.90)
  blocking collectives: 55.2 us -> 18.3 us
  starting transfers between devices: 39.8 us -> 56.3 us
  waiting for transfers between devices: 23.4 us -> 28 us
  Pallas kernels: 10.5 us -> 11.9 us
    all_to_all x2 -> x1, blocking collectives: 55.2 us -> 18.3 us  [exchange(): return lax.all_to_all(x, axis, 0, 0, axis_index_groups=groups)]
    ppermute x7 -> x12, starting transfers between devices: 16 us -> 26 us  [z_shift(): lax.ppermute(x, 'col', [(i, (i + 2 * s) % N_AX) for i in range(N_AX)])]
    all_to_all x3, waiting for transfers between devices: 6.37 us -> 13.6 us  [exchange(): return lax.all_to_all(x, axis, 0, 0, axis_index_groups=groups)]
    ppermute x2 -> x4, starting transfers between devices: 1.28 us -> 4.71 us  [the longest x1 1.66 us: local(): far_got = lax.ppermute(far_send, 'col', SWAP)]
    ppermute x7 -> x12, waiting for transfers between devices: 8.98 us -> 6.31 us  [z_shift(): lax.ppermute(x, 'col', [(i, (i + 2 * s) % N_AX) for i in range(N_AX)])]
    ppermute x1, starting transfers between devices: 2.19 us -> 3.76 us  [local(): send = lax.ppermute(send, 'row', SWAP)]
    all_to_all x3, starting transfers between devices: 18.6 us -> 20.1 us  [exchange(): return lax.all_to_all(x, axis, 0, 0, axis_index_groups=groups)]
    unnamed x20 -> x22, local copies, waits for them, and re-layouts: 2.43 us -> 3.14 us
  transfers between devices with their start and end apart: 15 -> 22, of which waited for: 10 -> 10; matrix products, arithmetic and copies ran while one was open for 0% -> 0% of each run, Pallas kernels for 1% -> 3%
where the time goes in v4:
time: 122 us; the launch traced here: 121 us
  starting transfers between devices  56.3 us (46%)
  waiting for transfers between devices  28 us (23%)
  blocking collectives  18.3 us (15%)
  Pallas kernels  11.9 us (10%)
  local copies, waits for them, and re-layouts  4.86 us (4%)
  between operations  1.49 us (1%)
    ppermute x12, starting transfers between devices, z_shift(): lax.ppermute(x, 'col', [(i, (i + 2 * s) % N_AX) for i in range(N_AX)])  26 us
    all_to_all x3, starting transfers between devices, exchange(): return lax.all_to_all(x, axis, 0, 0, axis_index_groups=groups)  20.1 us
    all_to_all x1, blocking collectives, exchange(): return lax.all_to_all(x, axis, 0, 0, axis_index_groups=groups)  18.3 us
    all_to_all x3, waiting for transfers between devices, exchange(): return lax.all_to_all(x, axis, 0, 0, axis_index_groups=groups)  13.6 us
    ppermute x12, waiting for transfers between devices, z_shift(): lax.ppermute(x, 'col', [(i, (i + 2 * s) % N_AX) for i in range(N_AX)])  6.31 us
    ppermute x1, waiting for transfers between devices, local(): far_got = lax.ppermute(far_send, 'col', SWAP)  5.03 us
    ppermute x1, starting transfers between devices, local(): send = lax.ppermute(send, 'row', SWAP)  3.76 us
    unnamed x22, local copies, waits for them, and re-layouts  3.14 us
  transfers between devices with their start and end apart: 22, of which 10 were waited for; matrix products, arithmetic and copies ran while one was open for 0% of the time, Pallas kernels for 3%

profile of v4, /device:TPU:1, one launch (start us, length us, event | category | flops | bytes accessed | tf_op | source)
XLA Modules:
  0.0 120.9 jit_solution(16302189103277947274)
XLA Ops:
  0.6 0.0 copy-start.7
  0.7 1.7 %broadcast_in_dim.2 = bf16[8,256,128]{2,1,0:T(8,128)(2,1)} broadcast(bf16[256,128]{1,0:T(8,128)(2,1)} %refs_7_.1), dimensions={1,2} | broadcast | bytes 589824 | tf_op jit(solution)/shard_map/broadcast_in_dim | solution.py:258
  2.4 7.5 %all-to-all-start = ((bf16[8,256,128]{2,1,0:T(8,128)(2,1)}), bf16[8,256,128]{2,1,0:T(8,128)(2,1)S(1)}, u32[]{:S(2)}, u32[]{:S(2)}) async-start(bf16[8,256,128]{2,1,0:T(8,128)(2,1)} %broadcast_in_dim.2), calls=%async_computation | async-start | bytes 1048576 | tf_op jit(solution)/shard_map/all_to_all | solution.py:234
  10.5 0.0 copy-start
  10.5 1.7 %copy-done = bf16[1,1,80,128,128]{4,3,2,1,0:T(8,128)(2,1)S(1)} copy-done((bf16[1,1,80,128,128]{4,3,2,1,0:T(8,128)(2,1)S(1)}, bf16[1,1,80,128,128]{4,3,2,1,0:T(8,128)(2,1)}, u32[]{:S(2)}) %copy-start) | copy-done | bytes 2621464
  12.2 0.7 copy-done.6
  12.9 1.8 %shard_map.103.deg_ref = f32[16,8,128]{2,1,0:T(8,128)S(1)} custom-call(s32[1,1]{1,0:T(1,128)S(6)} %copy.15.count_ref, s32[1,80]{1,0:T(1,128)S(1)} %bitcast.16, bf16[80,128,128]{2,1,0:T(8,128)(2,1)S(1)} %bitcast.9), custom_call_target="tpu_custom_call" | custom-call | flops 20971520 | bytes 2621440 | tf_op jit(solution)/shard_map/pallas_call | solution.py:259
  14.7 5.3 %all-to-all-done.mine_ref = bf16[8,256,128]{2,1,0:T(8,128)(2,1)S(1)} async-done(((bf16[8,256,128]{2,1,0:T(8,128)(2,1)}), bf16[8,256,128]{2,1,0:T(8,128)(2,1)S(1)}, u32[]{:S(2)}, u32[]{:S(2)}) %all-to-all-start) | async-done | bytes 524320 | tf_op jit(solution)/shard_map/all_to_all | solution.py:234
  20.1 1.6 %collective-permute-start = (bf16[8,256,128]{2,1,0:T(8,128)(2,1)S(1)}, bf16[8,256,128]{2,1,0:T(8,128)(2,1)}, u32[]{:S(2)}, u32[]{:S(2)}) collective-permute-start(bf16[8,256,128]{2,1,0:T(8,128)(2,1)S(1)} %all-to-all-done.mine_ref), channel_id=1, source_target_pairs={{0,16},{16,0},{32,48},{48,32},{64,80},{80,64},{96,112},{112,96},{1... | collective-permute-start | bytes 1572872 | tf_op jit(solution)/shard_map/ppermute | solution.py:267
  21.7 0.1 pad_add_fusion.place_ref
  21.8 1.6 %collective-permute-done.other_ref = bf16[8,256,128]{2,1,0:T(8,128)(2,1)} collective-permute-done((bf16[8,256,128]{2,1,0:T(8,128)(2,1)S(1)}, bf16[8,256,128]{2,1,0:T(8,128)(2,1)}, u32[]{:S(2)}, u32[]{:S(2)}) %collective-permute-start) | collective-permute-done | bytes 524320 | tf_op jit(solution)/shard_map/ppermute | solution.py:267
  23.4 0.0 copy-start.4
  23.4 0.0 copy-start.9
  23.4 0.0 copy-start.10
  23.4 2.7 %shard_map.104 = (f32[5,256,128]{2,1,0:T(8,128)S(1)}, f32[3,256,128]{2,1,0:T(8,128)S(1)}, f32[5,8,128]{2,1,0:T(8,128)S(1)}, f32[3,8,128]{2,1,0:T(8,128)S(1)}, bf...) custom-call(s32[3]{0:T(128)S(1)} %pad_add_fusion.place_ref, s32[1,1]{1,0:T(1,128)S(6)} %copy.15.count_ref, ...), custom_call_target="tpu_custom_call" | custom-call | flops 335544320 | bytes 5242880 | tf_op jit(solution)/shard_map/pallas_call | solution.py:269
  26.1 1.7 %collective-permute-start.1 = (bf16[3,272,128]{2,1,0:T(8,128)(2,1)S(1)}, bf16[3,272,128]{2,1,0:T(8,128)(2,1)S(1)}, u32[]{:S(2)}, u32[]{:S(2)}) collective-permute-start(bf16[3,272,128]{2,1,0:T(8,128)(2,1)S(1)} %get-tuple-element.30), channel_id=1, source_target_pairs={{0,1},{1,0},{2,3},{3,2},{4,5},{5,4},{6,7},{7,6},{8,9},{9,8},{10,11... | collective-permute-start | bytes 626696 | tf_op jit(solution)/shard_map/ppermute | solution.py:285
  27.7 5.0 %collective-permute-done.1.after_ref.got_ref = bf16[3,272,128]{2,1,0:T(8,128)(2,1)S(1)} collective-permute-done((bf16[3,272,128]{2,1,0:T(8,128)(2,1)S(1)}, bf16[3,272,128]{2,1,0:T(8,128)(2,1)S(1)}, u32[]{:S(2)}, u32[]{:S(2)}) %collective-permute-start.1) | collective-permute-done | bytes 208928 | tf_op jit(solution)/shard_map/ppermute | solution.py:285
  32.8 1.5 %collective-permute-start.2 = (bf16[5,272,128]{2,1,0:T(8,128)(2,1)S(1)}, bf16[5,272,128]{2,1,0:T(8,128)(2,1)S(1)}, u32[]{:S(2)}, u32[]{:S(2)}) collective-permute-start(bf16[5,272,128]{2,1,0:T(8,128)(2,1)S(1)} %shard_map.105), channel_id=1, source_target_pairs={{0,1},{1,0},{2,3},{3,2},{4,5},{5,4},{6,7},{7,6},{8,9},{9,8},{10,11... | collective-permute-start | bytes 1044488 | tf_op jit(solution)/shard_map/ppermute | solution.py:289
  34.3 0.1 shard_map.107
  34.4 5.6 %collective-permute-start.3 = (bf16[272,128]{1,0:T(8,128)(2,1)S(1)}, bf16[272,128]{1,0:T(8,128)(2,1)S(1)}, u32[]{:S(2)}, u32[]{:S(2)}) collective-permute-start(bf16[272,128]{1,0:T(8,128)(2,1)S(1)} %get-tuple-element.35), channel_id=1, source_target_pairs={{0,8},{1,9},{2,10},{3,11},{4,12},{5,13},{6,14},{7,15},{8,0},{9,1},... | collective-permute-start | bytes 208904 | tf_op jit(solution)/shard_map/ppermute | solution.py:242
  40.0 1.8 %collective-permute-start.4 = (bf16[272,128]{1,0:T(8,128)(2,1)S(1)}, bf16[272,128]{1,0:T(8,128)(2,1)S(1)}, u32[]{:S(2)}, u32[]{:S(2)}) collective-permute-start(bf16[272,128]{1,0:T(8,128)(2,1)S(1)} %get-tuple-element.36), channel_id=1, source_target_pairs={{0,6},{1,7},{2,8},{3,9},{4,10},{5,11},{6,12},{7,13},{8,14},{9,15},... | collective-permute-start | bytes 208904 | tf_op jit(solution)/shard_map/ppermute | solution.py:242
  41.8 2.7 %collective-permute-start.5 = (bf16[272,128]{1,0:T(8,128)(2,1)S(1)}, bf16[272,128]{1,0:T(8,128)(2,1)S(1)}, u32[]{:S(2)}, u32[]{:S(2)}) collective-permute-start(bf16[272,128]{1,0:T(8,128)(2,1)S(1)} %get-tuple-element.37), channel_id=1, source_target_pairs={{0,10},{1,11},{2,12},{3,13},{4,14},{5,15},{6,0},{7,1},{8,2},{9,3},... | collective-permute-start | bytes 208904 | tf_op jit(solution)/shard_map/ppermute | solution.py:242
  44.5 0.0 collective-permute-done.2.got_ref
  44.5 0.1 shard_map.106
  44.6 2.4 %collective-permute-start.6 = (bf16[272,128]{1,0:T(8,128)(2,1)S(1)}, bf16[272,128]{1,0:T(8,128)(2,1)S(1)}, u32[]{:S(2)}, u32[]{:S(2)}) collective-permute-start(bf16[272,128]{1,0:T(8,128)(2,1)S(1)} %get-tuple-element.38), channel_id=1, source_target_pairs={{0,4},{1,5},{2,6},{3,7},{4,8},{5,9},{6,10},{7,11},{8,12},{9,13},{1... | collective-permute-start | bytes 208904 | tf_op jit(solution)/shard_map/ppermute | solution.py:242
  46.9 1.5 %collective-permute-start.7 = (bf16[272,128]{1,0:T(8,128)(2,1)S(1)}, bf16[272,128]{1,0:T(8,128)(2,1)S(1)}, u32[]{:S(2)}, u32[]{:S(2)}) collective-permute-start(bf16[272,128]{1,0:T(8,128)(2,1)S(1)} %get-tuple-element.39), channel_id=1, source_target_pairs={{0,12},{1,13},{2,14},{3,15},{4,0},{5,1},{6,2},{7,3},{8,4},{9,5},{1... | collective-permute-start | bytes 208904 | tf_op jit(solution)/shard_map/ppermute | solution.py:242
  48.4 0.0 collective-permute-done.3.refs_0_
  48.4 0.6 collective-permute-start.8
  49.1 0.4 collective-permute-done.4.refs_1_
  49.5 1.6 %collective-permute-start.9 = (bf16[272,128]{1,0:T(8,128)(2,1)S(1)}, bf16[272,128]{1,0:T(8,128)(2,1)S(1)}, u32[]{:S(2)}, u32[]{:S(2)}) collective-permute-start(bf16[272,128]{1,0:T(8,128)(2,1)S(1)} %get-tuple-element.41), channel_id=1, source_target_pairs={{0,14},{1,15},{2,0},{3,1},{4,2},{5,3},{6,4},{7,5},{8,6},{9,7},{10,... | collective-permute-start | bytes 208904 | tf_op jit(solution)/shard_map/ppermute | solution.py:242
  51.1 0.0 collective-permute-done.5.refs_2_
  51.1 0.0 collective-permute-done.6.refs_3_
  51.1 1.2 %collective-permute-done.7.refs_4_ = bf16[272,128]{1,0:T(8,128)(2,1)S(1)} collective-permute-done((bf16[272,128]{1,0:T(8,128)(2,1)S(1)}, bf16[272,128]{1,0:T(8,128)(2,1)S(1)}, u32[]{:S(2)}, u32[]{:S(2)}) %collective-permute-start.7) | collective-permute-done | bytes 69664 | tf_op jit(solution)/shard_map/ppermute | solution.py:242
  52.3 1.3 %collective-permute-done.8.refs_5_ = bf16[272,128]{1,0:T(8,128)(2,1)S(1)} collective-permute-done((bf16[272,128]{1,0:T(8,128)(2,1)S(1)}, bf16[272,128]{1,0:T(8,128)(2,1)S(1)}, u32[]{:S(2)}, u32[]{:S(2)}) %collective-permute-start.8) | collective-permute-done | bytes 69664 | tf_op jit(solution)/shard_map/ppermute | solution.py:242
  53.6 0.2 collective-permute-done.9.refs_6_
  53.8 1.3 %shard_map.108 = (bf16[256,128]{1,0:T(8,128)(2,1)S(1)}, bf16[16,64,128]{2,1,0:T(8,128)(2,1)}, bf16[256,256]{1,0:T(8,128)(2,1)S(1)}) custom-call(f32[256,128]{1,0:T(8,128)S(1)} %get-tuple-element.31.own_ref, f32[8,128]{1,0:T(8,128)S(1)} %get-tuple-element.32.own_deg_ref, bf16[272,128]{1,0:T(8,128)(2,1)S(1)} %collective-permute-done.3.refs_0_, ...), custom_call_target="tpu_custom_call" | custom-call | flops 335544320 | bytes 1310720 | tf_op jit(solution)/shard_map/pallas_call | solution.py:298
  55.1 3.1 %collective-permute-start.10 = (bf16[256,128]{1,0:T(8,128)(2,1)S(1)}, bf16[256,128]{1,0:T(8,128)(2,1)S(1)}, u32[]{:S(2)}, u32[]{:S(2)}) collective-permute-start(bf16[256,128]{1,0:T(8,128)(2,1)S(1)} %get-tuple-element.42.refs_0_), channel_id=1, source_target_pairs={{0,8},{1,9},{2,10},{3,11},{4,12},{5,13},{6,14},{7,15},{8,0},{9,1},... | collective-permute-start | bytes 196616 | tf_op jit(solution)/shard_map/ppermute | solution.py:242
  58.2 7.5 %all-to-all-start.1 = ((bf16[16,64,128]{2,1,0:T(8,128)(2,1)}), bf16[16,64,128]{2,1,0:T(8,128)(2,1)}, u32[]{:S(2)}, u32[]{:S(2)}) async-start(bf16[16,64,128]{2,1,0:T(8,128)(2,1)} %get-tuple-element.43), calls=%async_computation.1 | async-start | bytes 524288 | tf_op jit(solution)/shard_map/all_to_all | solution.py:234
  65.7 0.0 collective-permute-done.10.refs_1_
  65.7 0.4 collective-permute-start.13
  66.1 2.8 %collective-permute-start.14 = (bf16[2,256,128]{2,1,0:T(8,128)(2,1)S(1)}, bf16[2,256,128]{2,1,0:T(8,128)(2,1)S(1)}, u32[]{:S(2)}, u32[]{:S(2)}) collective-permute-start(bf16[2,256,128]{2,1,0:T(8,128)(2,1)S(1)} %pad_maximum_fusion), channel_id=1, source_target_pairs={{0,14},{1,15},{2,0},{3,1},{4,2},{5,3},{6,4},{7,5},{8,6},{9,7},{10,... | collective-permute-start | bytes 393224 | tf_op jit(solution)/shard_map/ppermute | solution.py:242
  68.8 0.0 collective-permute-start.11
  68.8 3.6 %collective-permute-start.12 = (bf16[256,128]{1,0:T(8,128)(2,1)S(1)}, bf16[256,128]{1,0:T(8,128)(2,1)S(1)}, u32[]{:S(2)}, u32[]{:S(2)}) collective-permute-start(bf16[256,128]{1,0:T(8,128)(2,1)S(1)} %get-tuple-element.42.refs_0_), channel_id=1, source_target_pairs={{0,12},{1,13},{2,14},{3,15},{4,0},{5,1},{6,2},{7,3},{8,4},{9,5},{1... | collective-permute-start | bytes 196616 | tf_op jit(solution)/shard_map/ppermute | solution.py:242
  72.4 3.2 %collective-permute-done.11.refs_2_ = bf16[256,128]{1,0:T(8,128)(2,1)S(1)} collective-permute-done((bf16[256,128]{1,0:T(8,128)(2,1)S(1)}, bf16[256,128]{1,0:T(8,128)(2,1)S(1)}, u32[]{:S(2)}, u32[]{:S(2)}) %collective-permute-start.11) | collective-permute-done | bytes 65568 | tf_op jit(solution)/shard_map/ppermute | solution.py:242
  75.6 0.1 collective-permute-start.15
  75.7 0.0 collective-permute-done.13.refs_0_
  75.7 0.0 collective-permute-done.14.refs_1_
  75.8 0.0 all-to-all-done.1.got_ref
  75.8 1.0 shard_map.112
  76.8 0.7 copy-done.2
  77.5 5.1 %all-to-all-start.2 = ((bf16[16,64,128]{2,1,0:T(8,128)(2,1)}), bf16[16,64,128]{2,1,0:T(8,128)(2,1)}, u32[]{:S(2)}, u32[]{:S(2)}) async-start(bf16[16,64,128]{2,1,0:T(8,128)(2,1)} %copy-done.2), calls=%async_computation.2 | async-start | bytes 524288 | tf_op jit(solution)/shard_map/all_to_all | solution.py:234
  82.6 0.0 collective-permute-done.15.after_ref.even2_ref
  82.7 1.4 %collective-permute-start.16 = (bf16[4,256,128]{2,1,0:T(8,128)(2,1)S(1)}, bf16[4,256,128]{2,1,0:T(8,128)(2,1)}, u32[]{:S(2)}, u32[]{:S(2)}) collective-permute-start(bf16[4,256,128]{2,1,0:T(8,128)(2,1)S(1)} %shard_map.111.odd_ref), channel_id=1, source_target_pairs={{0,1},{1,0},{2,3},{3,2},{4,5},{5,4},{6,7},{7,6},{8,9},{9,8},{10,11... | collective-permute-start | bytes 786440 | tf_op jit(solution)/shard_map/ppermute | solution.py:322
  84.1 8.3 %all-to-all-done.2.got_ref = bf16[16,64,128]{2,1,0:T(8,128)(2,1)} async-done(((bf16[16,64,128]{2,1,0:T(8,128)(2,1)}), bf16[16,64,128]{2,1,0:T(8,128)(2,1)}, u32[]{:S(2)}, u32[]{:S(2)}) %all-to-all-start.2) | async-done | bytes 262176 | tf_op jit(solution)/shard_map/all_to_all | solution.py:234
  92.3 1.0 shard_map.113.after_ref.piece_ref
  93.3 2.5 %shard_map.114 = (f32[8,256,128]{2,1,0:T(8,128)S(1)}, bf16[8,256,128]{2,1,0:T(8,128)(2,1)S(1)}) custom-call(s32[3]{0:T(128)S(1)} %pad_add_fusion.place_ref, s32[1,1]{1,0:T(1,128)S(6)} %copy.15.count_ref, s32[1,80]{1,0:T(1,128)S(1)} %bitcast.18, s32[1,80]{1,0:T(1,128)S(1)} %bitcast.20, bf16[80,128,128]{2,1,0:T(8,128)(2,1)S(1)} %bitcast.11, ...), custom_call_target="tpu_custom_call" | custom-call | flops 335544320 | bytes 5242880 | tf_op jit(solution)/shard_map/pallas_call | solution.py:330
  95.8 0.0 copy-start.5
  95.8 3.8 %collective-permute-start.17 = (bf16[8,256,128]{2,1,0:T(8,128)(2,1)S(1)}, bf16[8,256,128]{2,1,0:T(8,128)(2,1)S(1)}, u32[]{:S(2)}, u32[]{:S(2)}) collective-permute-start(bf16[8,256,128]{2,1,0:T(8,128)(2,1)S(1)} %get-tuple-element.45), channel_id=1, source_target_pairs={{0,16},{16,0},{32,48},{48,32},{64,80},{80,64},{96,112},{112,96},{1... | collective-permute-start | bytes 1572872 | tf_op jit(solution)/shard_map/ppermute | solution.py:339
  99.6 0.1 collective-permute-start.18
  99.7 1.4 %collective-permute-done.18.piece2_ref = bf16[32,128]{1,0:T(8,128)(2,1)S(1)} collective-permute-done((bf16[32,128]{1,0:T(8,128)(2,1)S(1)}, bf16[32,128]{1,0:T(8,128)(2,1)S(1)}, u32[]{:S(2)}, u32[]{:S(2)}) %collective-permute-start.18) | collective-permute-done | bytes 8224 | tf_op jit(solution)/shard_map/ppermute | solution.py:328
  101.1 0.0 collective-permute-done.17.got_ref
  101.1 0.6 shard_map.115
  101.8 18.3 %all_to_all.20.got_ref = bf16[8,320,128]{2,1,0:T(8,128)(2,1)S(1)} all-to-all(bf16[8,320,128]{2,1,0:T(8,128)(2,1)S(1)} %shard_map.115), channel_id=1, replica_groups={{0,32,64,96,128,160,192,224},{16,48,80,112,144,176,208,240},{1,33,65,97..., dimensions={0} | all-to-all | bytes 1310720 | tf_op jit(solution)/shard_map/all_to_all | solution.py:234
  120.1 0.9 shard_map.116
  (20 shorter events, 0.1 us)
Async XLA Ops:
  0.6 22.7 %copy-start.7 = (s32[1,1,80]{2,1,0:T(1,128)S(1)}, s32[1,1,80]{2,1,0:T(1,128)}, u32[]{:S(2)}) copy-start(s32[1,1,80]{2,1,0:T(1,128)} %param.13) | copy-start | bytes 964
  0.6 22.7 %copy-start.8 = (s32[1,1,80]{2,1,0:T(1,128)S(1)}, s32[1,1,80]{2,1,0:T(1,128)}, u32[]{:S(2)}) copy-start(s32[1,1,80]{2,1,0:T(1,128)} %param.14) | copy-start | bytes 964
  2.4 17.7 %all-to-all-start = ((bf16[8,256,128]{2,1,0:T(8,128)(2,1)}), bf16[8,256,128]{2,1,0:T(8,128)(2,1)S(1)}, u32[]{:S(2)}, u32[]{:S(2)}) async-start(bf16[8,256,128]{2,1,0:T(8,128)(2,1)} %broadcast_in_dim.2), calls=%async_computation | async-start | bytes 1048576 | tf_op jit(solution)/shard_map/all_to_all | solution.py:234
  10.5 1.7 %copy-start = (bf16[1,1,80,128,128]{4,3,2,1,0:T(8,128)(2,1)S(1)}, bf16[1,1,80,128,128]{4,3,2,1,0:T(8,128)(2,1)}, u32[]{:S(2)}) copy-start(bf16[1,1,80,128,128]{4,3,2,1,0:T(8,128)(2,1)} %param.12) | copy-start | bytes 7864324
  12.2 0.7 copy-start.6
  12.9 10.5 %copy-start.1 = (bf16[1,1,80,128,128]{4,3,2,1,0:T(8,128)(2,1)S(1)}, bf16[1,1,80,128,128]{4,3,2,1,0:T(8,128)(2,1)}, u32[]{:S(2)}) copy-start(bf16[1,1,80,128,128]{4,3,2,1,0:T(8,128)(2,1)} %param.12) | copy-start | bytes 7864324
  20.1 3.3 %collective-permute-start = (bf16[8,256,128]{2,1,0:T(8,128)(2,1)S(1)}, bf16[8,256,128]{2,1,0:T(8,128)(2,1)}, u32[]{:S(2)}, u32[]{:S(2)}) collective-permute-start(bf16[8,256,128]{2,1,0:T(8,128)(2,1)S(1)} %all-to-all-done.mine_ref), channel_id=1, source_target_pairs={{0,16},{16,0},{32,48},{48,32},{64,80},{80,64},{96,112},{112,96},{1... | collective-permute-start | bytes 1572872 | tf_op jit(solution)/shard_map/ppermute | solution.py:267
  23.4 30.5 %copy-start.3 = (bf16[256,128]{1,0:T(8,128)(2,1)S(1)}, bf16[256,128]{1,0:T(8,128)(2,1)}, u32[]{:S(2)}) copy-start(bf16[256,128]{1,0:T(8,128)(2,1)} %refs_7_.1) | copy-start | bytes 196612
  23.4 30.4 %copy-start.4 = (bf16[128,256]{1,0:T(8,128)(2,1)S(1)}, bf16[128,256]{1,0:T(8,128)(2,1)}, u32[]{:S(2)}) copy-start(bf16[128,256]{1,0:T(8,128)(2,1)} %ws_ref.1) | copy-start | bytes 196612
  23.4 30.4 %copy-start.9 = (bf16[256,256]{1,0:T(8,128)(2,1)S(1)}, bf16[256,256]{1,0:T(8,128)(2,1)}, u32[]{:S(2)}) copy-start(bf16[256,256]{1,0:T(8,128)(2,1)} %refs_8_.1) | copy-start | bytes 393220
  23.4 30.4 %copy-start.10 = (bf16[128,256]{1,0:T(8,128)(2,1)S(1)}, bf16[128,256]{1,0:T(8,128)(2,1)}, u32[]{:S(2)}) copy-start(bf16[128,256]{1,0:T(8,128)(2,1)} %refs_10_.1) | copy-start | bytes 196612
  26.1 6.7 %collective-permute-start.1 = (bf16[3,272,128]{2,1,0:T(8,128)(2,1)S(1)}, bf16[3,272,128]{2,1,0:T(8,128)(2,1)S(1)}, u32[]{:S(2)}, u32[]{:S(2)}) collective-permute-start(bf16[3,272,128]{2,1,0:T(8,128)(2,1)S(1)} %get-tuple-element.30), channel_id=1, source_target_pairs={{0,1},{1,0},{2,3},{3,2},{4,5},{5,4},{6,7},{7,6},{8,9},{9,8},{10,11... | collective-permute-start | bytes 626696 | tf_op jit(solution)/shard_map/ppermute | solution.py:285
  32.8 11.7 %collective-permute-start.2 = (bf16[5,272,128]{2,1,0:T(8,128)(2,1)S(1)}, bf16[5,272,128]{2,1,0:T(8,128)(2,1)S(1)}, u32[]{:S(2)}, u32[]{:S(2)}) collective-permute-start(bf16[5,272,128]{2,1,0:T(8,128)(2,1)S(1)} %shard_map.105), channel_id=1, source_target_pairs={{0,1},{1,0},{2,3},{3,2},{4,5},{5,4},{6,7},{7,6},{8,9},{9,8},{10,11... | collective-permute-start | bytes 1044488 | tf_op jit(solution)/shard_map/ppermute | solution.py:289
  34.4 14.1 %collective-permute-start.3 = (bf16[272,128]{1,0:T(8,128)(2,1)S(1)}, bf16[272,128]{1,0:T(8,128)(2,1)S(1)}, u32[]{:S(2)}, u32[]{:S(2)}) collective-permute-start(bf16[272,128]{1,0:T(8,128)(2,1)S(1)} %get-tuple-element.35), channel_id=1, source_target_pairs={{0,8},{1,9},{2,10},{3,11},{4,12},{5,13},{6,14},{7,15},{8,0},{9,1},... | collective-permute-start | bytes 208904 | tf_op jit(solution)/shard_map/ppermute | solution.py:242
  40.0 9.5 %collective-permute-start.4 = (bf16[272,128]{1,0:T(8,128)(2,1)S(1)}, bf16[272,128]{1,0:T(8,128)(2,1)S(1)}, u32[]{:S(2)}, u32[]{:S(2)}) collective-permute-start(bf16[272,128]{1,0:T(8,128)(2,1)S(1)} %get-tuple-element.36), channel_id=1, source_target_pairs={{0,6},{1,7},{2,8},{3,9},{4,10},{5,11},{6,12},{7,13},{8,14},{9,15},... | collective-permute-start | bytes 208904 | tf_op jit(solution)/shard_map/ppermute | solution.py:242
  41.8 9.4 %collective-permute-start.5 = (bf16[272,128]{1,0:T(8,128)(2,1)S(1)}, bf16[272,128]{1,0:T(8,128)(2,1)S(1)}, u32[]{:S(2)}, u32[]{:S(2)}) collective-permute-start(bf16[272,128]{1,0:T(8,128)(2,1)S(1)} %get-tuple-element.37), channel_id=1, source_target_pairs={{0,10},{1,11},{2,12},{3,13},{4,14},{5,15},{6,0},{7,1},{8,2},{9,3},... | collective-permute-start | bytes 208904 | tf_op jit(solution)/shard_map/ppermute | solution.py:242
  44.6 6.6 %collective-permute-start.6 = (bf16[272,128]{1,0:T(8,128)(2,1)S(1)}, bf16[272,128]{1,0:T(8,128)(2,1)S(1)}, u32[]{:S(2)}, u32[]{:S(2)}) collective-permute-start(bf16[272,128]{1,0:T(8,128)(2,1)S(1)} %get-tuple-element.38), channel_id=1, source_target_pairs={{0,4},{1,5},{2,6},{3,7},{4,8},{5,9},{6,10},{7,11},{8,12},{9,13},{1... | collective-permute-start | bytes 208904 | tf_op jit(solution)/shard_map/ppermute | solution.py:242
  46.9 5.4 %collective-permute-start.7 = (bf16[272,128]{1,0:T(8,128)(2,1)S(1)}, bf16[272,128]{1,0:T(8,128)(2,1)S(1)}, u32[]{:S(2)}, u32[]{:S(2)}) collective-permute-start(bf16[272,128]{1,0:T(8,128)(2,1)S(1)} %get-tuple-element.39), channel_id=1, source_target_pairs={{0,12},{1,13},{2,14},{3,15},{4,0},{5,1},{6,2},{7,3},{8,4},{9,5},{1... | collective-permute-start | bytes 208904 | tf_op jit(solution)/shard_map/ppermute | solution.py:242
  48.4 5.2 %collective-permute-start.8 = (bf16[272,128]{1,0:T(8,128)(2,1)S(1)}, bf16[272,128]{1,0:T(8,128)(2,1)S(1)}, u32[]{:S(2)}, u32[]{:S(2)}) collective-permute-start(bf16[272,128]{1,0:T(8,128)(2,1)S(1)} %get-tuple-element.40), channel_id=1, source_target_pairs={{0,2},{1,3},{2,4},{3,5},{4,6},{5,7},{6,8},{7,9},{8,10},{9,11},{10,... | collective-permute-start | bytes 208904 | tf_op jit(solution)/shard_map/ppermute | solution.py:242
  49.5 4.3 %collective-permute-start.9 = (bf16[272,128]{1,0:T(8,128)(2,1)S(1)}, bf16[272,128]{1,0:T(8,128)(2,1)S(1)}, u32[]{:S(2)}, u32[]{:S(2)}) collective-permute-start(bf16[272,128]{1,0:T(8,128)(2,1)S(1)} %get-tuple-element.41), channel_id=1, source_target_pairs={{0,14},{1,15},{2,0},{3,1},{4,2},{5,3},{6,4},{7,5},{8,6},{9,7},{10,... | collective-permute-start | bytes 208904 | tf_op jit(solution)/shard_map/ppermute | solution.py:242
  55.1 10.6 %collective-permute-start.10 = (bf16[256,128]{1,0:T(8,128)(2,1)S(1)}, bf16[256,128]{1,0:T(8,128)(2,1)S(1)}, u32[]{:S(2)}, u32[]{:S(2)}) collective-permute-start(bf16[256,128]{1,0:T(8,128)(2,1)S(1)} %get-tuple-element.42.refs_0_), channel_id=1, source_target_pairs={{0,8},{1,9},{2,10},{3,11},{4,12},{5,13},{6,14},{7,15},{8,0},{9,1},... | collective-permute-start | bytes 196616 | tf_op jit(solution)/shard_map/ppermute | solution.py:242
  58.2 17.6 %all-to-all-start.1 = ((bf16[16,64,128]{2,1,0:T(8,128)(2,1)}), bf16[16,64,128]{2,1,0:T(8,128)(2,1)}, u32[]{:S(2)}, u32[]{:S(2)}) async-start(bf16[16,64,128]{2,1,0:T(8,128)(2,1)} %get-tuple-element.43), calls=%async_computation.1 | async-start | bytes 524288 | tf_op jit(solution)/shard_map/all_to_all | solution.py:234
  65.7 10.0 %collective-permute-start.13 = (bf16[2,256,128]{2,1,0:T(8,128)(2,1)S(1)}, bf16[2,256,128]{2,1,0:T(8,128)(2,1)S(1)}, u32[]{:S(2)}, u32[]{:S(2)}) collective-permute-start(bf16[2,256,128]{2,1,0:T(8,128)(2,1)S(1)} %pad_maximum_fusion), channel_id=1, source_target_pairs={{0,2},{1,3},{2,4},{3,5},{4,6},{5,7},{6,8},{7,9},{8,10},{9,11},{10,... | collective-permute-start | bytes 393224 | tf_op jit(solution)/shard_map/ppermute | solution.py:242
  66.1 9.7 %collective-permute-start.14 = (bf16[2,256,128]{2,1,0:T(8,128)(2,1)S(1)}, bf16[2,256,128]{2,1,0:T(8,128)(2,1)S(1)}, u32[]{:S(2)}, u32[]{:S(2)}) collective-permute-start(bf16[2,256,128]{2,1,0:T(8,128)(2,1)S(1)} %pad_maximum_fusion), channel_id=1, source_target_pairs={{0,14},{1,15},{2,0},{3,1},{4,2},{5,3},{6,4},{7,5},{8,6},{9,7},{10,... | collective-permute-start | bytes 393224 | tf_op jit(solution)/shard_map/ppermute | solution.py:242
  68.8 6.8 %collective-permute-start.11 = (bf16[256,128]{1,0:T(8,128)(2,1)S(1)}, bf16[256,128]{1,0:T(8,128)(2,1)S(1)}, u32[]{:S(2)}, u32[]{:S(2)}) collective-permute-start(bf16[256,128]{1,0:T(8,128)(2,1)S(1)} %get-tuple-element.42.refs_0_), channel_id=1, source_target_pairs={{0,4},{1,5},{2,6},{3,7},{4,8},{5,9},{6,10},{7,11},{8,12},{9,13},{1... | collective-permute-start | bytes 196616 | tf_op jit(solution)/shard_map/ppermute | solution.py:242
  68.8 6.8 %collective-permute-start.12 = (bf16[256,128]{1,0:T(8,128)(2,1)S(1)}, bf16[256,128]{1,0:T(8,128)(2,1)S(1)}, u32[]{:S(2)}, u32[]{:S(2)}) collective-permute-start(bf16[256,128]{1,0:T(8,128)(2,1)S(1)} %get-tuple-element.42.refs_0_), channel_id=1, source_target_pairs={{0,12},{1,13},{2,14},{3,15},{4,0},{5,1},{6,2},{7,3},{8,4},{9,5},{1... | collective-permute-start | bytes 196616 | tf_op jit(solution)/shard_map/ppermute | solution.py:242
  75.6 7.0 %collective-permute-start.15 = (bf16[4,256,128]{2,1,0:T(8,128)(2,1)S(1)}, bf16[4,256,128]{2,1,0:T(8,128)(2,1)S(1)}, u32[]{:S(2)}, u32[]{:S(2)}) collective-permute-start(bf16[4,256,128]{2,1,0:T(8,128)(2,1)S(1)} %shard_map.109.after_ref.even_ref), channel_id=1, source_target_pairs={{0,1},{1,0},{2,3},{3,2},{4,5},{5,4},{6,7},{7,6},{8,9},{9,8},{10,11... | collective-permute-start | bytes 786440 | tf_op jit(solution)/shard_map/ppermute | solution.py:313
  76.8 0.7 copy-start.2
  77.5 14.8 %all-to-all-start.2 = ((bf16[16,64,128]{2,1,0:T(8,128)(2,1)}), bf16[16,64,128]{2,1,0:T(8,128)(2,1)}, u32[]{:S(2)}, u32[]{:S(2)}) async-start(bf16[16,64,128]{2,1,0:T(8,128)(2,1)} %copy-done.2), calls=%async_computation.2 | async-start | bytes 524288 | tf_op jit(solution)/shard_map/all_to_all | solution.py:234
  82.7 10.7 %collective-permute-start.16 = (bf16[4,256,128]{2,1,0:T(8,128)(2,1)S(1)}, bf16[4,256,128]{2,1,0:T(8,128)(2,1)}, u32[]{:S(2)}, u32[]{:S(2)}) collective-permute-start(bf16[4,256,128]{2,1,0:T(8,128)(2,1)S(1)} %shard_map.111.odd_ref), channel_id=1, source_target_pairs={{0,1},{1,0},{2,3},{3,2},{4,5},{5,4},{6,7},{7,6},{8,9},{9,8},{10,11... | collective-permute-start | bytes 786440 | tf_op jit(solution)/shard_map/ppermute | solution.py:322
  95.8 24.3 %copy-start.5 = (bf16[128,256]{1,0:T(8,128)(2,1)S(1)}, bf16[128,256]{1,0:T(8,128)(2,1)}, u32[]{:S(2)}) copy-start(bf16[128,256]{1,0:T(8,128)(2,1)} %ws_ref.1) | copy-start | bytes 196612
  95.8 5.3 %collective-permute-start.17 = (bf16[8,256,128]{2,1,0:T(8,128)(2,1)S(1)}, bf16[8,256,128]{2,1,0:T(8,128)(2,1)S(1)}, u32[]{:S(2)}, u32[]{:S(2)}) collective-permute-start(bf16[8,256,128]{2,1,0:T(8,128)(2,1)S(1)} %get-tuple-element.45), channel_id=1, source_target_pairs={{0,16},{16,0},{32,48},{48,32},{64,80},{80,64},{96,112},{112,96},{1... | collective-permute-start | bytes 1572872 | tf_op jit(solution)/shard_map/ppermute | solution.py:339
  99.6 1.5 %collective-permute-start.18 = (bf16[32,128]{1,0:T(8,128)(2,1)S(1)}, bf16[32,128]{1,0:T(8,128)(2,1)S(1)}, u32[]{:S(2)}, u32[]{:S(2)}) collective-permute-start(bf16[32,128]{1,0:T(8,128)(2,1)S(1)} %shard_map.113.after_ref.piece_ref), channel_id=1, source_target_pairs={{0,16},{16,0},{32,48},{48,32},{64,80},{80,64},{96,112},{112,96},{1... | collective-permute-start | bytes 24584 | tf_op jit(solution)/shard_map/ppermute | solution.py:328

commit v5 on v4

--- a/solution.py
+++ b/solution.py
@@ -11,15 +11,14 @@
 N_AX = 16
 BPD = 2
 STRIPE = N_AX * BPD
-UNROLL = 8
+UNROLL = 16
 PIECE = 32
 TAIL = 16
 HALF = N_AX // 2
 Z = 8
 NEAR = (0, 2, 6, 1, 7)
 FAR = (4, 3, 5)
-EVEN = (0, 4, 2, 6)
-ODD = (1, 5, 7, 3)
+SHIFTS = (0, 4, 1, 5, 7, 3, 2, 6)
 f32 = jnp.float32
 bf16 = jnp.bfloat16
 
@@ -155,11 +154,14 @@
 
 def stack_kernel(*refs):
     *parts, out_ref = refs
-    for j, part in enumerate(parts):
-        out_ref[j] = part[...]
-
-
-def spread_kernel(got_ref, after_ref, after2_ref, out_ref):
+    at = 0
+    for part in parts:
+        count = part.shape[0] if len(part.shape) == 3 else 1
+        out_ref[at : at + count] = part[...].reshape(count, *out_ref.shape[1:])
+        at += count
+
+
+def spread_kernel(got_ref, after_ref, out_ref):
     total = wide(narrow(got_ref))
     for d in range(N_AX):
         out_ref[d] = total
@@ -170,14 +172,13 @@
 
 
 def adjoint_kernel(
-    place_ref, count_ref, rows_ref, cols_ref, adj_ref, even_ref, odd_ref, even2_ref, odd2_ref, after_ref, keep_ref, send_ref, x_ref, acc_ref
+    place_ref, count_ref, rows_ref, cols_ref, adj_ref, mine_ref, other_ref, after_ref, keep_ref, send_ref, x_ref, acc_ref
 ):
     z, yl = place_ref[1], place_ref[2]
-    for mine, other, shifts in ((even_ref, even2_ref, EVEN), (odd_ref, odd2_ref, ODD)):
-        for j, s in enumerate(shifts):
-            at = 2 * ((z + Z - s) % Z)
-            x_ref[at + yl] = mine[j]
-            x_ref[at + 1 - yl] = other[j]
+    for j, s in enumerate(SHIFTS):
+        at = 2 * ((z + Z - s) % Z)
+        x_ref[at + yl] = mine_ref[j]
+        x_ref[at + 1 - yl] = other_ref[j]
 
     def product(k):
         row = rows_ref[0, k]
@@ -304,25 +305,14 @@
     )(in_specs=[VMEM] * (6 + len(sums)), out_specs=(VMEM,) * 3)(own, own_deg, *sums, features, cotangent, w_self, w_neigh)
 
     grads = exchange(grads, "row")
-    opposite = z_shift(back, 4)
-    even = [back, opposite, z_shift(back, 2), z_shift(back, 6)]
-    two = jnp.stack([back, opposite])
-    even = call(stack_kernel, shape((4, n, BLK), bf16), (), adj.size, adj.size)(
-        in_specs=[VMEM] * 4, out_specs=VMEM
-    )(*even)
-    even2 = lax.ppermute(even, "col", SWAP)
-    odd = [z_shift(two, 1), z_shift(two, 7)]
-    odd = call(stack_kernel, shape((2, 2, n, BLK), bf16), (), adj.size, adj.size)(
-        in_specs=[VMEM] * 2, out_specs=VMEM
-    )(*odd).reshape(4, n, BLK)
-    odd_at = odd
-    odd = call(gate_kernel, shape(odd.shape, bf16))(
-        in_specs=[ANY, ANY], out_specs=ANY, input_output_aliases={0: 0}
-    )(odd, even2)
-    odd2 = lax.ppermute(odd, "col", SWAP)
+    pair = jnp.stack([back, z_shift(back, 4)])
+    shards = call(stack_kernel, shape((Z, n, BLK), bf16), (), adj.size, adj.size)(in_specs=[VMEM] * 5, out_specs=VMEM)(
+        pair, z_shift(pair, 1), z_shift(pair, 7), z_shift(back, 2), z_shift(back, 6)
+    )
+    shards2 = lax.ppermute(shards, "col", SWAP)
     grads = call(spread_kernel, shape(grads.shape, bf16), (), adj.size, adj.size)(
-        in_specs=[VMEM, ANY, ANY], out_specs=VMEM
-    )(grads, even, odd_at)
+        in_specs=[VMEM, ANY], out_specs=VMEM
+    )(grads, shards)
     grads = exchange(grads, "col")
     piece = call(piece_kernel, shape((PIECE, BLK), bf16), (), adj.size, adj.size)(in_specs=[VMEM], out_specs=VMEM)(grads)
     piece2 = lax.ppermute(piece, "row", SWAP)
@@ -333,8 +323,8 @@
         [stripe, sums_acc],
         product_flops,
         adj.size * 4,
-    )(in_specs=[SMEM] * 4 + [VMEM] * 5 + [ANY], out_specs=(VMEM,) * 2)(
-        place, block_count, rows, cols, adj, even, odd, even2, odd2, piece
+    )(in_specs=[SMEM] * 4 + [VMEM] * 3 + [ANY], out_specs=(VMEM,) * 2)(
+        place, block_count, rows, cols, adj, shards, shards2, piece
     )
     send = lax.ppermute(send, "row", SWAP)
     merged = call(

time: 122 us -> 118 us (0.967)
  blocking collectives: 18.3 us -> 31.4 us
  waiting for transfers between devices: 28 us -> 21.3 us
  starting transfers between devices: 56.3 us -> 50.5 us
  Pallas kernels: 11.9 us -> 8.55 us
    all_to_all x1 -> x2, blocking collectives: 18.3 us -> 31.4 us  [exchange(): return lax.all_to_all(x, axis, 0, 0, axis_index_groups=groups)]
    all_to_all x3 -> x2, waiting for transfers between devices: 13.6 us -> 5.8 us  [exchange(): return lax.all_to_all(x, axis, 0, 0, axis_index_groups=groups)]
    all_to_all x3 -> x2, starting transfers between devices: 20.1 us -> 14.2 us  [exchange(): return lax.all_to_all(x, axis, 0, 0, axis_index_groups=groups)]
    ppermute x1, starting transfers between devices: 3.76 us -> 5.64 us  [local(): send = lax.ppermute(send, 'row', SWAP)]
    ppermute x2 -> x1, starting transfers between devices: 1.51 us -> 0.09 us  [local(): shards2 = lax.ppermute(shards, 'col', SWAP)]
    ppermute x12, waiting for transfers between devices: 6.31 us -> 7.55 us  [z_shift(): lax.ppermute(x, 'col', [(i, (i + 2 * s) % N_AX) for i in range(N_AX)])]
    unnamed x22 -> x20, local copies, waits for them, and re-layouts: 3.14 us -> 2.43 us
  transfers between devices with their start and end apart: 22 -> 20, of which waited for: 10 -> 8; matrix products, arithmetic and copies ran while one was open for 0% -> 0% of each run, Pallas kernels for 3% -> 1%
where the time goes in v5:
time: 118 us; the launch traced here: 117 us
  starting transfers between devices  50.5 us (43%)
  blocking collectives  31.4 us (27%)
  waiting for transfers between devices  21.3 us (18%)
  Pallas kernels  8.55 us (7%)
  local copies, waits for them, and re-layouts  4.15 us (4%)
  between operations  1.46 us (1%)
    all_to_all x2, blocking collectives, exchange(): return lax.all_to_all(x, axis, 0, 0, axis_index_groups=groups)  31.4 us
    ppermute x12, starting transfers between devices, z_shift(): lax.ppermute(x, 'col', [(i, (i + 2 * s) % N_AX) for i in range(N_AX)])  27.2 us
    all_to_all x2, starting transfers between devices, exchange(): return lax.all_to_all(x, axis, 0, 0, axis_index_groups=groups)  14.2 us
    ppermute x12, waiting for transfers between devices, z_shift(): lax.ppermute(x, 'col', [(i, (i + 2 * s) % N_AX) for i in range(N_AX)])  7.55 us
    all_to_all x2, waiting for transfers between devices, exchange(): return lax.all_to_all(x, axis, 0, 0, axis_index_groups=groups)  5.8 us
    ppermute x1, starting transfers between devices, local(): send = lax.ppermute(send, 'row', SWAP)  5.64 us
    ppermute x1, waiting for transfers between devices, local(): far_got = lax.ppermute(far_send, 'col', SWAP)  4.9 us
    unnamed x20, local copies, waits for them, and re-layouts  2.43 us
  transfers between devices with their start and end apart: 20, of which 8 were waited for; matrix products, arithmetic and copies ran while one was open for 0% of the time, Pallas kernels for 1%

profile of v5, /device:TPU:1, one launch (start us, length us, event | category | flops | bytes accessed | tf_op | source)
XLA Modules:
  0.0 117.5 jit_solution(6817442126961985861)
XLA Ops:
  0.6 0.0 copy-start.6
  0.6 0.0 copy-start.7
  0.7 1.7 %broadcast_in_dim.2 = bf16[8,256,128]{2,1,0:T(8,128)(2,1)} broadcast(bf16[256,128]{1,0:T(8,128)(2,1)} %refs_7_.1), dimensions={1,2} | broadcast | bytes 589824 | tf_op jit(solution)/shard_map/broadcast_in_dim | solution.py:259
  2.4 7.5 %all-to-all-start = ((bf16[8,256,128]{2,1,0:T(8,128)(2,1)}), bf16[8,256,128]{2,1,0:T(8,128)(2,1)S(1)}, u32[]{:S(2)}, u32[]{:S(2)}) async-start(bf16[8,256,128]{2,1,0:T(8,128)(2,1)} %broadcast_in_dim.2), calls=%async_computation | async-start | bytes 1048576 | tf_op jit(solution)/shard_map/all_to_all | solution.py:235
  10.5 0.0 copy-start
  10.5 1.7 %copy-done = bf16[1,1,80,128,128]{4,3,2,1,0:T(8,128)(2,1)S(1)} copy-done((bf16[1,1,80,128,128]{4,3,2,1,0:T(8,128)(2,1)S(1)}, bf16[1,1,80,128,128]{4,3,2,1,0:T(8,128)(2,1)}, u32[]{:S(2)}) %copy-start) | copy-done | bytes 2621464
  12.2 0.7 copy-done.5
  12.9 1.3 %shard_map.103.deg_ref = f32[16,8,128]{2,1,0:T(8,128)S(1)} custom-call(s32[1,1]{1,0:T(1,128)S(6)} %copy.13.count_ref, s32[1,80]{1,0:T(1,128)S(1)} %bitcast.12, bf16[80,128,128]{2,1,0:T(8,128)(2,1)S(1)} %bitcast.8), custom_call_target="tpu_custom_call" | custom-call | flops 20971520 | bytes 2621440 | tf_op jit(solution)/shard_map/pallas_call | solution.py:260
  14.2 5.8 %all-to-all-done.mine_ref = bf16[8,256,128]{2,1,0:T(8,128)(2,1)S(1)} async-done(((bf16[8,256,128]{2,1,0:T(8,128)(2,1)}), bf16[8,256,128]{2,1,0:T(8,128)(2,1)S(1)}, u32[]{:S(2)}, u32[]{:S(2)}) %all-to-all-start) | async-done | bytes 524320 | tf_op jit(solution)/shard_map/all_to_all | solution.py:235
  20.0 1.6 %collective-permute-start = (bf16[8,256,128]{2,1,0:T(8,128)(2,1)S(1)}, bf16[8,256,128]{2,1,0:T(8,128)(2,1)}, u32[]{:S(2)}, u32[]{:S(2)}) collective-permute-start(bf16[8,256,128]{2,1,0:T(8,128)(2,1)S(1)} %all-to-all-done.mine_ref), channel_id=1, source_target_pairs={{0,16},{16,0},{32,48},{48,32},{64,80},{80,64},{96,112},{112,96},{1... | collective-permute-start | bytes 1572872 | tf_op jit(solution)/shard_map/ppermute | solution.py:268
  21.7 0.1 pad_add_fusion.place_ref
  21.8 1.6 %collective-permute-done.other_ref = bf16[8,256,128]{2,1,0:T(8,128)(2,1)} collective-permute-done((bf16[8,256,128]{2,1,0:T(8,128)(2,1)S(1)}, bf16[8,256,128]{2,1,0:T(8,128)(2,1)}, u32[]{:S(2)}, u32[]{:S(2)}) %collective-permute-start) | collective-permute-done | bytes 524320 | tf_op jit(solution)/shard_map/ppermute | solution.py:268
  23.4 0.0 copy-done.6
  23.4 0.0 copy-start.3
  23.4 0.0 copy-start.8
  23.4 0.0 copy-start.9
  23.4 2.1 %shard_map.104 = (f32[5,256,128]{2,1,0:T(8,128)S(1)}, f32[3,256,128]{2,1,0:T(8,128)S(1)}, f32[5,8,128]{2,1,0:T(8,128)S(1)}, f32[3,8,128]{2,1,0:T(8,128)S(1)}, bf...) custom-call(s32[3]{0:T(128)S(1)} %pad_add_fusion.place_ref, s32[1,1]{1,0:T(1,128)S(6)} %copy.13.count_ref, ...), custom_call_target="tpu_custom_call" | custom-call | flops 335544320 | bytes 5242880 | tf_op jit(solution)/shard_map/pallas_call | solution.py:270
  25.6 0.5 collective-permute-start.1
  26.0 4.9 %collective-permute-done.1.after_ref.got_ref = bf16[3,272,128]{2,1,0:T(8,128)(2,1)S(1)} collective-permute-done((bf16[3,272,128]{2,1,0:T(8,128)(2,1)S(1)}, bf16[3,272,128]{2,1,0:T(8,128)(2,1)S(1)}, u32[]{:S(2)}, u32[]{:S(2)}) %collective-permute-start.1) | collective-permute-done | bytes 208928 | tf_op jit(solution)/shard_map/ppermute | solution.py:286
  30.9 1.1 collective-permute-start.2
  32.1 0.1 shard_map.107
  32.1 7.0 %collective-permute-start.3 = (bf16[272,128]{1,0:T(8,128)(2,1)S(1)}, bf16[272,128]{1,0:T(8,128)(2,1)S(1)}, u32[]{:S(2)}, u32[]{:S(2)}) collective-permute-start(bf16[272,128]{1,0:T(8,128)(2,1)S(1)} %get-tuple-element.35), channel_id=1, source_target_pairs={{0,8},{1,9},{2,10},{3,11},{4,12},{5,13},{6,14},{7,15},{8,0},{9,1},... | collective-permute-start | bytes 208904 | tf_op jit(solution)/shard_map/ppermute | solution.py:243
  39.1 3.2 %collective-permute-start.4 = (bf16[272,128]{1,0:T(8,128)(2,1)S(1)}, bf16[272,128]{1,0:T(8,128)(2,1)S(1)}, u32[]{:S(2)}, u32[]{:S(2)}) collective-permute-start(bf16[272,128]{1,0:T(8,128)(2,1)S(1)} %get-tuple-element.36), channel_id=1, source_target_pairs={{0,6},{1,7},{2,8},{3,9},{4,10},{5,11},{6,12},{7,13},{8,14},{9,15},... | collective-permute-start | bytes 208904 | tf_op jit(solution)/shard_map/ppermute | solution.py:243
  42.3 1.3 %collective-permute-start.5 = (bf16[272,128]{1,0:T(8,128)(2,1)S(1)}, bf16[272,128]{1,0:T(8,128)(2,1)S(1)}, u32[]{:S(2)}, u32[]{:S(2)}) collective-permute-start(bf16[272,128]{1,0:T(8,128)(2,1)S(1)} %get-tuple-element.37), channel_id=1, source_target_pairs={{0,10},{1,11},{2,12},{3,13},{4,14},{5,15},{6,0},{7,1},{8,2},{9,3},... | collective-permute-start | bytes 208904 | tf_op jit(solution)/shard_map/ppermute | solution.py:243
  43.6 0.0 collective-permute-done.2.got_ref
  43.6 0.1 shard_map.106
  43.6 3.2 %collective-permute-start.6 = (bf16[272,128]{1,0:T(8,128)(2,1)S(1)}, bf16[272,128]{1,0:T(8,128)(2,1)S(1)}, u32[]{:S(2)}, u32[]{:S(2)}) collective-permute-start(bf16[272,128]{1,0:T(8,128)(2,1)S(1)} %get-tuple-element.38), channel_id=1, source_target_pairs={{0,4},{1,5},{2,6},{3,7},{4,8},{5,9},{6,10},{7,11},{8,12},{9,13},{1... | collective-permute-start | bytes 208904 | tf_op jit(solution)/shard_map/ppermute | solution.py:243
  46.8 0.9 collective-permute-start.7
  47.7 0.0 collective-permute-done.3.refs_0_
  47.7 2.2 %collective-permute-start.8 = (bf16[272,128]{1,0:T(8,128)(2,1)S(1)}, bf16[272,128]{1,0:T(8,128)(2,1)S(1)}, u32[]{:S(2)}, u32[]{:S(2)}) collective-permute-start(bf16[272,128]{1,0:T(8,128)(2,1)S(1)} %get-tuple-element.40), channel_id=1, source_target_pairs={{0,2},{1,3},{2,4},{3,5},{4,6},{5,7},{6,8},{7,9},{8,10},{9,11},{10,... | collective-permute-start | bytes 208904 | tf_op jit(solution)/shard_map/ppermute | solution.py:243
  49.9 0.0 collective-permute-done.4.refs_1_
  49.9 1.2 collective-permute-start.9
  51.1 0.0 collective-permute-done.5.refs_2_
  51.1 0.0 collective-permute-done.6.refs_3_
  51.1 2.0 %collective-permute-done.7.refs_4_ = bf16[272,128]{1,0:T(8,128)(2,1)S(1)} collective-permute-done((bf16[272,128]{1,0:T(8,128)(2,1)S(1)}, bf16[272,128]{1,0:T(8,128)(2,1)S(1)}, u32[]{:S(2)}, u32[]{:S(2)}) %collective-permute-start.7) | collective-permute-done | bytes 69664 | tf_op jit(solution)/shard_map/ppermute | solution.py:243
  53.1 0.9 collective-permute-done.8.refs_5_
  53.9 1.7 %collective-permute-done.9.refs_6_ = bf16[272,128]{1,0:T(8,128)(2,1)S(1)} collective-permute-done((bf16[272,128]{1,0:T(8,128)(2,1)S(1)}, bf16[272,128]{1,0:T(8,128)(2,1)S(1)}, u32[]{:S(2)}, u32[]{:S(2)}) %collective-permute-start.9) | collective-permute-done | bytes 69664 | tf_op jit(solution)/shard_map/ppermute | solution.py:243
  55.6 0.0 copy-done.3
  55.6 1.3 %shard_map.108 = (bf16[256,128]{1,0:T(8,128)(2,1)S(1)}, bf16[16,64,128]{2,1,0:T(8,128)(2,1)}, bf16[256,256]{1,0:T(8,128)(2,1)S(1)}) custom-call(f32[256,128]{1,0:T(8,128)S(1)} %get-tuple-element.31.own_ref, f32[8,128]{1,0:T(8,128)S(1)} %get-tuple-element.32.own_deg_ref, bf16[272,128]{1,0:T(8,128)(2,1)S(1)} %collective-permute-done.3.refs_0_, ...), custom_call_target="tpu_custom_call" | custom-call | flops 335544320 | bytes 1310720 | tf_op jit(solution)/shard_map/pallas_call | solution.py:299
  56.9 2.1 %collective-permute-start.10 = (bf16[256,128]{1,0:T(8,128)(2,1)S(1)}, bf16[256,128]{1,0:T(8,128)(2,1)S(1)}, u32[]{:S(2)}, u32[]{:S(2)}) collective-permute-start(bf16[256,128]{1,0:T(8,128)(2,1)S(1)} %get-tuple-element.42), channel_id=1, source_target_pairs={{0,8},{1,9},{2,10},{3,11},{4,12},{5,13},{6,14},{7,15},{8,0},{9,1},... | collective-permute-start | bytes 196616 | tf_op jit(solution)/shard_map/ppermute | solution.py:243
  58.9 6.7 %all-to-all-start.1 = ((bf16[16,64,128]{2,1,0:T(8,128)(2,1)}), bf16[16,64,128]{2,1,0:T(8,128)(2,1)S(1)}, u32[]{:S(2)}, u32[]{:S(2)}) async-start(bf16[16,64,128]{2,1,0:T(8,128)(2,1)} %get-tuple-element.43), calls=%async_computation.1 | async-start | bytes 524288 | tf_op jit(solution)/shard_map/all_to_all | solution.py:235
  65.7 0.0 collective-permute-done.10
  65.7 0.7 collective-permute-start.11
  66.4 2.1 %collective-permute-start.12 = (bf16[2,256,128]{2,1,0:T(8,128)(2,1)S(1)}, bf16[2,256,128]{2,1,0:T(8,128)(2,1)S(1)}, u32[]{:S(2)}, u32[]{:S(2)}) collective-permute-start(bf16[2,256,128]{2,1,0:T(8,128)(2,1)S(1)} %pad_maximum_fusion.refs_0_), channel_id=1, source_target_pairs={{0,14},{1,15},{2,0},{3,1},{4,2},{5,3},{6,4},{7,5},{8,6},{9,7},{10,... | collective-permute-start | bytes 393224 | tf_op jit(solution)/shard_map/ppermute | solution.py:243
  68.5 0.0 collective-permute-start.13
  68.5 3.6 %collective-permute-start.14 = (bf16[256,128]{1,0:T(8,128)(2,1)S(1)}, bf16[256,128]{1,0:T(8,128)(2,1)S(1)}, u32[]{:S(2)}, u32[]{:S(2)}) collective-permute-start(bf16[256,128]{1,0:T(8,128)(2,1)S(1)} %get-tuple-element.42), channel_id=1, source_target_pairs={{0,12},{1,13},{2,14},{3,15},{4,0},{5,1},{6,2},{7,3},{8,4},{9,5},{1... | collective-permute-start | bytes 196616 | tf_op jit(solution)/shard_map/ppermute | solution.py:243
  72.0 3.0 %collective-permute-done.13.refs_3_ = bf16[256,128]{1,0:T(8,128)(2,1)S(1)} collective-permute-done((bf16[256,128]{1,0:T(8,128)(2,1)S(1)}, bf16[256,128]{1,0:T(8,128)(2,1)S(1)}, u32[]{:S(2)}, u32[]{:S(2)}) %collective-permute-start.13) | collective-permute-done | bytes 65568 | tf_op jit(solution)/shard_map/ppermute | solution.py:243
  75.0 0.0 collective-permute-done.14.refs_4_
  75.0 0.0 collective-permute-done.11.refs_1_
  75.0 0.0 collective-permute-done.12.refs_2_
  75.1 0.1 collective-permute-start.15
  75.2 0.0 all-to-all-done.1.got_ref
  75.2 0.1 shard_map.110
  75.3 15.2 %all_to_all.20.got_ref = bf16[16,64,128]{2,1,0:T(8,128)(2,1)S(1)} all-to-all(bf16[16,64,128]{2,1,0:T(8,128)(2,1)S(1)} %shard_map.110), channel_id=1, replica_groups=mesh['row'=16,'col'=16] {'col'}, dimensions={0} | all-to-all | bytes 524288 | tf_op jit(solution)/shard_map/all_to_all | solution.py:235
  90.5 0.0 collective-permute-done.15.other_ref
  90.5 2.0 %shard_map.112 = (f32[8,256,128]{2,1,0:T(8,128)S(1)}, bf16[8,256,128]{2,1,0:T(8,128)(2,1)S(1)}) custom-call(s32[3]{0:T(128)S(1)} %pad_add_fusion.place_ref, s32[1,1]{1,0:T(1,128)S(6)} %copy.13.count_ref, s32[1,80]{1,0:T(1,128)S(1)} %bitcast.14, s32[1,80]{1,0:T(1,128)S(1)} %bitcast.16, bf16[80,128,128]{2,1,0:T(8,128)(2,1)S(1)} %bitcast.10, ...), custom_call_target="tpu_custom_call" | custom-call | flops 335544320 | bytes 5242880 | tf_op jit(solution)/shard_map/pallas_call | solution.py:320
  92.6 0.0 copy-start.4
  92.6 5.6 %collective-permute-start.16 = (bf16[8,256,128]{2,1,0:T(8,128)(2,1)S(1)}, bf16[8,256,128]{2,1,0:T(8,128)(2,1)S(1)}, u32[]{:S(2)}, u32[]{:S(2)}) collective-permute-start(bf16[8,256,128]{2,1,0:T(8,128)(2,1)S(1)} %get-tuple-element.45), channel_id=1, source_target_pairs={{0,16},{16,0},{32,48},{48,32},{64,80},{80,64},{96,112},{112,96},{1... | collective-permute-start | bytes 1572872 | tf_op jit(solution)/shard_map/ppermute | solution.py:329
  98.2 0.1 collective-permute-start.17
  98.3 1.4 %collective-permute-done.17.piece2_ref = bf16[32,128]{1,0:T(8,128)(2,1)S(1)} collective-permute-done((bf16[32,128]{1,0:T(8,128)(2,1)S(1)}, bf16[32,128]{1,0:T(8,128)(2,1)S(1)}, u32[]{:S(2)}, u32[]{:S(2)}) %collective-permute-start.17) | collective-permute-done | bytes 8224 | tf_op jit(solution)/shard_map/ppermute | solution.py:318
  99.8 0.0 collective-permute-done.16.got_ref
  99.8 0.6 shard_map.113
  100.4 16.2 %all_to_all.21.got_ref = bf16[8,320,128]{2,1,0:T(8,128)(2,1)S(1)} all-to-all(bf16[8,320,128]{2,1,0:T(8,128)(2,1)S(1)} %shard_map.113), channel_id=1, replica_groups={{0,32,64,96,128,160,192,224},{16,48,80,112,144,176,208,240},{1,33,65,97..., dimensions={0} | all-to-all | bytes 1310720 | tf_op jit(solution)/shard_map/all_to_all | solution.py:235
  116.6 0.9 shard_map.114
  (13 shorter events, 0.1 us)
Async XLA Ops:
  0.6 22.7 %copy-start.6 = (s32[1,1,80]{2,1,0:T(1,128)S(1)}, s32[1,1,80]{2,1,0:T(1,128)}, u32[]{:S(2)}) copy-start(s32[1,1,80]{2,1,0:T(1,128)} %param.13) | copy-start | bytes 964
  0.6 22.7 %copy-start.7 = (s32[1,1,80]{2,1,0:T(1,128)S(1)}, s32[1,1,80]{2,1,0:T(1,128)}, u32[]{:S(2)}) copy-start(s32[1,1,80]{2,1,0:T(1,128)} %param.14) | copy-start | bytes 964
  2.4 17.7 %all-to-all-start = ((bf16[8,256,128]{2,1,0:T(8,128)(2,1)}), bf16[8,256,128]{2,1,0:T(8,128)(2,1)S(1)}, u32[]{:S(2)}, u32[]{:S(2)}) async-start(bf16[8,256,128]{2,1,0:T(8,128)(2,1)} %broadcast_in_dim.2), calls=%async_computation | async-start | bytes 1048576 | tf_op jit(solution)/shard_map/all_to_all | solution.py:235
  10.5 1.7 %copy-start = (bf16[1,1,80,128,128]{4,3,2,1,0:T(8,128)(2,1)S(1)}, bf16[1,1,80,128,128]{4,3,2,1,0:T(8,128)(2,1)}, u32[]{:S(2)}) copy-start(bf16[1,1,80,128,128]{4,3,2,1,0:T(8,128)(2,1)} %param.12) | copy-start | bytes 7864324
  12.2 0.7 copy-start.5
  12.9 10.5 %copy-start.1 = (bf16[1,1,80,128,128]{4,3,2,1,0:T(8,128)(2,1)S(1)}, bf16[1,1,80,128,128]{4,3,2,1,0:T(8,128)(2,1)}, u32[]{:S(2)}) copy-start(bf16[1,1,80,128,128]{4,3,2,1,0:T(8,128)(2,1)} %param.12) | copy-start | bytes 7864324
  20.0 3.3 %collective-permute-start = (bf16[8,256,128]{2,1,0:T(8,128)(2,1)S(1)}, bf16[8,256,128]{2,1,0:T(8,128)(2,1)}, u32[]{:S(2)}, u32[]{:S(2)}) collective-permute-start(bf16[8,256,128]{2,1,0:T(8,128)(2,1)S(1)} %all-to-all-done.mine_ref), channel_id=1, source_target_pairs={{0,16},{16,0},{32,48},{48,32},{64,80},{80,64},{96,112},{112,96},{1... | collective-permute-start | bytes 1572872 | tf_op jit(solution)/shard_map/ppermute | solution.py:268
  23.4 32.2 %copy-start.2 = (bf16[256,128]{1,0:T(8,128)(2,1)S(1)}, bf16[256,128]{1,0:T(8,128)(2,1)}, u32[]{:S(2)}) copy-start(bf16[256,128]{1,0:T(8,128)(2,1)} %refs_7_.1) | copy-start | bytes 196612
  23.4 32.2 %copy-start.3 = (bf16[128,256]{1,0:T(8,128)(2,1)S(1)}, bf16[128,256]{1,0:T(8,128)(2,1)}, u32[]{:S(2)}) copy-start(bf16[128,256]{1,0:T(8,128)(2,1)} %ws_ref.1) | copy-start | bytes 196612
  23.4 32.2 %copy-start.8 = (bf16[256,256]{1,0:T(8,128)(2,1)S(1)}, bf16[256,256]{1,0:T(8,128)(2,1)}, u32[]{:S(2)}) copy-start(bf16[256,256]{1,0:T(8,128)(2,1)} %refs_8_.1) | copy-start | bytes 393220
  23.4 32.2 %copy-start.9 = (bf16[128,256]{1,0:T(8,128)(2,1)S(1)}, bf16[128,256]{1,0:T(8,128)(2,1)}, u32[]{:S(2)}) copy-start(bf16[128,256]{1,0:T(8,128)(2,1)} %refs_10_.1) | copy-start | bytes 196612
  25.6 5.4 %collective-permute-start.1 = (bf16[3,272,128]{2,1,0:T(8,128)(2,1)S(1)}, bf16[3,272,128]{2,1,0:T(8,128)(2,1)S(1)}, u32[]{:S(2)}, u32[]{:S(2)}) collective-permute-start(bf16[3,272,128]{2,1,0:T(8,128)(2,1)S(1)} %get-tuple-element.30), channel_id=1, source_target_pairs={{0,1},{1,0},{2,3},{3,2},{4,5},{5,4},{6,7},{7,6},{8,9},{9,8},{10,11... | collective-permute-start | bytes 626696 | tf_op jit(solution)/shard_map/ppermute | solution.py:286
  30.9 12.6 %collective-permute-start.2 = (bf16[5,272,128]{2,1,0:T(8,128)(2,1)S(1)}, bf16[5,272,128]{2,1,0:T(8,128)(2,1)S(1)}, u32[]{:S(2)}, u32[]{:S(2)}) collective-permute-start(bf16[5,272,128]{2,1,0:T(8,128)(2,1)S(1)} %shard_map.105), channel_id=1, source_target_pairs={{0,1},{1,0},{2,3},{3,2},{4,5},{5,4},{6,7},{7,6},{8,9},{9,8},{10,11... | collective-permute-start | bytes 1044488 | tf_op jit(solution)/shard_map/ppermute | solution.py:290
  32.1 15.6 %collective-permute-start.3 = (bf16[272,128]{1,0:T(8,128)(2,1)S(1)}, bf16[272,128]{1,0:T(8,128)(2,1)S(1)}, u32[]{:S(2)}, u32[]{:S(2)}) collective-permute-start(bf16[272,128]{1,0:T(8,128)(2,1)S(1)} %get-tuple-element.35), channel_id=1, source_target_pairs={{0,8},{1,9},{2,10},{3,11},{4,12},{5,13},{6,14},{7,15},{8,0},{9,1},... | collective-permute-start | bytes 208904 | tf_op jit(solution)/shard_map/ppermute | solution.py:243
  39.1 10.8 %collective-permute-start.4 = (bf16[272,128]{1,0:T(8,128)(2,1)S(1)}, bf16[272,128]{1,0:T(8,128)(2,1)S(1)}, u32[]{:S(2)}, u32[]{:S(2)}) collective-permute-start(bf16[272,128]{1,0:T(8,128)(2,1)S(1)} %get-tuple-element.36), channel_id=1, source_target_pairs={{0,6},{1,7},{2,8},{3,9},{4,10},{5,11},{6,12},{7,13},{8,14},{9,15},... | collective-permute-start | bytes 208904 | tf_op jit(solution)/shard_map/ppermute | solution.py:243
  42.3 8.8 %collective-permute-start.5 = (bf16[272,128]{1,0:T(8,128)(2,1)S(1)}, bf16[272,128]{1,0:T(8,128)(2,1)S(1)}, u32[]{:S(2)}, u32[]{:S(2)}) collective-permute-start(bf16[272,128]{1,0:T(8,128)(2,1)S(1)} %get-tuple-element.37), channel_id=1, source_target_pairs={{0,10},{1,11},{2,12},{3,13},{4,14},{5,15},{6,0},{7,1},{8,2},{9,3},... | collective-permute-start | bytes 208904 | tf_op jit(solution)/shard_map/ppermute | solution.py:243
  43.6 7.4 %collective-permute-start.6 = (bf16[272,128]{1,0:T(8,128)(2,1)S(1)}, bf16[272,128]{1,0:T(8,128)(2,1)S(1)}, u32[]{:S(2)}, u32[]{:S(2)}) collective-permute-start(bf16[272,128]{1,0:T(8,128)(2,1)S(1)} %get-tuple-element.38), channel_id=1, source_target_pairs={{0,4},{1,5},{2,6},{3,7},{4,8},{5,9},{6,10},{7,11},{8,12},{9,13},{1... | collective-permute-start | bytes 208904 | tf_op jit(solution)/shard_map/ppermute | solution.py:243
  46.8 6.3 %collective-permute-start.7 = (bf16[272,128]{1,0:T(8,128)(2,1)S(1)}, bf16[272,128]{1,0:T(8,128)(2,1)S(1)}, u32[]{:S(2)}, u32[]{:S(2)}) collective-permute-start(bf16[272,128]{1,0:T(8,128)(2,1)S(1)} %get-tuple-element.39), channel_id=1, source_target_pairs={{0,12},{1,13},{2,14},{3,15},{4,0},{5,1},{6,2},{7,3},{8,4},{9,5},{1... | collective-permute-start | bytes 208904 | tf_op jit(solution)/shard_map/ppermute | solution.py:243
  47.7 6.3 %collective-permute-start.8 = (bf16[272,128]{1,0:T(8,128)(2,1)S(1)}, bf16[272,128]{1,0:T(8,128)(2,1)S(1)}, u32[]{:S(2)}, u32[]{:S(2)}) collective-permute-start(bf16[272,128]{1,0:T(8,128)(2,1)S(1)} %get-tuple-element.40), channel_id=1, source_target_pairs={{0,2},{1,3},{2,4},{3,5},{4,6},{5,7},{6,8},{7,9},{8,10},{9,11},{10,... | collective-permute-start | bytes 208904 | tf_op jit(solution)/shard_map/ppermute | solution.py:243
  49.9 5.7 %collective-permute-start.9 = (bf16[272,128]{1,0:T(8,128)(2,1)S(1)}, bf16[272,128]{1,0:T(8,128)(2,1)S(1)}, u32[]{:S(2)}, u32[]{:S(2)}) collective-permute-start(bf16[272,128]{1,0:T(8,128)(2,1)S(1)} %get-tuple-element.41), channel_id=1, source_target_pairs={{0,14},{1,15},{2,0},{3,1},{4,2},{5,3},{6,4},{7,5},{8,6},{9,7},{10,... | collective-permute-start | bytes 208904 | tf_op jit(solution)/shard_map/ppermute | solution.py:243
  56.9 8.8 %collective-permute-start.10 = (bf16[256,128]{1,0:T(8,128)(2,1)S(1)}, bf16[256,128]{1,0:T(8,128)(2,1)S(1)}, u32[]{:S(2)}, u32[]{:S(2)}) collective-permute-start(bf16[256,128]{1,0:T(8,128)(2,1)S(1)} %get-tuple-element.42), channel_id=1, source_target_pairs={{0,8},{1,9},{2,10},{3,11},{4,12},{5,13},{6,14},{7,15},{8,0},{9,1},... | collective-permute-start | bytes 196616 | tf_op jit(solution)/shard_map/ppermute | solution.py:243
  58.9 16.3 %all-to-all-start.1 = ((bf16[16,64,128]{2,1,0:T(8,128)(2,1)}), bf16[16,64,128]{2,1,0:T(8,128)(2,1)S(1)}, u32[]{:S(2)}, u32[]{:S(2)}) async-start(bf16[16,64,128]{2,1,0:T(8,128)(2,1)} %get-tuple-element.43), calls=%async_computation.1 | async-start | bytes 524288 | tf_op jit(solution)/shard_map/all_to_all | solution.py:235
  65.7 9.3 %collective-permute-start.11 = (bf16[2,256,128]{2,1,0:T(8,128)(2,1)S(1)}, bf16[2,256,128]{2,1,0:T(8,128)(2,1)S(1)}, u32[]{:S(2)}, u32[]{:S(2)}) collective-permute-start(bf16[2,256,128]{2,1,0:T(8,128)(2,1)S(1)} %pad_maximum_fusion.refs_0_), channel_id=1, source_target_pairs={{0,2},{1,3},{2,4},{3,5},{4,6},{5,7},{6,8},{7,9},{8,10},{9,11},{10,... | collective-permute-start | bytes 393224 | tf_op jit(solution)/shard_map/ppermute | solution.py:243
  66.4 8.7 %collective-permute-start.12 = (bf16[2,256,128]{2,1,0:T(8,128)(2,1)S(1)}, bf16[2,256,128]{2,1,0:T(8,128)(2,1)S(1)}, u32[]{:S(2)}, u32[]{:S(2)}) collective-permute-start(bf16[2,256,128]{2,1,0:T(8,128)(2,1)S(1)} %pad_maximum_fusion.refs_0_), channel_id=1, source_target_pairs={{0,14},{1,15},{2,0},{3,1},{4,2},{5,3},{6,4},{7,5},{8,6},{9,7},{10,... | collective-permute-start | bytes 393224 | tf_op jit(solution)/shard_map/ppermute | solution.py:243
  68.5 6.6 %collective-permute-start.13 = (bf16[256,128]{1,0:T(8,128)(2,1)S(1)}, bf16[256,128]{1,0:T(8,128)(2,1)S(1)}, u32[]{:S(2)}, u32[]{:S(2)}) collective-permute-start(bf16[256,128]{1,0:T(8,128)(2,1)S(1)} %get-tuple-element.42), channel_id=1, source_target_pairs={{0,4},{1,5},{2,6},{3,7},{4,8},{5,9},{6,10},{7,11},{8,12},{9,13},{1... | collective-permute-start | bytes 196616 | tf_op jit(solution)/shard_map/ppermute | solution.py:243
  68.5 6.6 %collective-permute-start.14 = (bf16[256,128]{1,0:T(8,128)(2,1)S(1)}, bf16[256,128]{1,0:T(8,128)(2,1)S(1)}, u32[]{:S(2)}, u32[]{:S(2)}) collective-permute-start(bf16[256,128]{1,0:T(8,128)(2,1)S(1)} %get-tuple-element.42), channel_id=1, source_target_pairs={{0,12},{1,13},{2,14},{3,15},{4,0},{5,1},{6,2},{7,3},{8,4},{9,5},{1... | collective-permute-start | bytes 196616 | tf_op jit(solution)/shard_map/ppermute | solution.py:243
  75.1 15.4 %collective-permute-start.15 = (bf16[8,256,128]{2,1,0:T(8,128)(2,1)S(1)}, bf16[8,256,128]{2,1,0:T(8,128)(2,1)}, u32[]{:S(2)}, u32[]{:S(2)}) collective-permute-start(bf16[8,256,128]{2,1,0:T(8,128)(2,1)S(1)} %shard_map.109.after_ref.mine_ref), channel_id=1, source_target_pairs={{0,1},{1,0},{2,3},{3,2},{4,5},{5,4},{6,7},{7,6},{8,9},{9,8},{10,11... | collective-permute-start | bytes 1572872 | tf_op jit(solution)/shard_map/ppermute | solution.py:312
  92.6 24.1 %copy-start.4 = (bf16[128,256]{1,0:T(8,128)(2,1)S(1)}, bf16[128,256]{1,0:T(8,128)(2,1)}, u32[]{:S(2)}) copy-start(bf16[128,256]{1,0:T(8,128)(2,1)} %ws_ref.1) | copy-start | bytes 196612
  92.6 7.2 %collective-permute-start.16 = (bf16[8,256,128]{2,1,0:T(8,128)(2,1)S(1)}, bf16[8,256,128]{2,1,0:T(8,128)(2,1)S(1)}, u32[]{:S(2)}, u32[]{:S(2)}) collective-permute-start(bf16[8,256,128]{2,1,0:T(8,128)(2,1)S(1)} %get-tuple-element.45), channel_id=1, source_target_pairs={{0,16},{16,0},{32,48},{48,32},{64,80},{80,64},{96,112},{112,96},{1... | collective-permute-start | bytes 1572872 | tf_op jit(solution)/shard_map/ppermute | solution.py:329
  98.2 1.5 %collective-permute-start.17 = (bf16[32,128]{1,0:T(8,128)(2,1)S(1)}, bf16[32,128]{1,0:T(8,128)(2,1)S(1)}, u32[]{:S(2)}, u32[]{:S(2)}) collective-permute-start(bf16[32,128]{1,0:T(8,128)(2,1)S(1)} %shard_map.111.after_ref.piece_ref), channel_id=1, source_target_pairs={{0,16},{16,0},{32,48},{48,32},{64,80},{80,64},{96,112},{112,96},{1... | collective-permute-start | bytes 24584 | tf_op jit(solution)/shard_map/ppermute | solution.py:318

commit v6 on v5

--- a/solution.py
+++ b/solution.py
@@ -11,7 +11,7 @@
 N_AX = 16
 BPD = 2
 STRIPE = N_AX * BPD
-UNROLL = 16
+UNROLL = 20
 PIECE = 32
 TAIL = 16
 HALF = N_AX // 2
@@ -120,7 +120,7 @@
 
 def narrow(parts):
     total = parts[0].astype(f32)
-    for d in range(1, N_AX):
+    for d in range(1, parts.shape[0]):
         total += parts[d].astype(f32)
     return total[:PIECE] + total[PIECE:]
 
@@ -153,7 +153,7 @@
 
 
 def stack_kernel(*refs):
-    *parts, out_ref = refs
+    *parts, _, out_ref = refs
     at = 0
     for part in parts:
         count = part.shape[0] if len(part.shape) == 3 else 1
@@ -161,9 +161,14 @@
         at += count
 
 
-def spread_kernel(got_ref, after_ref, out_ref):
-    total = wide(narrow(got_ref))
-    for d in range(N_AX):
+def row_kernel(got_ref, out_ref):
+    out_ref[...] = wide(narrow(got_ref))
+
+
+def spread_kernel(mine_ref, other_ref, after_ref, out_ref):
+    total = mine_ref[...].astype(f32) + other_ref[...].astype(f32)
+    total = wide(total[:PIECE] + total[PIECE:])
+    for d in range(out_ref.shape[0]):
         out_ref[d] = total
 
 
@@ -235,7 +240,7 @@
     return lax.all_to_all(x, axis, 0, 0, axis_index_groups=groups)
 
 
-SAME_CORE = [list(range(core, N_AX, 2)) for core in range(2)]
+SAME_PARITY = [list(range(core, N_AX, 2)) for core in range(2)]
 SWAP = [(i, i ^ 1) for i in range(N_AX)]
 
 
@@ -256,7 +261,7 @@
     row_at, col_at = lax.axis_index("row"), lax.axis_index("col")
     place = jnp.stack([row_at % 2, col_at // 2, col_at % 2]).astype(jnp.int32)
 
-    mine = exchange(jnp.broadcast_to(features[None], (HALF, n, width)), "row", SAME_CORE)
+    mine = exchange(jnp.broadcast_to(features[None], (HALF, n, width)), "row", SAME_PARITY)
     degree = call(
         degree_kernel,
         shape((N_AX, 8, BLK), f32),
@@ -306,14 +311,16 @@
 
     grads = exchange(grads, "row")
     pair = jnp.stack([back, z_shift(back, 4)])
-    shards = call(stack_kernel, shape((Z, n, BLK), bf16), (), adj.size, adj.size)(in_specs=[VMEM] * 5, out_specs=VMEM)(
-        pair, z_shift(pair, 1), z_shift(pair, 7), z_shift(back, 2), z_shift(back, 6)
+    part = call(row_kernel, shape((2 * PIECE, BLK), bf16), (), adj.size, adj.size)(in_specs=[VMEM], out_specs=VMEM)(grads)
+    part2 = lax.ppermute(part, "col", SWAP)
+    shards = call(stack_kernel, shape((Z, n, BLK), bf16), (), adj.size, adj.size)(in_specs=[VMEM] * 5 + [ANY], out_specs=VMEM)(
+        pair, z_shift(pair, 1), z_shift(pair, 7), z_shift(back, 2), z_shift(back, 6), part2
     )
     shards2 = lax.ppermute(shards, "col", SWAP)
-    grads = call(spread_kernel, shape(grads.shape, bf16), (), adj.size, adj.size)(
-        in_specs=[VMEM, ANY], out_specs=VMEM
-    )(grads, shards)
-    grads = exchange(grads, "col")
+    grads = call(spread_kernel, shape((Z, 2 * PIECE, BLK), bf16), (), adj.size, adj.size)(
+        in_specs=[VMEM] * 2 + [ANY], out_specs=VMEM
+    )(part, part2, shards)
+    grads = exchange(grads, "col", SAME_PARITY)
     piece = call(piece_kernel, shape((PIECE, BLK), bf16), (), adj.size, adj.size)(in_specs=[VMEM], out_specs=VMEM)(grads)
     piece2 = lax.ppermute(piece, "row", SWAP)
 
@@ -334,7 +341,7 @@
         adj.size,
         adj.size,
     )(in_specs=[SMEM] + [VMEM] * 4, out_specs=VMEM)(place, keep, send, piece, piece2)
-    merged = exchange(merged, "row", SAME_CORE)
+    merged = exchange(merged, "row", SAME_PARITY)
     scale = (n * N_AX * N_AX) ** (-0.5)
     return call(
         functools.partial(final_kernel, scale),

time: 118 us -> 116 us (0.983)
  blocking collectives: 31.4 us -> 29.3 us
    ppermute x12, waiting for transfers between devices: 7.55 us -> 3.73 us  [z_shift(): lax.ppermute(x, 'col', [(i, (i + 2 * s) % N_AX) for i in range(N_AX)])]
    ppermute x1, starting transfers between devices: 5.64 us -> 3.24 us  [local(): send = lax.ppermute(send, 'row', SWAP)]
    all_to_all x2, blocking collectives: 31.4 us -> 29.3 us  [exchange(): return lax.all_to_all(x, axis, 0, 0, axis_index_groups=groups)]
    ppermute x0 -> x1, waiting for transfers between devices: none -> 1.6 us  [local(): part2 = lax.ppermute(part, 'col', SWAP)]
    all_to_all x2, waiting for transfers between devices: 5.8 us -> 7 us  [exchange(): return lax.all_to_all(x, axis, 0, 0, axis_index_groups=groups)]
  transfers between devices with their start and end apart: 20 -> 21, of which waited for: 8 -> 9; matrix products, arithmetic and copies ran while one was open for 0% -> 1% of each run, Pallas kernels for 1% -> 1%
where the time goes in v6:
time: 116 us
  starting transfers between devices  50.1 us (43%)
  blocking collectives  29.3 us (25%)
  waiting for transfers between devices  21.3 us (18%)
  Pallas kernels  8.33 us (7%)
  local copies, waits for them, and re-layouts  4.14 us (4%)
  between operations  1.45 us (1%)
    all_to_all x2, blocking collectives, exchange(): return lax.all_to_all(x, axis, 0, 0, axis_index_groups=groups)  29.3 us
    ppermute x12, starting transfers between devices, z_shift(): lax.ppermute(x, 'col', [(i, (i + 2 * s) % N_AX) for i in range(N_AX)])  27 us
    all_to_all x2, starting transfers between devices, exchange(): return lax.all_to_all(x, axis, 0, 0, axis_index_groups=groups)  15.4 us
    all_to_all x2, waiting for transfers between devices, exchange(): return lax.all_to_all(x, axis, 0, 0, axis_index_groups=groups)  7 us
    ppermute x1, waiting for transfers between devices, local(): far_got = lax.ppermute(far_send, 'col', SWAP)  5.95 us
    ppermute x12, waiting for transfers between devices, z_shift(): lax.ppermute(x, 'col', [(i, (i + 2 * s) % N_AX) for i in range(N_AX)])  3.73 us
    ppermute x1, starting transfers between devices, local(): send = lax.ppermute(send, 'row', SWAP)  3.24 us
    unnamed x20, local copies, waits for them, and re-layouts  2.43 us
  transfers between devices with their start and end apart: 21, of which 9 were waited for; matrix products, arithmetic and copies ran while one was open for 1% of the time, Pallas kernels for 1%

profile of v6, /device:TPU:1, one launch (start us, length us, event | category | flops | bytes accessed | tf_op | source)
XLA Modules:
  0.0 115.6 jit_solution(11438408654167143517)
XLA Ops:
  0.6 0.0 copy-start.6
  0.7 1.7 %broadcast_in_dim.2 = bf16[8,256,128]{2,1,0:T(8,128)(2,1)} broadcast(bf16[256,128]{1,0:T(8,128)(2,1)} %refs_7_.1), dimensions={1,2} | broadcast | bytes 589824 | tf_op jit(solution)/shard_map/broadcast_in_dim | solution.py:264
  2.4 7.5 %all-to-all-start = ((bf16[8,256,128]{2,1,0:T(8,128)(2,1)}), bf16[8,256,128]{2,1,0:T(8,128)(2,1)S(1)}, u32[]{:S(2)}, u32[]{:S(2)}) async-start(bf16[8,256,128]{2,1,0:T(8,128)(2,1)} %broadcast_in_dim.2), calls=%async_computation | async-start | bytes 1048576 | tf_op jit(solution)/shard_map/all_to_all | solution.py:240
  10.5 0.0 copy-start
  10.5 1.7 %copy-done = bf16[1,1,80,128,128]{4,3,2,1,0:T(8,128)(2,1)S(1)} copy-done((bf16[1,1,80,128,128]{4,3,2,1,0:T(8,128)(2,1)S(1)}, bf16[1,1,80,128,128]{4,3,2,1,0:T(8,128)(2,1)}, u32[]{:S(2)}) %copy-start) | copy-done | bytes 2621464
  12.2 0.7 copy-done.5
  12.9 1.5 %shard_map.103.deg_ref = f32[16,8,128]{2,1,0:T(8,128)S(1)} custom-call(s32[1,1]{1,0:T(1,128)S(6)} %copy.13.count_ref, s32[1,80]{1,0:T(1,128)S(1)} %bitcast.11, bf16[80,128,128]{2,1,0:T(8,128)(2,1)S(1)} %bitcast.8), custom_call_target="tpu_custom_call" | custom-call | flops 20971520 | bytes 2621440 | tf_op jit(solution)/shard_map/pallas_call | solution.py:265
  14.4 5.7 %all-to-all-done.mine_ref = bf16[8,256,128]{2,1,0:T(8,128)(2,1)S(1)} async-done(((bf16[8,256,128]{2,1,0:T(8,128)(2,1)}), bf16[8,256,128]{2,1,0:T(8,128)(2,1)S(1)}, u32[]{:S(2)}, u32[]{:S(2)}) %all-to-all-start) | async-done | bytes 524320 | tf_op jit(solution)/shard_map/all_to_all | solution.py:240
  20.0 1.6 %collective-permute-start = (bf16[8,256,128]{2,1,0:T(8,128)(2,1)S(1)}, bf16[8,256,128]{2,1,0:T(8,128)(2,1)}, u32[]{:S(2)}, u32[]{:S(2)}) collective-permute-start(bf16[8,256,128]{2,1,0:T(8,128)(2,1)S(1)} %all-to-all-done.mine_ref), channel_id=1, source_target_pairs={{0,16},{16,0},{32,48},{48,32},{64,80},{80,64},{96,112},{112,96},{1... | collective-permute-start | bytes 1572872 | tf_op jit(solution)/shard_map/ppermute | solution.py:273
  21.7 0.1 pad_add_fusion.place_ref
  21.8 1.6 %collective-permute-done.other_ref = bf16[8,256,128]{2,1,0:T(8,128)(2,1)} collective-permute-done((bf16[8,256,128]{2,1,0:T(8,128)(2,1)S(1)}, bf16[8,256,128]{2,1,0:T(8,128)(2,1)}, u32[]{:S(2)}, u32[]{:S(2)}) %collective-permute-start) | collective-permute-done | bytes 524320 | tf_op jit(solution)/shard_map/ppermute | solution.py:273
  23.4 0.0 copy-done.6
  23.4 0.0 copy-start.3
  23.4 0.0 copy-start.8
  23.4 0.0 copy-start.9
  23.4 2.2 %shard_map.104 = (f32[5,256,128]{2,1,0:T(8,128)S(1)}, f32[3,256,128]{2,1,0:T(8,128)S(1)}, f32[5,8,128]{2,1,0:T(8,128)S(1)}, f32[3,8,128]{2,1,0:T(8,128)S(1)}, bf...) custom-call(s32[3]{0:T(128)S(1)} %pad_add_fusion.place_ref, s32[1,1]{1,0:T(1,128)S(6)} %copy.13.count_ref, ...), custom_call_target="tpu_custom_call" | custom-call | flops 335544320 | bytes 5242880 | tf_op jit(solution)/shard_map/pallas_call | solution.py:275
  25.6 0.5 collective-permute-start.1
  26.1 5.9 %collective-permute-done.1.after_ref.got_ref = bf16[3,272,128]{2,1,0:T(8,128)(2,1)S(1)} collective-permute-done((bf16[3,272,128]{2,1,0:T(8,128)(2,1)S(1)}, bf16[3,272,128]{2,1,0:T(8,128)(2,1)S(1)}, u32[]{:S(2)}, u32[]{:S(2)}) %collective-permute-start.1) | collective-permute-done | bytes 208928 | tf_op jit(solution)/shard_map/ppermute | solution.py:291
  32.1 0.4 collective-permute-start.2
  32.5 0.1 shard_map.107
  32.5 6.7 %collective-permute-start.3 = (bf16[272,128]{1,0:T(8,128)(2,1)S(1)}, bf16[272,128]{1,0:T(8,128)(2,1)S(1)}, u32[]{:S(2)}, u32[]{:S(2)}) collective-permute-start(bf16[272,128]{1,0:T(8,128)(2,1)S(1)} %get-tuple-element.35), channel_id=1, source_target_pairs={{0,8},{1,9},{2,10},{3,11},{4,12},{5,13},{6,14},{7,15},{8,0},{9,1},... | collective-permute-start | bytes 208904 | tf_op jit(solution)/shard_map/ppermute | solution.py:248
  39.2 0.8 collective-permute-start.4
  40.0 3.7 %collective-permute-start.5 = (bf16[272,128]{1,0:T(8,128)(2,1)S(1)}, bf16[272,128]{1,0:T(8,128)(2,1)S(1)}, u32[]{:S(2)}, u32[]{:S(2)}) collective-permute-start(bf16[272,128]{1,0:T(8,128)(2,1)S(1)} %get-tuple-element.37), channel_id=1, source_target_pairs={{0,10},{1,11},{2,12},{3,13},{4,14},{5,15},{6,0},{7,1},{8,2},{9,3},... | collective-permute-start | bytes 208904 | tf_op jit(solution)/shard_map/ppermute | solution.py:248
  43.7 0.0 collective-permute-done.2.got_ref
  43.7 0.1 shard_map.106
  43.7 1.9 %collective-permute-start.6 = (bf16[272,128]{1,0:T(8,128)(2,1)S(1)}, bf16[272,128]{1,0:T(8,128)(2,1)S(1)}, u32[]{:S(2)}, u32[]{:S(2)}) collective-permute-start(bf16[272,128]{1,0:T(8,128)(2,1)S(1)} %get-tuple-element.38), channel_id=1, source_target_pairs={{0,4},{1,5},{2,6},{3,7},{4,8},{5,9},{6,10},{7,11},{8,12},{9,13},{1... | collective-permute-start | bytes 208904 | tf_op jit(solution)/shard_map/ppermute | solution.py:248
  45.6 1.8 %collective-permute-start.7 = (bf16[272,128]{1,0:T(8,128)(2,1)S(1)}, bf16[272,128]{1,0:T(8,128)(2,1)S(1)}, u32[]{:S(2)}, u32[]{:S(2)}) collective-permute-start(bf16[272,128]{1,0:T(8,128)(2,1)S(1)} %get-tuple-element.39), channel_id=1, source_target_pairs={{0,12},{1,13},{2,14},{3,15},{4,0},{5,1},{6,2},{7,3},{8,4},{9,5},{1... | collective-permute-start | bytes 208904 | tf_op jit(solution)/shard_map/ppermute | solution.py:248
  47.4 0.0 collective-permute-done.3.refs_0_
  47.4 0.4 collective-permute-start.8
  47.8 0.0 collective-permute-done.4.refs_1_
  47.8 2.3 %collective-permute-start.9 = (bf16[272,128]{1,0:T(8,128)(2,1)S(1)}, bf16[272,128]{1,0:T(8,128)(2,1)S(1)}, u32[]{:S(2)}, u32[]{:S(2)}) collective-permute-start(bf16[272,128]{1,0:T(8,128)(2,1)S(1)} %get-tuple-element.41), channel_id=1, source_target_pairs={{0,14},{1,15},{2,0},{3,1},{4,2},{5,3},{6,4},{7,5},{8,6},{9,7},{10,... | collective-permute-start | bytes 208904 | tf_op jit(solution)/shard_map/ppermute | solution.py:248
  50.1 0.0 collective-permute-done.5.refs_2_
  50.1 0.0 collective-permute-done.6.refs_3_
  50.1 2.7 %collective-permute-done.7.refs_4_ = bf16[272,128]{1,0:T(8,128)(2,1)S(1)} collective-permute-done((bf16[272,128]{1,0:T(8,128)(2,1)S(1)}, bf16[272,128]{1,0:T(8,128)(2,1)S(1)}, u32[]{:S(2)}, u32[]{:S(2)}) %collective-permute-start.7) | collective-permute-done | bytes 69664 | tf_op jit(solution)/shard_map/ppermute | solution.py:248
  52.8 0.6 collective-permute-done.8.refs_5_
  53.4 0.0 collective-permute-done.9.refs_6_
  53.4 1.3 %shard_map.108 = (bf16[256,128]{1,0:T(8,128)(2,1)}, bf16[16,64,128]{2,1,0:T(8,128)(2,1)}, bf16[256,256]{1,0:T(8,128)(2,1)S(1)}) custom-call(f32[256,128]{1,0:T(8,128)S(1)} %get-tuple-element.31.own_ref, f32[8,128]{1,0:T(8,128)S(1)} %get-tuple-element.32.own_deg_ref, bf16[272,128]{1,0:T(8,128)(2,1)S(1)} %collective-permute-done.3.refs_0_, ...), custom_call_target="tpu_custom_call" | custom-call | flops 335544320 | bytes 1310720 | tf_op jit(solution)/shard_map/pallas_call | solution.py:304
  54.7 2.8 %collective-permute-start.10 = (bf16[256,128]{1,0:T(8,128)(2,1)}, bf16[256,128]{1,0:T(8,128)(2,1)S(1)}, u32[]{:S(2)}, u32[]{:S(2)}) collective-permute-start(bf16[256,128]{1,0:T(8,128)(2,1)} %get-tuple-element.42), channel_id=1, source_target_pairs={{0,8},{1,9},{2,10},{3,11},{4,12},{5,13},{6,14},{7,15},{8,0},{9,1},... | collective-permute-start | bytes 196616 | tf_op jit(solution)/shard_map/ppermute | solution.py:248
  57.5 7.9 %all-to-all-start.1 = ((bf16[16,64,128]{2,1,0:T(8,128)(2,1)}), bf16[16,64,128]{2,1,0:T(8,128)(2,1)S(1)}, u32[]{:S(2)}, u32[]{:S(2)}) async-start(bf16[16,64,128]{2,1,0:T(8,128)(2,1)} %get-tuple-element.43), calls=%async_computation.1 | async-start | bytes 524288 | tf_op jit(solution)/shard_map/all_to_all | solution.py:240
  65.4 0.0 collective-permute-done.10
  65.4 0.9 pad_maximum_fusion.refs_0_
  66.3 0.5 collective-permute-start.11
  66.7 2.7 %collective-permute-start.12 = (bf16[2,256,128]{2,1,0:T(8,128)(2,1)S(1)}, bf16[2,256,128]{2,1,0:T(8,128)(2,1)S(1)}, u32[]{:S(2)}, u32[]{:S(2)}) collective-permute-start(bf16[2,256,128]{2,1,0:T(8,128)(2,1)S(1)} %pad_maximum_fusion.refs_0_), channel_id=1, source_target_pairs={{0,14},{1,15},{2,0},{3,1},{4,2},{5,3},{6,4},{7,5},{8,6},{9,7},{10,... | collective-permute-start | bytes 393224 | tf_op jit(solution)/shard_map/ppermute | solution.py:248
  69.4 0.3 collective-permute-start.13
  69.7 3.2 %collective-permute-start.14 = (bf16[256,128]{1,0:T(8,128)(2,1)}, bf16[256,128]{1,0:T(8,128)(2,1)S(1)}, u32[]{:S(2)}, u32[]{:S(2)}) collective-permute-start(bf16[256,128]{1,0:T(8,128)(2,1)} %get-tuple-element.42), channel_id=1, source_target_pairs={{0,12},{1,13},{2,14},{3,15},{4,0},{5,1},{6,2},{7,3},{8,4},{9,5},{1... | collective-permute-start | bytes 196616 | tf_op jit(solution)/shard_map/ppermute | solution.py:248
  73.0 1.3 %all-to-all-done.1.got_ref = bf16[16,64,128]{2,1,0:T(8,128)(2,1)S(1)} async-done(((bf16[16,64,128]{2,1,0:T(8,128)(2,1)}), bf16[16,64,128]{2,1,0:T(8,128)(2,1)S(1)}, u32[]{:S(2)}, u32[]{:S(2)}) %all-to-all-start.1) | async-done | bytes 262176 | tf_op jit(solution)/shard_map/all_to_all | solution.py:240
  74.4 0.9 collective-permute-start.15
  75.3 0.4 collective-permute-done.13.refs_3_
  75.7 0.0 collective-permute-done.14.refs_4_
  75.7 0.0 collective-permute-done.11.refs_1_
  75.7 0.0 collective-permute-done.12.refs_2_
  75.7 1.6 %collective-permute-done.15.refs_5_.other_ref = bf16[64,128]{1,0:T(8,128)(2,1)S(1)} collective-permute-done((bf16[64,128]{1,0:T(8,128)(2,1)S(1)}, bf16[64,128]{1,0:T(8,128)(2,1)S(1)}, u32[]{:S(2)}, u32[]{:S(2)}) %collective-permute-start.15) | collective-permute-done | bytes 16416 | tf_op jit(solution)/shard_map/ppermute | solution.py:315
  77.4 0.9 collective-permute-start.16
  78.3 11.8 %all_to_all.20.got_ref = bf16[8,64,128]{2,1,0:T(8,128)(2,1)S(1)} all-to-all(bf16[8,64,128]{2,1,0:T(8,128)(2,1)S(1)} %shard_map.111), channel_id=1, replica_groups={{0,2,4,6,8,10,12,14},{1,3,5,7,9,11,13,15},{16,18,20,22,24,26,28,30},{17..., dimensions={0} | all-to-all | bytes 262144 | tf_op jit(solution)/shard_map/all_to_all | solution.py:240
  90.1 0.0 collective-permute-done.16.other_ref
  90.1 1.6 %shard_map.113 = (f32[8,256,128]{2,1,0:T(8,128)S(1)}, bf16[8,256,128]{2,1,0:T(8,128)(2,1)S(1)}) custom-call(s32[3]{0:T(128)S(1)} %pad_add_fusion.place_ref, s32[1,1]{1,0:T(1,128)S(6)} %copy.13.count_ref, s32[1,80]{1,0:T(1,128)S(1)} %bitcast.13, s32[1,80]{1,0:T(1,128)S(1)} %bitcast.15, bf16[80,128,128]{2,1,0:T(8,128)(2,1)S(1)} %bitcast.10, ...), custom_call_target="tpu_custom_call" | custom-call | flops 335544320 | bytes 5242880 | tf_op jit(solution)/shard_map/pallas_call | solution.py:327
  91.7 0.0 copy-start.4
  91.7 3.2 %collective-permute-start.17 = (bf16[8,256,128]{2,1,0:T(8,128)(2,1)S(1)}, bf16[8,256,128]{2,1,0:T(8,128)(2,1)S(1)}, u32[]{:S(2)}, u32[]{:S(2)}) collective-permute-start(bf16[8,256,128]{2,1,0:T(8,128)(2,1)S(1)} %get-tuple-element.45), channel_id=1, source_target_pairs={{0,16},{16,0},{32,48},{48,32},{64,80},{80,64},{96,112},{112,96},{1... | collective-permute-start | bytes 1572872 | tf_op jit(solution)/shard_map/ppermute | solution.py:336
  95.0 0.1 collective-permute-start.18
  95.1 1.4 %collective-permute-done.18.piece2_ref = bf16[32,128]{1,0:T(8,128)(2,1)S(1)} collective-permute-done((bf16[32,128]{1,0:T(8,128)(2,1)S(1)}, bf16[32,128]{1,0:T(8,128)(2,1)S(1)}, u32[]{:S(2)}, u32[]{:S(2)}) %collective-permute-start.18) | collective-permute-done | bytes 8224 | tf_op jit(solution)/shard_map/ppermute | solution.py:325
  96.5 0.0 collective-permute-done.17.got_ref
  96.5 0.6 shard_map.114
  97.2 17.6 %all_to_all.21.got_ref = bf16[8,320,128]{2,1,0:T(8,128)(2,1)S(1)} all-to-all(bf16[8,320,128]{2,1,0:T(8,128)(2,1)S(1)} %shard_map.114), channel_id=1, replica_groups={{0,32,64,96,128,160,192,224},{16,48,80,112,144,176,208,240},{1,33,65,97..., dimensions={0} | all-to-all | bytes 1310720 | tf_op jit(solution)/shard_map/all_to_all | solution.py:240
  114.8 0.9 shard_map.115
  (16 shorter events, 0.1 us)
Async XLA Ops:
  0.6 22.7 %copy-start.6 = (s32[1,1,80]{2,1,0:T(1,128)S(1)}, s32[1,1,80]{2,1,0:T(1,128)}, u32[]{:S(2)}) copy-start(s32[1,1,80]{2,1,0:T(1,128)} %param.13) | copy-start | bytes 964
  0.6 22.7 %copy-start.7 = (s32[1,1,80]{2,1,0:T(1,128)S(1)}, s32[1,1,80]{2,1,0:T(1,128)}, u32[]{:S(2)}) copy-start(s32[1,1,80]{2,1,0:T(1,128)} %param.14) | copy-start | bytes 964
  2.4 17.7 %all-to-all-start = ((bf16[8,256,128]{2,1,0:T(8,128)(2,1)}), bf16[8,256,128]{2,1,0:T(8,128)(2,1)S(1)}, u32[]{:S(2)}, u32[]{:S(2)}) async-start(bf16[8,256,128]{2,1,0:T(8,128)(2,1)} %broadcast_in_dim.2), calls=%async_computation | async-start | bytes 1048576 | tf_op jit(solution)/shard_map/all_to_all | solution.py:240
  10.5 1.7 %copy-start = (bf16[1,1,80,128,128]{4,3,2,1,0:T(8,128)(2,1)S(1)}, bf16[1,1,80,128,128]{4,3,2,1,0:T(8,128)(2,1)}, u32[]{:S(2)}) copy-start(bf16[1,1,80,128,128]{4,3,2,1,0:T(8,128)(2,1)} %param.12) | copy-start | bytes 7864324
  12.2 0.7 copy-start.5
  12.9 10.5 %copy-start.1 = (bf16[1,1,80,128,128]{4,3,2,1,0:T(8,128)(2,1)S(1)}, bf16[1,1,80,128,128]{4,3,2,1,0:T(8,128)(2,1)}, u32[]{:S(2)}) copy-start(bf16[1,1,80,128,128]{4,3,2,1,0:T(8,128)(2,1)} %param.12) | copy-start | bytes 7864324
  20.0 3.3 %collective-permute-start = (bf16[8,256,128]{2,1,0:T(8,128)(2,1)S(1)}, bf16[8,256,128]{2,1,0:T(8,128)(2,1)}, u32[]{:S(2)}, u32[]{:S(2)}) collective-permute-start(bf16[8,256,128]{2,1,0:T(8,128)(2,1)S(1)} %all-to-all-done.mine_ref), channel_id=1, source_target_pairs={{0,16},{16,0},{32,48},{48,32},{64,80},{80,64},{96,112},{112,96},{1... | collective-permute-start | bytes 1572872 | tf_op jit(solution)/shard_map/ppermute | solution.py:273
  23.4 30.0 %copy-start.2 = (bf16[256,128]{1,0:T(8,128)(2,1)S(1)}, bf16[256,128]{1,0:T(8,128)(2,1)}, u32[]{:S(2)}) copy-start(bf16[256,128]{1,0:T(8,128)(2,1)} %refs_7_.1) | copy-start | bytes 196612
  23.4 30.0 %copy-start.3 = (bf16[128,256]{1,0:T(8,128)(2,1)S(1)}, bf16[128,256]{1,0:T(8,128)(2,1)}, u32[]{:S(2)}) copy-start(bf16[128,256]{1,0:T(8,128)(2,1)} %ws_ref.1) | copy-start | bytes 196612
  23.4 30.0 %copy-start.8 = (bf16[256,256]{1,0:T(8,128)(2,1)S(1)}, bf16[256,256]{1,0:T(8,128)(2,1)}, u32[]{:S(2)}) copy-start(bf16[256,256]{1,0:T(8,128)(2,1)} %refs_8_.1) | copy-start | bytes 393220
  23.4 30.0 %copy-start.9 = (bf16[128,256]{1,0:T(8,128)(2,1)S(1)}, bf16[128,256]{1,0:T(8,128)(2,1)}, u32[]{:S(2)}) copy-start(bf16[128,256]{1,0:T(8,128)(2,1)} %refs_10_.1) | copy-start | bytes 196612
  25.6 6.4 %collective-permute-start.1 = (bf16[3,272,128]{2,1,0:T(8,128)(2,1)S(1)}, bf16[3,272,128]{2,1,0:T(8,128)(2,1)S(1)}, u32[]{:S(2)}, u32[]{:S(2)}) collective-permute-start(bf16[3,272,128]{2,1,0:T(8,128)(2,1)S(1)} %get-tuple-element.30), channel_id=1, source_target_pairs={{0,1},{1,0},{2,3},{3,2},{4,5},{5,4},{6,7},{7,6},{8,9},{9,8},{10,11... | collective-permute-start | bytes 626696 | tf_op jit(solution)/shard_map/ppermute | solution.py:291
  32.1 11.6 %collective-permute-start.2 = (bf16[5,272,128]{2,1,0:T(8,128)(2,1)S(1)}, bf16[5,272,128]{2,1,0:T(8,128)(2,1)S(1)}, u32[]{:S(2)}, u32[]{:S(2)}) collective-permute-start(bf16[5,272,128]{2,1,0:T(8,128)(2,1)S(1)} %shard_map.105), channel_id=1, source_target_pairs={{0,1},{1,0},{2,3},{3,2},{4,5},{5,4},{6,7},{7,6},{8,9},{9,8},{10,11... | collective-permute-start | bytes 1044488 | tf_op jit(solution)/shard_map/ppermute | solution.py:295
  32.5 14.9 %collective-permute-start.3 = (bf16[272,128]{1,0:T(8,128)(2,1)S(1)}, bf16[272,128]{1,0:T(8,128)(2,1)S(1)}, u32[]{:S(2)}, u32[]{:S(2)}) collective-permute-start(bf16[272,128]{1,0:T(8,128)(2,1)S(1)} %get-tuple-element.35), channel_id=1, source_target_pairs={{0,8},{1,9},{2,10},{3,11},{4,12},{5,13},{6,14},{7,15},{8,0},{9,1},... | collective-permute-start | bytes 208904 | tf_op jit(solution)/shard_map/ppermute | solution.py:248
  39.2 8.6 %collective-permute-start.4 = (bf16[272,128]{1,0:T(8,128)(2,1)S(1)}, bf16[272,128]{1,0:T(8,128)(2,1)S(1)}, u32[]{:S(2)}, u32[]{:S(2)}) collective-permute-start(bf16[272,128]{1,0:T(8,128)(2,1)S(1)} %get-tuple-element.36), channel_id=1, source_target_pairs={{0,6},{1,7},{2,8},{3,9},{4,10},{5,11},{6,12},{7,13},{8,14},{9,15},... | collective-permute-start | bytes 208904 | tf_op jit(solution)/shard_map/ppermute | solution.py:248
  40.0 10.1 %collective-permute-start.5 = (bf16[272,128]{1,0:T(8,128)(2,1)S(1)}, bf16[272,128]{1,0:T(8,128)(2,1)S(1)}, u32[]{:S(2)}, u32[]{:S(2)}) collective-permute-start(bf16[272,128]{1,0:T(8,128)(2,1)S(1)} %get-tuple-element.37), channel_id=1, source_target_pairs={{0,10},{1,11},{2,12},{3,13},{4,14},{5,15},{6,0},{7,1},{8,2},{9,3},... | collective-permute-start | bytes 208904 | tf_op jit(solution)/shard_map/ppermute | solution.py:248
  43.7 6.3 %collective-permute-start.6 = (bf16[272,128]{1,0:T(8,128)(2,1)S(1)}, bf16[272,128]{1,0:T(8,128)(2,1)S(1)}, u32[]{:S(2)}, u32[]{:S(2)}) collective-permute-start(bf16[272,128]{1,0:T(8,128)(2,1)S(1)} %get-tuple-element.38), channel_id=1, source_target_pairs={{0,4},{1,5},{2,6},{3,7},{4,8},{5,9},{6,10},{7,11},{8,12},{9,13},{1... | collective-permute-start | bytes 208904 | tf_op jit(solution)/shard_map/ppermute | solution.py:248
  45.6 7.2 %collective-permute-start.7 = (bf16[272,128]{1,0:T(8,128)(2,1)S(1)}, bf16[272,128]{1,0:T(8,128)(2,1)S(1)}, u32[]{:S(2)}, u32[]{:S(2)}) collective-permute-start(bf16[272,128]{1,0:T(8,128)(2,1)S(1)} %get-tuple-element.39), channel_id=1, source_target_pairs={{0,12},{1,13},{2,14},{3,15},{4,0},{5,1},{6,2},{7,3},{8,4},{9,5},{1... | collective-permute-start | bytes 208904 | tf_op jit(solution)/shard_map/ppermute | solution.py:248
  47.4 6.0 %collective-permute-start.8 = (bf16[272,128]{1,0:T(8,128)(2,1)S(1)}, bf16[272,128]{1,0:T(8,128)(2,1)S(1)}, u32[]{:S(2)}, u32[]{:S(2)}) collective-permute-start(bf16[272,128]{1,0:T(8,128)(2,1)S(1)} %get-tuple-element.40), channel_id=1, source_target_pairs={{0,2},{1,3},{2,4},{3,5},{4,6},{5,7},{6,8},{7,9},{8,10},{9,11},{10,... | collective-permute-start | bytes 208904 | tf_op jit(solution)/shard_map/ppermute | solution.py:248
  47.8 5.6 %collective-permute-start.9 = (bf16[272,128]{1,0:T(8,128)(2,1)S(1)}, bf16[272,128]{1,0:T(8,128)(2,1)S(1)}, u32[]{:S(2)}, u32[]{:S(2)}) collective-permute-start(bf16[272,128]{1,0:T(8,128)(2,1)S(1)} %get-tuple-element.41), channel_id=1, source_target_pairs={{0,14},{1,15},{2,0},{3,1},{4,2},{5,3},{6,4},{7,5},{8,6},{9,7},{10,... | collective-permute-start | bytes 208904 | tf_op jit(solution)/shard_map/ppermute | solution.py:248
  54.7 10.7 %collective-permute-start.10 = (bf16[256,128]{1,0:T(8,128)(2,1)}, bf16[256,128]{1,0:T(8,128)(2,1)S(1)}, u32[]{:S(2)}, u32[]{:S(2)}) collective-permute-start(bf16[256,128]{1,0:T(8,128)(2,1)} %get-tuple-element.42), channel_id=1, source_target_pairs={{0,8},{1,9},{2,10},{3,11},{4,12},{5,13},{6,14},{7,15},{8,0},{9,1},... | collective-permute-start | bytes 196616 | tf_op jit(solution)/shard_map/ppermute | solution.py:248
  57.5 16.8 %all-to-all-start.1 = ((bf16[16,64,128]{2,1,0:T(8,128)(2,1)}), bf16[16,64,128]{2,1,0:T(8,128)(2,1)S(1)}, u32[]{:S(2)}, u32[]{:S(2)}) async-start(bf16[16,64,128]{2,1,0:T(8,128)(2,1)} %get-tuple-element.43), calls=%async_computation.1 | async-start | bytes 524288 | tf_op jit(solution)/shard_map/all_to_all | solution.py:240
  66.3 9.4 %collective-permute-start.11 = (bf16[2,256,128]{2,1,0:T(8,128)(2,1)S(1)}, bf16[2,256,128]{2,1,0:T(8,128)(2,1)S(1)}, u32[]{:S(2)}, u32[]{:S(2)}) collective-permute-start(bf16[2,256,128]{2,1,0:T(8,128)(2,1)S(1)} %pad_maximum_fusion.refs_0_), channel_id=1, source_target_pairs={{0,2},{1,3},{2,4},{3,5},{4,6},{5,7},{6,8},{7,9},{8,10},{9,11},{10,... | collective-permute-start | bytes 393224 | tf_op jit(solution)/shard_map/ppermute | solution.py:248
  66.7 9.0 %collective-permute-start.12 = (bf16[2,256,128]{2,1,0:T(8,128)(2,1)S(1)}, bf16[2,256,128]{2,1,0:T(8,128)(2,1)S(1)}, u32[]{:S(2)}, u32[]{:S(2)}) collective-permute-start(bf16[2,256,128]{2,1,0:T(8,128)(2,1)S(1)} %pad_maximum_fusion.refs_0_), channel_id=1, source_target_pairs={{0,14},{1,15},{2,0},{3,1},{4,2},{5,3},{6,4},{7,5},{8,6},{9,7},{10,... | collective-permute-start | bytes 393224 | tf_op jit(solution)/shard_map/ppermute | solution.py:248
  69.4 6.3 %collective-permute-start.13 = (bf16[256,128]{1,0:T(8,128)(2,1)}, bf16[256,128]{1,0:T(8,128)(2,1)S(1)}, u32[]{:S(2)}, u32[]{:S(2)}) collective-permute-start(bf16[256,128]{1,0:T(8,128)(2,1)} %get-tuple-element.42), channel_id=1, source_target_pairs={{0,4},{1,5},{2,6},{3,7},{4,8},{5,9},{6,10},{7,11},{8,12},{9,13},{1... | collective-permute-start | bytes 196616 | tf_op jit(solution)/shard_map/ppermute | solution.py:248
  69.7 6.0 %collective-permute-start.14 = (bf16[256,128]{1,0:T(8,128)(2,1)}, bf16[256,128]{1,0:T(8,128)(2,1)S(1)}, u32[]{:S(2)}, u32[]{:S(2)}) collective-permute-start(bf16[256,128]{1,0:T(8,128)(2,1)} %get-tuple-element.42), channel_id=1, source_target_pairs={{0,12},{1,13},{2,14},{3,15},{4,0},{5,1},{6,2},{7,3},{8,4},{9,5},{1... | collective-permute-start | bytes 196616 | tf_op jit(solution)/shard_map/ppermute | solution.py:248
  74.4 3.0 %collective-permute-start.15 = (bf16[64,128]{1,0:T(8,128)(2,1)S(1)}, bf16[64,128]{1,0:T(8,128)(2,1)S(1)}, u32[]{:S(2)}, u32[]{:S(2)}) collective-permute-start(bf16[64,128]{1,0:T(8,128)(2,1)S(1)} %shard_map.109.mine_ref), channel_id=1, source_target_pairs={{0,1},{1,0},{2,3},{3,2},{4,5},{5,4},{6,7},{7,6},{8,9},{9,8},{10,11... | collective-permute-start | bytes 49160 | tf_op jit(solution)/shard_map/ppermute | solution.py:315
  77.4 12.7 %collective-permute-start.16 = (bf16[8,256,128]{2,1,0:T(8,128)(2,1)S(1)}, bf16[8,256,128]{2,1,0:T(8,128)(2,1)S(1)}, u32[]{:S(2)}, u32[]{:S(2)}) collective-permute-start(bf16[8,256,128]{2,1,0:T(8,128)(2,1)S(1)} %shard_map.110.after_ref.mine_ref), channel_id=1, source_target_pairs={{0,1},{1,0},{2,3},{3,2},{4,5},{5,4},{6,7},{7,6},{8,9},{9,8},{10,11... | collective-permute-start | bytes 1572872 | tf_op jit(solution)/shard_map/ppermute | solution.py:319
  91.7 23.0 %copy-start.4 = (bf16[128,256]{1,0:T(8,128)(2,1)S(1)}, bf16[128,256]{1,0:T(8,128)(2,1)}, u32[]{:S(2)}) copy-start(bf16[128,256]{1,0:T(8,128)(2,1)} %ws_ref.1) | copy-start | bytes 196612
  91.7 4.8 %collective-permute-start.17 = (bf16[8,256,128]{2,1,0:T(8,128)(2,1)S(1)}, bf16[8,256,128]{2,1,0:T(8,128)(2,1)S(1)}, u32[]{:S(2)}, u32[]{:S(2)}) collective-permute-start(bf16[8,256,128]{2,1,0:T(8,128)(2,1)S(1)} %get-tuple-element.45), channel_id=1, source_target_pairs={{0,16},{16,0},{32,48},{48,32},{64,80},{80,64},{96,112},{112,96},{1... | collective-permute-start | bytes 1572872 | tf_op jit(solution)/shard_map/ppermute | solution.py:336
  95.0 1.5 %collective-permute-start.18 = (bf16[32,128]{1,0:T(8,128)(2,1)S(1)}, bf16[32,128]{1,0:T(8,128)(2,1)S(1)}, u32[]{:S(2)}, u32[]{:S(2)}) collective-permute-start(bf16[32,128]{1,0:T(8,128)(2,1)S(1)} %shard_map.112.after_ref.piece_ref), channel_id=1, source_target_pairs={{0,16},{16,0},{32,48},{48,32},{64,80},{80,64},{96,112},{112,96},{1... | collective-permute-start | bytes 24584 | tf_op jit(solution)/shard_map/ppermute | solution.py:325

commit v7 on v6

--- a/solution.py
+++ b/solution.py
@@ -11,7 +11,7 @@
 N_AX = 16
 BPD = 2
 STRIPE = N_AX * BPD
-UNROLL = 20
+UNROLL = 40
 PIECE = 32
 TAIL = 16
 HALF = N_AX // 2

time: 116 us -> 116 us (level)
  starting transfers between devices: 50.1 us -> 46.3 us
  waiting for transfers between devices: 21.3 us -> 22.9 us
  Pallas kernels: 8.33 us -> 9.82 us
  transfers between devices with their start and end apart: 21 -> 21, of which waited for: 9 -> 10; matrix products, arithmetic and copies ran while one was open for 1% -> 1% of each run, Pallas kernels for 1% -> 2%
where the time goes in v7:
time: 116 us; the launch traced here: 115 us
  starting transfers between devices  46.3 us (40%)
  blocking collectives  29.4 us (25%)
  waiting for transfers between devices  22.9 us (20%)
  Pallas kernels  9.82 us (8%)
  local copies, waits for them, and re-layouts  4.14 us (4%)
  between operations  1.45 us (1%)
    all_to_all x2, blocking collectives, exchange(): return lax.all_to_all(x, axis, 0, 0, axis_index_groups=groups)  29.4 us
    ppermute x12, starting transfers between devices, z_shift(): lax.ppermute(x, 'col', [(i, (i + 2 * s) % N_AX) for i in range(N_AX)])  25.9 us
    all_to_all x2, starting transfers between devices, exchange(): return lax.all_to_all(x, axis, 0, 0, axis_index_groups=groups)  15 us
    ppermute x1, waiting for transfers between devices, local(): far_got = lax.ppermute(far_send, 'col', SWAP)  6.89 us
    all_to_all x2, waiting for transfers between devices, exchange(): return lax.all_to_all(x, axis, 0, 0, axis_index_groups=groups)  6.69 us
    ppermute x12, waiting for transfers between devices, z_shift(): lax.ppermute(x, 'col', [(i, (i + 2 * s) % N_AX) for i in range(N_AX)])  4.44 us
    ppermute x1, starting transfers between devices, local(): send = lax.ppermute(send, 'row', SWAP)  2.99 us
    pallas_call x1, Pallas kernels, local(): call(forward_kernel, (shape((near, n, BLK), f32), shape((far, n, BLK), f3...  2.63 us
  transfers between devices with their start and end apart: 21, of which 10 were waited for; matrix products, arithmetic and copies ran while one was open for 1% of the time, Pallas kernels for 2%

profile of v7, /device:TPU:1, one launch (start us, length us, event | category | flops | bytes accessed | tf_op | source)
XLA Modules:
  0.0 114.9 jit_solution(11583020188629293053)
XLA Ops:
  0.6 0.0 copy-start.6
  0.7 1.7 %broadcast_in_dim.2 = bf16[8,256,128]{2,1,0:T(8,128)(2,1)} broadcast(bf16[256,128]{1,0:T(8,128)(2,1)} %refs_7_.1), dimensions={1,2} | broadcast | bytes 589824 | tf_op jit(solution)/shard_map/broadcast_in_dim | solution.py:264
  2.4 7.5 %all-to-all-start = ((bf16[8,256,128]{2,1,0:T(8,128)(2,1)}), bf16[8,256,128]{2,1,0:T(8,128)(2,1)S(1)}, u32[]{:S(2)}, u32[]{:S(2)}) async-start(bf16[8,256,128]{2,1,0:T(8,128)(2,1)} %broadcast_in_dim.2), calls=%async_computation | async-start | bytes 1048576 | tf_op jit(solution)/shard_map/all_to_all | solution.py:240
  10.5 0.0 copy-start
  10.5 1.7 %copy-done = bf16[1,1,80,128,128]{4,3,2,1,0:T(8,128)(2,1)S(1)} copy-done((bf16[1,1,80,128,128]{4,3,2,1,0:T(8,128)(2,1)S(1)}, bf16[1,1,80,128,128]{4,3,2,1,0:T(8,128)(2,1)}, u32[]{:S(2)}) %copy-start) | copy-done | bytes 2621464
  12.2 0.7 copy-done.5
  12.9 2.2 %shard_map.103.deg_ref = f32[16,8,128]{2,1,0:T(8,128)S(1)} custom-call(s32[1,1]{1,0:T(1,128)S(6)} %copy.13.count_ref, s32[1,80]{1,0:T(1,128)S(1)} %bitcast.11, bf16[80,128,128]{2,1,0:T(8,128)(2,1)S(1)} %bitcast.8), custom_call_target="tpu_custom_call" | custom-call | flops 20971520 | bytes 2621440 | tf_op jit(solution)/shard_map/pallas_call | solution.py:265
  15.1 5.0 %all-to-all-done.mine_ref = bf16[8,256,128]{2,1,0:T(8,128)(2,1)S(1)} async-done(((bf16[8,256,128]{2,1,0:T(8,128)(2,1)}), bf16[8,256,128]{2,1,0:T(8,128)(2,1)S(1)}, u32[]{:S(2)}, u32[]{:S(2)}) %all-to-all-start) | async-done | bytes 524320 | tf_op jit(solution)/shard_map/all_to_all | solution.py:240
  20.0 1.6 %collective-permute-start = (bf16[8,256,128]{2,1,0:T(8,128)(2,1)S(1)}, bf16[8,256,128]{2,1,0:T(8,128)(2,1)}, u32[]{:S(2)}, u32[]{:S(2)}) collective-permute-start(bf16[8,256,128]{2,1,0:T(8,128)(2,1)S(1)} %all-to-all-done.mine_ref), channel_id=1, source_target_pairs={{0,16},{16,0},{32,48},{48,32},{64,80},{80,64},{96,112},{112,96},{1... | collective-permute-start | bytes 1572872 | tf_op jit(solution)/shard_map/ppermute | solution.py:273
  21.7 0.1 pad_add_fusion.place_ref
  21.8 1.6 %collective-permute-done.other_ref = bf16[8,256,128]{2,1,0:T(8,128)(2,1)} collective-permute-done((bf16[8,256,128]{2,1,0:T(8,128)(2,1)S(1)}, bf16[8,256,128]{2,1,0:T(8,128)(2,1)}, u32[]{:S(2)}, u32[]{:S(2)}) %collective-permute-start) | collective-permute-done | bytes 524320 | tf_op jit(solution)/shard_map/ppermute | solution.py:273
  23.4 0.0 copy-done.7
  23.4 0.0 copy-start.3
  23.4 0.0 copy-start.8
  23.4 0.0 copy-start.9
  23.4 2.6 %shard_map.104 = (f32[5,256,128]{2,1,0:T(8,128)S(1)}, f32[3,256,128]{2,1,0:T(8,128)S(1)}, f32[5,8,128]{2,1,0:T(8,128)S(1)}, f32[3,8,128]{2,1,0:T(8,128)S(1)}, bf...) custom-call(s32[3]{0:T(128)S(1)} %pad_add_fusion.place_ref, s32[1,1]{1,0:T(1,128)S(6)} %copy.13.count_ref, ...), custom_call_target="tpu_custom_call" | custom-call | flops 335544320 | bytes 5242880 | tf_op jit(solution)/shard_map/pallas_call | solution.py:275
  26.0 0.1 collective-permute-start.1
  26.1 6.9 %collective-permute-done.1.after_ref.got_ref = bf16[3,272,128]{2,1,0:T(8,128)(2,1)S(1)} collective-permute-done((bf16[3,272,128]{2,1,0:T(8,128)(2,1)S(1)}, bf16[3,272,128]{2,1,0:T(8,128)(2,1)S(1)}, u32[]{:S(2)}, u32[]{:S(2)}) %collective-permute-start.1) | collective-permute-done | bytes 208928 | tf_op jit(solution)/shard_map/ppermute | solution.py:291
  33.0 0.0 collective-permute-start.2
  33.0 0.1 shard_map.107
  33.1 5.9 %collective-permute-start.3 = (bf16[272,128]{1,0:T(8,128)(2,1)S(1)}, bf16[272,128]{1,0:T(8,128)(2,1)S(1)}, u32[]{:S(2)}, u32[]{:S(2)}) collective-permute-start(bf16[272,128]{1,0:T(8,128)(2,1)S(1)} %get-tuple-element.35), channel_id=1, source_target_pairs={{0,8},{1,9},{2,10},{3,11},{4,12},{5,13},{6,14},{7,15},{8,0},{9,1},... | collective-permute-start | bytes 208904 | tf_op jit(solution)/shard_map/ppermute | solution.py:248
  39.0 1.6 %collective-permute-start.4 = (bf16[272,128]{1,0:T(8,128)(2,1)S(1)}, bf16[272,128]{1,0:T(8,128)(2,1)S(1)}, u32[]{:S(2)}, u32[]{:S(2)}) collective-permute-start(bf16[272,128]{1,0:T(8,128)(2,1)S(1)} %get-tuple-element.36), channel_id=1, source_target_pairs={{0,6},{1,7},{2,8},{3,9},{4,10},{5,11},{6,12},{7,13},{8,14},{9,15},... | collective-permute-start | bytes 208904 | tf_op jit(solution)/shard_map/ppermute | solution.py:248
  40.6 2.8 %collective-permute-start.5 = (bf16[272,128]{1,0:T(8,128)(2,1)S(1)}, bf16[272,128]{1,0:T(8,128)(2,1)S(1)}, u32[]{:S(2)}, u32[]{:S(2)}) collective-permute-start(bf16[272,128]{1,0:T(8,128)(2,1)S(1)} %get-tuple-element.37), channel_id=1, source_target_pairs={{0,10},{1,11},{2,12},{3,13},{4,14},{5,15},{6,0},{7,1},{8,2},{9,3},... | collective-permute-start | bytes 208904 | tf_op jit(solution)/shard_map/ppermute | solution.py:248
  43.5 0.0 collective-permute-done.2.got_ref
  43.5 0.1 shard_map.106
  43.6 1.7 %collective-permute-start.6 = (bf16[272,128]{1,0:T(8,128)(2,1)S(1)}, bf16[272,128]{1,0:T(8,128)(2,1)S(1)}, u32[]{:S(2)}, u32[]{:S(2)}) collective-permute-start(bf16[272,128]{1,0:T(8,128)(2,1)S(1)} %get-tuple-element.38), channel_id=1, source_target_pairs={{0,4},{1,5},{2,6},{3,7},{4,8},{5,9},{6,10},{7,11},{8,12},{9,13},{1... | collective-permute-start | bytes 208904 | tf_op jit(solution)/shard_map/ppermute | solution.py:248
  45.2 2.0 %collective-permute-start.7 = (bf16[272,128]{1,0:T(8,128)(2,1)S(1)}, bf16[272,128]{1,0:T(8,128)(2,1)S(1)}, u32[]{:S(2)}, u32[]{:S(2)}) collective-permute-start(bf16[272,128]{1,0:T(8,128)(2,1)S(1)} %get-tuple-element.39), channel_id=1, source_target_pairs={{0,12},{1,13},{2,14},{3,15},{4,0},{5,1},{6,2},{7,3},{8,4},{9,5},{1... | collective-permute-start | bytes 208904 | tf_op jit(solution)/shard_map/ppermute | solution.py:248
  47.2 0.0 collective-permute-done.3.refs_0_
  47.2 0.7 collective-permute-start.8
  47.9 0.0 collective-permute-done.4.refs_1_
  47.9 2.0 %collective-permute-start.9 = (bf16[272,128]{1,0:T(8,128)(2,1)S(1)}, bf16[272,128]{1,0:T(8,128)(2,1)S(1)}, u32[]{:S(2)}, u32[]{:S(2)}) collective-permute-start(bf16[272,128]{1,0:T(8,128)(2,1)S(1)} %get-tuple-element.41), channel_id=1, source_target_pairs={{0,14},{1,15},{2,0},{3,1},{4,2},{5,3},{6,4},{7,5},{8,6},{9,7},{10,... | collective-permute-start | bytes 208904 | tf_op jit(solution)/shard_map/ppermute | solution.py:248
  49.9 0.0 collective-permute-done.5.refs_2_
  49.9 0.0 collective-permute-done.6.refs_3_
  49.9 2.5 %collective-permute-done.7.refs_4_ = bf16[272,128]{1,0:T(8,128)(2,1)S(1)} collective-permute-done((bf16[272,128]{1,0:T(8,128)(2,1)S(1)}, bf16[272,128]{1,0:T(8,128)(2,1)S(1)}, u32[]{:S(2)}, u32[]{:S(2)}) %collective-permute-start.7) | collective-permute-done | bytes 69664 | tf_op jit(solution)/shard_map/ppermute | solution.py:248
  52.4 0.7 collective-permute-done.8.refs_5_
  53.1 0.5 collective-permute-done.9.refs_6_
  53.6 1.3 %shard_map.108 = (bf16[256,128]{1,0:T(8,128)(2,1)}, bf16[16,64,128]{2,1,0:T(8,128)(2,1)}, bf16[256,256]{1,0:T(8,128)(2,1)S(1)}) custom-call(f32[256,128]{1,0:T(8,128)S(1)} %get-tuple-element.31.own_ref, f32[8,128]{1,0:T(8,128)S(1)} %get-tuple-element.32.own_deg_ref, bf16[272,128]{1,0:T(8,128)(2,1)S(1)} %collective-permute-done.3.refs_0_, ...), custom_call_target="tpu_custom_call" | custom-call | flops 335544320 | bytes 1310720 | tf_op jit(solution)/shard_map/pallas_call | solution.py:304
  54.9 2.9 %collective-permute-start.10 = (bf16[256,128]{1,0:T(8,128)(2,1)}, bf16[256,128]{1,0:T(8,128)(2,1)S(1)}, u32[]{:S(2)}, u32[]{:S(2)}) collective-permute-start(bf16[256,128]{1,0:T(8,128)(2,1)} %get-tuple-element.42), channel_id=1, source_target_pairs={{0,8},{1,9},{2,10},{3,11},{4,12},{5,13},{6,14},{7,15},{8,0},{9,1},... | collective-permute-start | bytes 196616 | tf_op jit(solution)/shard_map/ppermute | solution.py:248
  57.8 7.5 %all-to-all-start.1 = ((bf16[16,64,128]{2,1,0:T(8,128)(2,1)}), bf16[16,64,128]{2,1,0:T(8,128)(2,1)S(1)}, u32[]{:S(2)}, u32[]{:S(2)}) async-start(bf16[16,64,128]{2,1,0:T(8,128)(2,1)} %get-tuple-element.43), calls=%async_computation.1 | async-start | bytes 524288 | tf_op jit(solution)/shard_map/all_to_all | solution.py:240
  65.3 0.0 collective-permute-done.10
  65.3 0.9 pad_maximum_fusion.refs_0_
  66.2 1.8 %collective-permute-start.11 = (bf16[2,256,128]{2,1,0:T(8,128)(2,1)S(1)}, bf16[2,256,128]{2,1,0:T(8,128)(2,1)S(1)}, u32[]{:S(2)}, u32[]{:S(2)}) collective-permute-start(bf16[2,256,128]{2,1,0:T(8,128)(2,1)S(1)} %pad_maximum_fusion.refs_0_), channel_id=1, source_target_pairs={{0,2},{1,3},{2,4},{3,5},{4,6},{5,7},{6,8},{7,9},{8,10},{9,11},{10,... | collective-permute-start | bytes 393224 | tf_op jit(solution)/shard_map/ppermute | solution.py:248
  68.0 0.9 collective-permute-start.12
  68.9 0.3 collective-permute-start.13
  69.3 3.2 %collective-permute-start.14 = (bf16[256,128]{1,0:T(8,128)(2,1)}, bf16[256,128]{1,0:T(8,128)(2,1)S(1)}, u32[]{:S(2)}, u32[]{:S(2)}) collective-permute-start(bf16[256,128]{1,0:T(8,128)(2,1)} %get-tuple-element.42), channel_id=1, source_target_pairs={{0,12},{1,13},{2,14},{3,15},{4,0},{5,1},{6,2},{7,3},{8,4},{9,5},{1... | collective-permute-start | bytes 196616 | tf_op jit(solution)/shard_map/ppermute | solution.py:248
  72.5 1.7 %all-to-all-done.1.got_ref = bf16[16,64,128]{2,1,0:T(8,128)(2,1)S(1)} async-done(((bf16[16,64,128]{2,1,0:T(8,128)(2,1)}), bf16[16,64,128]{2,1,0:T(8,128)(2,1)S(1)}, u32[]{:S(2)}, u32[]{:S(2)}) %all-to-all-start.1) | async-done | bytes 262176 | tf_op jit(solution)/shard_map/all_to_all | solution.py:240
  74.3 0.1 collective-permute-start.15
  74.4 0.7 collective-permute-done.13.refs_3_
  75.1 0.0 collective-permute-done.14.refs_4_
  75.1 0.0 collective-permute-done.11.refs_1_
  75.1 0.0 collective-permute-done.12.refs_2_
  75.1 1.8 %collective-permute-done.15.refs_5_.other_ref = bf16[64,128]{1,0:T(8,128)(2,1)S(1)} collective-permute-done((bf16[64,128]{1,0:T(8,128)(2,1)S(1)}, bf16[64,128]{1,0:T(8,128)(2,1)S(1)}, u32[]{:S(2)}, u32[]{:S(2)}) %collective-permute-start.15) | collective-permute-done | bytes 16416 | tf_op jit(solution)/shard_map/ppermute | solution.py:315
  77.0 0.4 collective-permute-start.16
  77.4 11.8 %all_to_all.20.got_ref = bf16[8,64,128]{2,1,0:T(8,128)(2,1)S(1)} all-to-all(bf16[8,64,128]{2,1,0:T(8,128)(2,1)S(1)} %shard_map.111), channel_id=1, replica_groups={{0,2,4,6,8,10,12,14},{1,3,5,7,9,11,13,15},{16,18,20,22,24,26,28,30},{17..., dimensions={0} | all-to-all | bytes 262144 | tf_op jit(solution)/shard_map/all_to_all | solution.py:240
  89.2 0.0 collective-permute-done.16.other_ref
  89.2 2.0 %shard_map.113 = (f32[8,256,128]{2,1,0:T(8,128)S(1)}, bf16[8,256,128]{2,1,0:T(8,128)(2,1)S(1)}) custom-call(s32[3]{0:T(128)S(1)} %pad_add_fusion.place_ref, s32[1,1]{1,0:T(1,128)S(6)} %copy.13.count_ref, s32[1,80]{1,0:T(1,128)S(1)} %bitcast.13, s32[1,80]{1,0:T(1,128)S(1)} %bitcast.15, bf16[80,128,128]{2,1,0:T(8,128)(2,1)S(1)} %bitcast.10, ...), custom_call_target="tpu_custom_call" | custom-call | flops 335544320 | bytes 5242880 | tf_op jit(solution)/shard_map/pallas_call | solution.py:327
  91.2 0.0 copy-start.4
  91.2 3.0 %collective-permute-start.17 = (bf16[8,256,128]{2,1,0:T(8,128)(2,1)S(1)}, bf16[8,256,128]{2,1,0:T(8,128)(2,1)S(1)}, u32[]{:S(2)}, u32[]{:S(2)}) collective-permute-start(bf16[8,256,128]{2,1,0:T(8,128)(2,1)S(1)} %get-tuple-element.45), channel_id=1, source_target_pairs={{0,16},{16,0},{32,48},{48,32},{64,80},{80,64},{96,112},{112,96},{1... | collective-permute-start | bytes 1572872 | tf_op jit(solution)/shard_map/ppermute | solution.py:336
  94.2 0.1 collective-permute-start.18
  94.3 1.4 %collective-permute-done.18.piece2_ref = bf16[32,128]{1,0:T(8,128)(2,1)S(1)} collective-permute-done((bf16[32,128]{1,0:T(8,128)(2,1)S(1)}, bf16[32,128]{1,0:T(8,128)(2,1)S(1)}, u32[]{:S(2)}, u32[]{:S(2)}) %collective-permute-start.18) | collective-permute-done | bytes 8224 | tf_op jit(solution)/shard_map/ppermute | solution.py:325
  95.7 0.0 collective-permute-done.17.got_ref
  95.8 0.6 shard_map.114
  96.4 17.6 %all_to_all.21.got_ref = bf16[8,320,128]{2,1,0:T(8,128)(2,1)S(1)} all-to-all(bf16[8,320,128]{2,1,0:T(8,128)(2,1)S(1)} %shard_map.114), channel_id=1, replica_groups={{0,32,64,96,128,160,192,224},{16,48,80,112,144,176,208,240},{1,33,65,97..., dimensions={0} | all-to-all | bytes 1310720 | tf_op jit(solution)/shard_map/all_to_all | solution.py:240
  114.0 0.9 shard_map.115
  (16 shorter events, 0.1 us)
Async XLA Ops:
  0.6 22.7 %copy-start.6 = (s32[1,1,80]{2,1,0:T(1,128)S(1)}, s32[1,1,80]{2,1,0:T(1,128)}, u32[]{:S(2)}) copy-start(s32[1,1,80]{2,1,0:T(1,128)} %param.13) | copy-start | bytes 964
  0.6 22.7 %copy-start.7 = (s32[1,1,80]{2,1,0:T(1,128)S(1)}, s32[1,1,80]{2,1,0:T(1,128)}, u32[]{:S(2)}) copy-start(s32[1,1,80]{2,1,0:T(1,128)} %param.14) | copy-start | bytes 964
  2.4 17.7 %all-to-all-start = ((bf16[8,256,128]{2,1,0:T(8,128)(2,1)}), bf16[8,256,128]{2,1,0:T(8,128)(2,1)S(1)}, u32[]{:S(2)}, u32[]{:S(2)}) async-start(bf16[8,256,128]{2,1,0:T(8,128)(2,1)} %broadcast_in_dim.2), calls=%async_computation | async-start | bytes 1048576 | tf_op jit(solution)/shard_map/all_to_all | solution.py:240
  10.5 1.7 %copy-start = (bf16[1,1,80,128,128]{4,3,2,1,0:T(8,128)(2,1)S(1)}, bf16[1,1,80,128,128]{4,3,2,1,0:T(8,128)(2,1)}, u32[]{:S(2)}) copy-start(bf16[1,1,80,128,128]{4,3,2,1,0:T(8,128)(2,1)} %param.12) | copy-start | bytes 7864324
  12.2 0.7 copy-start.5
  12.9 10.5 %copy-start.1 = (bf16[1,1,80,128,128]{4,3,2,1,0:T(8,128)(2,1)S(1)}, bf16[1,1,80,128,128]{4,3,2,1,0:T(8,128)(2,1)}, u32[]{:S(2)}) copy-start(bf16[1,1,80,128,128]{4,3,2,1,0:T(8,128)(2,1)} %param.12) | copy-start | bytes 7864324
  20.0 3.3 %collective-permute-start = (bf16[8,256,128]{2,1,0:T(8,128)(2,1)S(1)}, bf16[8,256,128]{2,1,0:T(8,128)(2,1)}, u32[]{:S(2)}, u32[]{:S(2)}) collective-permute-start(bf16[8,256,128]{2,1,0:T(8,128)(2,1)S(1)} %all-to-all-done.mine_ref), channel_id=1, source_target_pairs={{0,16},{16,0},{32,48},{48,32},{64,80},{80,64},{96,112},{112,96},{1... | collective-permute-start | bytes 1572872 | tf_op jit(solution)/shard_map/ppermute | solution.py:273
  23.4 30.2 %copy-start.2 = (bf16[256,128]{1,0:T(8,128)(2,1)S(1)}, bf16[256,128]{1,0:T(8,128)(2,1)}, u32[]{:S(2)}) copy-start(bf16[256,128]{1,0:T(8,128)(2,1)} %refs_7_.1) | copy-start | bytes 196612
  23.4 30.2 %copy-start.3 = (bf16[128,256]{1,0:T(8,128)(2,1)S(1)}, bf16[128,256]{1,0:T(8,128)(2,1)}, u32[]{:S(2)}) copy-start(bf16[128,256]{1,0:T(8,128)(2,1)} %ws_ref.1) | copy-start | bytes 196612
  23.4 30.2 %copy-start.8 = (bf16[256,256]{1,0:T(8,128)(2,1)S(1)}, bf16[256,256]{1,0:T(8,128)(2,1)}, u32[]{:S(2)}) copy-start(bf16[256,256]{1,0:T(8,128)(2,1)} %refs_8_.1) | copy-start | bytes 393220
  23.4 30.2 %copy-start.9 = (bf16[128,256]{1,0:T(8,128)(2,1)S(1)}, bf16[128,256]{1,0:T(8,128)(2,1)}, u32[]{:S(2)}) copy-start(bf16[128,256]{1,0:T(8,128)(2,1)} %refs_10_.1) | copy-start | bytes 196612
  26.0 7.0 %collective-permute-start.1 = (bf16[3,272,128]{2,1,0:T(8,128)(2,1)S(1)}, bf16[3,272,128]{2,1,0:T(8,128)(2,1)S(1)}, u32[]{:S(2)}, u32[]{:S(2)}) collective-permute-start(bf16[3,272,128]{2,1,0:T(8,128)(2,1)S(1)} %get-tuple-element.30), channel_id=1, source_target_pairs={{0,1},{1,0},{2,3},{3,2},{4,5},{5,4},{6,7},{7,6},{8,9},{9,8},{10,11... | collective-permute-start | bytes 626696 | tf_op jit(solution)/shard_map/ppermute | solution.py:291
  33.0 10.4 %collective-permute-start.2 = (bf16[5,272,128]{2,1,0:T(8,128)(2,1)S(1)}, bf16[5,272,128]{2,1,0:T(8,128)(2,1)S(1)}, u32[]{:S(2)}, u32[]{:S(2)}) collective-permute-start(bf16[5,272,128]{2,1,0:T(8,128)(2,1)S(1)} %shard_map.105), channel_id=1, source_target_pairs={{0,1},{1,0},{2,3},{3,2},{4,5},{5,4},{6,7},{7,6},{8,9},{9,8},{10,11... | collective-permute-start | bytes 1044488 | tf_op jit(solution)/shard_map/ppermute | solution.py:295
  33.1 14.1 %collective-permute-start.3 = (bf16[272,128]{1,0:T(8,128)(2,1)S(1)}, bf16[272,128]{1,0:T(8,128)(2,1)S(1)}, u32[]{:S(2)}, u32[]{:S(2)}) collective-permute-start(bf16[272,128]{1,0:T(8,128)(2,1)S(1)} %get-tuple-element.35), channel_id=1, source_target_pairs={{0,8},{1,9},{2,10},{3,11},{4,12},{5,13},{6,14},{7,15},{8,0},{9,1},... | collective-permute-start | bytes 208904 | tf_op jit(solution)/shard_map/ppermute | solution.py:248
  39.0 8.9 %collective-permute-start.4 = (bf16[272,128]{1,0:T(8,128)(2,1)S(1)}, bf16[272,128]{1,0:T(8,128)(2,1)S(1)}, u32[]{:S(2)}, u32[]{:S(2)}) collective-permute-start(bf16[272,128]{1,0:T(8,128)(2,1)S(1)} %get-tuple-element.36), channel_id=1, source_target_pairs={{0,6},{1,7},{2,8},{3,9},{4,10},{5,11},{6,12},{7,13},{8,14},{9,15},... | collective-permute-start | bytes 208904 | tf_op jit(solution)/shard_map/ppermute | solution.py:248
  40.6 9.3 %collective-permute-start.5 = (bf16[272,128]{1,0:T(8,128)(2,1)S(1)}, bf16[272,128]{1,0:T(8,128)(2,1)S(1)}, u32[]{:S(2)}, u32[]{:S(2)}) collective-permute-start(bf16[272,128]{1,0:T(8,128)(2,1)S(1)} %get-tuple-element.37), channel_id=1, source_target_pairs={{0,10},{1,11},{2,12},{3,13},{4,14},{5,15},{6,0},{7,1},{8,2},{9,3},... | collective-permute-start | bytes 208904 | tf_op jit(solution)/shard_map/ppermute | solution.py:248
  43.6 6.3 %collective-permute-start.6 = (bf16[272,128]{1,0:T(8,128)(2,1)S(1)}, bf16[272,128]{1,0:T(8,128)(2,1)S(1)}, u32[]{:S(2)}, u32[]{:S(2)}) collective-permute-start(bf16[272,128]{1,0:T(8,128)(2,1)S(1)} %get-tuple-element.38), channel_id=1, source_target_pairs={{0,4},{1,5},{2,6},{3,7},{4,8},{5,9},{6,10},{7,11},{8,12},{9,13},{1... | collective-permute-start | bytes 208904 | tf_op jit(solution)/shard_map/ppermute | solution.py:248
  45.2 7.2 %collective-permute-start.7 = (bf16[272,128]{1,0:T(8,128)(2,1)S(1)}, bf16[272,128]{1,0:T(8,128)(2,1)S(1)}, u32[]{:S(2)}, u32[]{:S(2)}) collective-permute-start(bf16[272,128]{1,0:T(8,128)(2,1)S(1)} %get-tuple-element.39), channel_id=1, source_target_pairs={{0,12},{1,13},{2,14},{3,15},{4,0},{5,1},{6,2},{7,3},{8,4},{9,5},{1... | collective-permute-start | bytes 208904 | tf_op jit(solution)/shard_map/ppermute | solution.py:248
  47.2 5.9 %collective-permute-start.8 = (bf16[272,128]{1,0:T(8,128)(2,1)S(1)}, bf16[272,128]{1,0:T(8,128)(2,1)S(1)}, u32[]{:S(2)}, u32[]{:S(2)}) collective-permute-start(bf16[272,128]{1,0:T(8,128)(2,1)S(1)} %get-tuple-element.40), channel_id=1, source_target_pairs={{0,2},{1,3},{2,4},{3,5},{4,6},{5,7},{6,8},{7,9},{8,10},{9,11},{10,... | collective-permute-start | bytes 208904 | tf_op jit(solution)/shard_map/ppermute | solution.py:248
  47.9 5.6 %collective-permute-start.9 = (bf16[272,128]{1,0:T(8,128)(2,1)S(1)}, bf16[272,128]{1,0:T(8,128)(2,1)S(1)}, u32[]{:S(2)}, u32[]{:S(2)}) collective-permute-start(bf16[272,128]{1,0:T(8,128)(2,1)S(1)} %get-tuple-element.41), channel_id=1, source_target_pairs={{0,14},{1,15},{2,0},{3,1},{4,2},{5,3},{6,4},{7,5},{8,6},{9,7},{10,... | collective-permute-start | bytes 208904 | tf_op jit(solution)/shard_map/ppermute | solution.py:248
  54.9 10.4 %collective-permute-start.10 = (bf16[256,128]{1,0:T(8,128)(2,1)}, bf16[256,128]{1,0:T(8,128)(2,1)S(1)}, u32[]{:S(2)}, u32[]{:S(2)}) collective-permute-start(bf16[256,128]{1,0:T(8,128)(2,1)} %get-tuple-element.42), channel_id=1, source_target_pairs={{0,8},{1,9},{2,10},{3,11},{4,12},{5,13},{6,14},{7,15},{8,0},{9,1},... | collective-permute-start | bytes 196616 | tf_op jit(solution)/shard_map/ppermute | solution.py:248
  57.8 16.4 %all-to-all-start.1 = ((bf16[16,64,128]{2,1,0:T(8,128)(2,1)}), bf16[16,64,128]{2,1,0:T(8,128)(2,1)S(1)}, u32[]{:S(2)}, u32[]{:S(2)}) async-start(bf16[16,64,128]{2,1,0:T(8,128)(2,1)} %get-tuple-element.43), calls=%async_computation.1 | async-start | bytes 524288 | tf_op jit(solution)/shard_map/all_to_all | solution.py:240
  66.2 8.9 %collective-permute-start.11 = (bf16[2,256,128]{2,1,0:T(8,128)(2,1)S(1)}, bf16[2,256,128]{2,1,0:T(8,128)(2,1)S(1)}, u32[]{:S(2)}, u32[]{:S(2)}) collective-permute-start(bf16[2,256,128]{2,1,0:T(8,128)(2,1)S(1)} %pad_maximum_fusion.refs_0_), channel_id=1, source_target_pairs={{0,2},{1,3},{2,4},{3,5},{4,6},{5,7},{6,8},{7,9},{8,10},{9,11},{10,... | collective-permute-start | bytes 393224 | tf_op jit(solution)/shard_map/ppermute | solution.py:248
  68.0 7.1 %collective-permute-start.12 = (bf16[2,256,128]{2,1,0:T(8,128)(2,1)S(1)}, bf16[2,256,128]{2,1,0:T(8,128)(2,1)S(1)}, u32[]{:S(2)}, u32[]{:S(2)}) collective-permute-start(bf16[2,256,128]{2,1,0:T(8,128)(2,1)S(1)} %pad_maximum_fusion.refs_0_), channel_id=1, source_target_pairs={{0,14},{1,15},{2,0},{3,1},{4,2},{5,3},{6,4},{7,5},{8,6},{9,7},{10,... | collective-permute-start | bytes 393224 | tf_op jit(solution)/shard_map/ppermute | solution.py:248
  68.9 6.2 %collective-permute-start.13 = (bf16[256,128]{1,0:T(8,128)(2,1)}, bf16[256,128]{1,0:T(8,128)(2,1)S(1)}, u32[]{:S(2)}, u32[]{:S(2)}) collective-permute-start(bf16[256,128]{1,0:T(8,128)(2,1)} %get-tuple-element.42), channel_id=1, source_target_pairs={{0,4},{1,5},{2,6},{3,7},{4,8},{5,9},{6,10},{7,11},{8,12},{9,13},{1... | collective-permute-start | bytes 196616 | tf_op jit(solution)/shard_map/ppermute | solution.py:248
  69.3 5.8 %collective-permute-start.14 = (bf16[256,128]{1,0:T(8,128)(2,1)}, bf16[256,128]{1,0:T(8,128)(2,1)S(1)}, u32[]{:S(2)}, u32[]{:S(2)}) collective-permute-start(bf16[256,128]{1,0:T(8,128)(2,1)} %get-tuple-element.42), channel_id=1, source_target_pairs={{0,12},{1,13},{2,14},{3,15},{4,0},{5,1},{6,2},{7,3},{8,4},{9,5},{1... | collective-permute-start | bytes 196616 | tf_op jit(solution)/shard_map/ppermute | solution.py:248
  74.3 2.7 %collective-permute-start.15 = (bf16[64,128]{1,0:T(8,128)(2,1)S(1)}, bf16[64,128]{1,0:T(8,128)(2,1)S(1)}, u32[]{:S(2)}, u32[]{:S(2)}) collective-permute-start(bf16[64,128]{1,0:T(8,128)(2,1)S(1)} %shard_map.109.mine_ref), channel_id=1, source_target_pairs={{0,1},{1,0},{2,3},{3,2},{4,5},{5,4},{6,7},{7,6},{8,9},{9,8},{10,11... | collective-permute-start | bytes 49160 | tf_op jit(solution)/shard_map/ppermute | solution.py:315
  77.0 12.2 %collective-permute-start.16 = (bf16[8,256,128]{2,1,0:T(8,128)(2,1)S(1)}, bf16[8,256,128]{2,1,0:T(8,128)(2,1)S(1)}, u32[]{:S(2)}, u32[]{:S(2)}) collective-permute-start(bf16[8,256,128]{2,1,0:T(8,128)(2,1)S(1)} %shard_map.110.after_ref.mine_ref), channel_id=1, source_target_pairs={{0,1},{1,0},{2,3},{3,2},{4,5},{5,4},{6,7},{7,6},{8,9},{9,8},{10,11... | collective-permute-start | bytes 1572872 | tf_op jit(solution)/shard_map/ppermute | solution.py:319
  91.2 22.8 %copy-start.4 = (bf16[128,256]{1,0:T(8,128)(2,1)S(1)}, bf16[128,256]{1,0:T(8,128)(2,1)}, u32[]{:S(2)}) copy-start(bf16[128,256]{1,0:T(8,128)(2,1)} %ws_ref.1) | copy-start | bytes 196612
  91.2 4.5 %collective-permute-start.17 = (bf16[8,256,128]{2,1,0:T(8,128)(2,1)S(1)}, bf16[8,256,128]{2,1,0:T(8,128)(2,1)S(1)}, u32[]{:S(2)}, u32[]{:S(2)}) collective-permute-start(bf16[8,256,128]{2,1,0:T(8,128)(2,1)S(1)} %get-tuple-element.45), channel_id=1, source_target_pairs={{0,16},{16,0},{32,48},{48,32},{64,80},{80,64},{96,112},{112,96},{1... | collective-permute-start | bytes 1572872 | tf_op jit(solution)/shard_map/ppermute | solution.py:336
  94.2 1.5 %collective-permute-start.18 = (bf16[32,128]{1,0:T(8,128)(2,1)S(1)}, bf16[32,128]{1,0:T(8,128)(2,1)S(1)}, u32[]{:S(2)}, u32[]{:S(2)}) collective-permute-start(bf16[32,128]{1,0:T(8,128)(2,1)S(1)} %shard_map.112.after_ref.piece_ref), channel_id=1, source_target_pairs={{0,16},{16,0},{32,48},{48,32},{64,80},{80,64},{96,112},{112,96},{1... | collective-permute-start | bytes 24584 | tf_op jit(solution)/shard_map/ppermute | solution.py:325
